TPU v7x, 256 devices: a whole 4x4x8 slice. The times are simulated.
256 devices in a mesh: ctx: 8 (over y, core), chan: 32 (over x, z).
Axes of the slice: x: 4, y: 4, z: 8, core: 2. Of those that a mesh axis runs over, the one named last changes fastest.
Arguments:
- query: bfloat16 [8192, 8192], P('ctx', 'chan'), may hold values from -6 to 6
- key: bfloat16 [8192, 8192], P('ctx', 'chan'), may hold values from -6 to 6
- value: bfloat16 [8192, 8192], P('ctx', 'chan'), may hold values from -6 to 6
- out_grad: bfloat16 [8192, 8192], P('ctx', 'chan'), may hold values from -6 to 6
- out_weight: bfloat16 [8192, 8192], P(None, 'chan'), may hold values from -0.0625 to 0.0625
- rate: float32 [512, 16], P('chan'), may hold values from 2.4414063e-05 to 0.05, as said below
- residue: float32 [512, 16], P('chan'), may hold values from -0.2 to 0.2
Outputs:
- d_query: bfloat16 [8192, 8192], P('ctx', 'chan')
- d_key: bfloat16 [8192, 8192], P('ctx', 'chan')
- d_value: bfloat16 [8192, 8192], P('ctx', 'chan')
- d_weight: float32 [8192, 8192], P('ctx', 'chan')
- d_residue: float32 [512, 16], P('chan')
- d_rate: float32 [512, 16], P('chan')
Inputs may be any that keep to these rules, and one draw needn't show every extreme that they name: `rate`: decay rates of the modes.
All inputs are finite; a program needn't handle non-finite values.
Results may differ from a plain program's by a relative error of at most 0.017.
Values may be sent and summed in bfloat16 or wider, within the bound.
No kernel may reach another device: no remote copies, remote signals or barrier semaphores. Data moves between devices by JAX's collectives and lax.ppermute only.
A program may use at most 128 MiB of HBM per device.

v0:
```python
import functools

import jax
import jax.numpy as jnp
from jax import lax
from jax.experimental import pallas as pl
from jax.experimental.pallas import tpu as pltpu
from jax.sharding import Mesh
from jax.sharding import PartitionSpec as P

BLK = 128
TILE = 256
F32 = jnp.float32
BF16 = jnp.bfloat16
VMEM_LIMIT = 56 * 1024 * 1024
CTX = ("y", "core")
CHAN = ("x", "z")


def split(x):
    hi = x.astype(BF16)
    return hi, (x - hi.astype(F32)).astype(BF16)


def mm(a, b, ca=1, cb=0):
    return lax.dot_general(a, b, (((ca,), (cb,)), ((), ())), preferred_element_type=F32)


def lanes(shape):
    return lax.broadcasted_iota(jnp.int32, shape, 1).astype(F32)


def rows(shape):
    return lax.broadcasted_iota(jnp.int32, shape, 0).astype(F32)


def exact(a, b, ca, cb):
    return lax.dot_general(
        a, b, (((ca,), (cb,)), ((), ())), preferred_element_type=F32, precision=lax.Precision.HIGHEST
    )


def by_column(param):
    turned = param.T
    groups, poles = param.shape
    return jnp.concatenate(
        [jnp.broadcast_to(turned[:, g : g + 1], (poles, BLK)) for g in range(groups)], axis=0
    )


def by_lane(param):
    groups, poles = param.shape
    return jnp.concatenate([param, param, jnp.zeros((groups, BLK - 2 * poles), F32)], axis=1)


def indicator(groups, channels):
    shape = (groups, channels)
    return (
        lax.broadcasted_iota(jnp.int32, shape, 0)
        == lax.broadcasted_iota(jnp.int32, shape, 1) // (channels // groups)
    ).astype(F32)


def by_channel(param, channels):
    return exact(param, indicator(param.shape[0], channels), 0, 0)


def stacked(ref, g, width, blocks):
    return jnp.concatenate(
        [ref[g * width : (g + 1) * width, b * BLK : (b + 1) * BLK] for b in range(blocks)], axis=0
    )


def with_states(x, taps, state, lead_hi, lead_lo):
    poles = lead_hi.shape[0]
    none = jnp.zeros((BLK - poles, BLK), BF16)
    s_hi, s_lo = split(state)
    first = mm(
        jnp.concatenate([x, s_hi], axis=1), jnp.concatenate([taps, lead_hi, none], axis=0)
    )
    second = mm(
        jnp.concatenate([s_lo, s_hi], axis=1),
        jnp.concatenate([lead_hi, none, lead_lo, none], axis=0),
    )
    return first + second


def sums_rhs(top, second, third, fourth):
    poles = top[0].shape[0]
    none = jnp.zeros((poles, 2 * BLK), BF16)
    rest = jnp.zeros((BLK - 2 * poles, 2 * BLK), BF16)

    def part(pair):
        return none if pair is None else jnp.concatenate(pair, axis=1)

    return jnp.concatenate(
        [part(top), part(second), rest, part(third), part(fourth), rest], axis=0
    )


def forward_kernel(
    key_ref, value_ref, rate_ref, res_ref, conv_ref, ends_ref, xt_ref, states_ref, ct_ref, sums_ref, fin_ref
):
    tokens, channels = key_ref.shape
    groups, poles = rate_ref.shape
    width, blocks = channels // groups, tokens // BLK
    for b in range(blocks):
        at = slice(b * BLK, (b + 1) * BLK)
        inner = key_ref[at, :].astype(F32) * value_ref[at, :].astype(F32)
        xt_ref[:, at] = inner.T.astype(BF16)
    rate, res = by_column(rate_ref[...]), by_column(res_ref[...])
    time = lanes(rate.shape)
    u_hi, u_lo = split(res * jnp.exp(-rate * (time - 64.0)))
    v_hi, v_lo = split(jnp.exp(rate * (time - 64.0)))
    tail_all = jnp.exp(-rate * (BLK - 1.0 - time))
    tail = split(tail_all)
    tail_lag = split((BLK - 1.0 - time) * tail_all)
    lead = split(res * jnp.exp(-rate * (time + 1.0)))
    for g in range(groups):
        own = slice(g * poles, (g + 1) * poles)
        x = stacked(xt_ref, g, width, blocks)
        top = tuple(part[own] for part in tail)
        lag = tuple(part[own] for part in tail_lag)
        sums_ref[g] = mm(
            jnp.concatenate([x, x], axis=1), sums_rhs(top, lag, None, top), 1, 1
        )
    rate_two = by_lane(rate_ref[...])
    span = jnp.exp(-float(BLK) * rate_two)
    lane = lanes((1, BLK))
    for g in range(groups):
        step = span[g : g + 1, :]
        couple = jnp.where(lane >= poles, float(BLK) * step, 0.0)
        state = jnp.zeros((width, BLK), F32)
        twin = jnp.zeros((width, BLK), F32)
        for b in range(blocks):
            at = slice(b * width, (b + 1) * width)
            states_ref[g, at, :] = state
            state = step * state + couple * twin + sums_ref[g, at, :BLK]
            twin = step * twin + sums_ref[g, at, BLK:]
        fin_ref[g * width : (g + 1) * width, :] = state
    ends_ref[...] = fin_ref[...].T[: 2 * poles, :]
    causal = lanes((BLK, BLK)) >= rows((BLK, BLK))
    for g in range(groups):
        own = slice(g * poles, (g + 1) * poles)
        x = stacked(xt_ref, g, width, blocks)
        taps = mm(
            jnp.concatenate([v_hi[own], v_lo[own], v_hi[own]], axis=0),
            jnp.concatenate([u_hi[own], u_hi[own], u_lo[own]], axis=0),
            0,
            0,
        )
        taps = jnp.where(causal, taps, 0.0).astype(BF16)
        out = with_states(x, taps, states_ref[g], lead[0][own], lead[1][own])
        for b in range(blocks):
            ct_ref[g * width : (g + 1) * width, b * BLK : (b + 1) * BLK] = out[
                b * width : (b + 1) * width
            ]
    for b in range(blocks):
        at = slice(b * BLK, (b + 1) * BLK)
        conv_ref[at, :] = ct_ref[:, at].T


def spread(state, groups):
    poles, channels = state.shape
    width = channels // groups
    tall = jnp.concatenate([state] * groups, axis=0)
    row = lax.broadcasted_iota(jnp.int32, tall.shape, 0) // poles
    col = lax.broadcasted_iota(jnp.int32, tall.shape, 1) // width
    return jnp.where(row == col, tall, 0.0)


def modes(lead, state_tall):
    l_hi, l_lo = split(lead)
    s_hi, s_lo = split(state_tall)
    return mm(l_hi, s_hi) + mm(l_hi, s_lo) + mm(l_lo, s_hi)


def enter_kernel(
    here_ref, all_ref, conv_ref, query_ref, rate_ref, res_ref, conv_out_ref, gated_ref, in_ref
):
    tokens, channels = conv_ref.shape
    groups, poles = rate_ref.shape
    mine = 2 * here_ref[0] + here_ref[1]
    count = all_ref.shape[0]
    rate_nc = by_channel(rate_ref[...], channels)
    rate_row, res_row = by_column(rate_ref[...]).T, by_column(res_ref[...]).T
    state = jnp.zeros((poles, channels), F32)
    slope = jnp.zeros((poles, channels), F32)
    for place in range(count):
        gap = (mine - 1 - place).astype(F32)
        lag = jnp.maximum(gap, 0.0) * float(tokens)
        weight = jnp.where(gap >= 0.0, jnp.exp(-rate_nc * lag), 0.0)
        end = all_ref[place, :poles, :]
        state = state + weight * end
        slope = slope + weight * (all_ref[place, poles:, :] + lag * end)
    in_ref[:poles, :] = state
    in_ref[poles:, :] = slope
    tall = spread(state, groups)
    for b in range(tokens // BLK):
        at = slice(b * BLK, (b + 1) * BLK)
        time = rows((BLK, groups * poles)) + float(b * BLK + 1)
        lead = res_row * jnp.exp(-rate_row * time)
        conv = conv_ref[at, :] + modes(lead, tall)
        conv_out_ref[at, :] = conv
        gated_ref[:, at] = (query_ref[at, :].astype(F32) * conv).T.astype(BF16)


def backward_kernel(
    own_ref, p1_ref, p2_ref, p3_ref, query_ref, conv_ref, xt_ref, states_ref, in_ref, rate_ref, res_ref,
    dq_ref, back_ref, pay_ref, gt_ref, bt_ref, sums_ref, rs_ref, fin_ref, cross_ref
):
    tokens, channels = query_ref.shape
    groups, poles = rate_ref.shape
    width, blocks = channels // groups, tokens // BLK
    for b in range(blocks):
        at = slice(b * BLK, (b + 1) * BLK)
        total = (own_ref[at, :].astype(F32) + p1_ref[at, :].astype(F32)) + (
            p2_ref[at, :].astype(F32) + p3_ref[at, :].astype(F32)
        )
        grad = total.astype(BF16).astype(F32)
        dq_ref[at, :] = (grad * conv_ref[at, :]).astype(BF16)
        gt_ref[:, at] = (grad * query_ref[at, :].astype(F32)).T.astype(BF16)
    rate, res = by_column(rate_ref[...]), by_column(res_ref[...])
    time = lanes(rate.shape)
    u_hi, u_lo = split(res * jnp.exp(-rate * (time - 64.0)))
    v_all = jnp.exp(rate * (time - 64.0))
    v_hi, v_lo = split(v_all)
    w_hi, w_lo = split((time - 64.0) * v_all)
    head_all = jnp.exp(-rate * time)
    head = split(head_all)
    head_lag = split(time * head_all)
    trail = split(res * jnp.exp(-rate * (BLK - time)))
    for g in range(groups):
        own = slice(g * poles, (g + 1) * poles)
        y = stacked(gt_ref, g, width, blocks)
        top = tuple(part[own] for part in head)
        lag = tuple(part[own] for part in head_lag)
        sums_ref[g] = mm(jnp.concatenate([y, y], axis=1), sums_rhs(top, lag, lag, top), 1, 1)
    rate_two = by_lane(rate_ref[...])
    span = jnp.exp(-float(BLK) * rate_two)
    lane = lanes((1, BLK))
    low = lane < poles
    for g in range(groups):
        step = span[g : g + 1, :]
        couple = jnp.where(lane >= poles, float(BLK) * step, 0.0)
        state = jnp.zeros((width, BLK), F32)
        twin = jnp.zeros((width, BLK), F32)
        res_sum = jnp.zeros((width, BLK), F32)
        rate_sum = jnp.zeros((width, BLK), F32)
        for b in reversed(range(blocks)):
            at = slice(b * width, (b + 1) * width)
            rs_ref[g, at, :] = state
            first, second = sums_ref[g, at, :BLK], sums_ref[g, at, BLK:]
            before = states_ref[g, at, :]
            res_sum = res_sum + jnp.where(low, first * before, 0.0)
            rate_sum = rate_sum + (second + jnp.where(low, first, 0.0)) * before
            state, twin = (
                step * state + couple * twin + first,
                step * twin + jnp.where(low, 0.0, second),
            )
        fin_ref[g * width : (g + 1) * width, :] = state
        decay = jnp.exp(-rate_two[g : g + 1, :])
        cross_ref[0, g * width : (g + 1) * width, :] = decay * res_sum
        cross_ref[1, g * width : (g + 1) * width, :] = decay * rate_sum
    causal = rows((BLK, BLK)) >= lanes((BLK, BLK))
    for g in range(groups):
        own = slice(g * poles, (g + 1) * poles)
        y = stacked(gt_ref, g, width, blocks)
        taps = mm(
            jnp.concatenate([u_hi[own], u_hi[own], u_lo[own]], axis=0),
            jnp.concatenate([v_hi[own], v_lo[own], v_hi[own]], axis=0),
            0,
            0,
        )
        taps = jnp.where(causal, taps, 0.0).astype(BF16)
        out = with_states(y, taps, rs_ref[g], trail[0][own], trail[1][own])
        for b in range(blocks):
            bt_ref[g * width : (g + 1) * width, b * BLK : (b + 1) * BLK] = out[
                b * width : (b + 1) * width
            ]
        x = stacked(xt_ref, g, width, blocks)
        pairs = jnp.where(causal, mm(y, x, 0, 0), 0.0).astype(BF16)
        rhs = jnp.concatenate(
            [
                jnp.concatenate([v_hi[own], v_lo[own]], axis=1),
                jnp.concatenate([w_hi[own], w_lo[own]], axis=1),
                jnp.zeros((BLK - 2 * poles, 2 * BLK), BF16),
            ],
            axis=0,
        )
        held = mm(jnp.concatenate([pairs, pairs], axis=1), rhs, 1, 1)
        since = rows((BLK, BLK)) - 64.0
        held = held * jnp.exp(-rate_two[g : g + 1, :] * since)
        res_row = jnp.sum(jnp.where(low, held, 0.0), axis=0, keepdims=True)
        rate_row = jnp.sum(jnp.where(low, since * held, -held), axis=0, keepdims=True)
        one = slice(g * width, g * width + 1)
        cross_ref[0, one, :] = cross_ref[0, one, :] + res_row
        cross_ref[1, one, :] = cross_ref[1, one, :] + rate_row
    starts = fin_ref[...].T
    start, start_lag = starts[:poles], starts[poles : 2 * poles]
    state_in, slope_in = in_ref[:poles, :], in_ref[poles:, :]
    decay = jnp.exp(-by_channel(rate_ref[...], channels))
    res_cross = cross_ref[0].T[:poles]
    rate_cross = cross_ref[1].T
    pay_ref[:poles, :] = start
    pay_ref[poles : 2 * poles, :] = res_cross + decay * start * state_in
    pay_ref[2 * poles :, :] = (
        rate_cross[:poles]
        + rate_cross[poles : 2 * poles]
        + decay * ((start_lag + start) * state_in + start * slope_in)
    )
    for b in range(blocks):
        at = slice(b * BLK, (b + 1) * BLK)
        back_ref[at, :] = bt_ref[:, at].T


def leave_kernel(
    here_ref, all_ref, back_ref, key_ref, value_ref, rate_ref, res_ref, dk_ref, dv_ref, dres_ref, drate_ref
):
    tokens, channels = back_ref.shape
    groups, poles = rate_ref.shape
    mine = 2 * here_ref[0] + here_ref[1]
    count = all_ref.shape[0]
    rate_nc = by_channel(rate_ref[...], channels)
    rate_row, res_row = by_column(rate_ref[...]).T, by_column(res_ref[...]).T
    state = jnp.zeros((poles, channels), F32)
    total = jnp.zeros((2 * poles, channels), F32)
    for place in range(count):
        gap = (place - 1 - mine).astype(F32)
        lag = jnp.maximum(gap, 0.0) * float(tokens)
        weight = jnp.where(gap >= 0.0, jnp.exp(-rate_nc * lag), 0.0)
        state = state + weight * all_ref[place, :poles, :]
        total = total + all_ref[place, poles:, :]
    tall = spread(state, groups)
    scale = 1.0 / float(tokens * count)
    both = exact(indicator(groups, channels), total, 1, 1)
    dres_ref[...] = both[:, :poles] * scale
    drate_ref[...] = -res_ref[...] * both[:, poles:] * scale
    for b in range(tokens // BLK):
        at = slice(b * BLK, (b + 1) * BLK)
        time = float(tokens - b * BLK) - rows((BLK, groups * poles))
        trail = res_row * jnp.exp(-rate_row * time)
        back = back_ref[at, :] + modes(trail, tall)
        dk_ref[at, :] = (back * value_ref[at, :].astype(F32)).astype(BF16)
        dv_ref[at, :] = (back * key_ref[at, :].astype(F32)).astype(BF16)


def block_copies(z, refs, to_ref, sem):
    own, r1, l1, r2, l2, r3, l3, r4, l4 = refs
    half = r4.shape[0]
    whole = ((0, own), (-1, r1), (1, l1), (-2, r2), (2, l2), (-3, r3), (3, l3))
    nz = len(whole) + 1
    for far, ref in whole:
        at = lax.rem(z + far + nz, nz)
        yield at, ref, lambda slot: to_ref.at[slot], lambda slot: sem.at[slot, 0]
    at = lax.rem(z + nz // 2, nz)
    yield at, r4, lambda slot: to_ref.at[slot, pl.ds(0, half), :], lambda slot: sem.at[slot, 0]
    yield at, l4, lambda slot: to_ref.at[slot, pl.ds(half, half), :], lambda slot: sem.at[slot, 1]


def fetch_half(z, which, refs, half_ref, sem):
    count = half_ref.shape[0]
    far_slot = lax.rem(z + count, count)
    far_here = lax.div(lax.rem(z + count, 2 * count), count) == which
    for at, ref, place, signal in block_copies(z, refs, half_ref, sem):
        slot = lax.rem(at, count)

        @pl.when(lax.div(at, count) == which)
        def _():
            pltpu.make_async_copy(ref, place(slot), signal(slot)).start()

    def wait(j):
        split_here = jnp.logical_and(far_here, far_slot == j)
        tokens = half_ref.shape[1]

        @pl.when(split_here)
        def _():
            for part in range(2):
                piece = half_ref.at[j, pl.ds(part * (tokens // 2), tokens // 2), :]
                pltpu.make_async_copy(piece, piece, sem.at[j, part]).wait()

        @pl.when(jnp.logical_not(split_here))
        def _():
            pltpu.make_async_copy(half_ref.at[j], half_ref.at[j], sem.at[j, 0]).wait()

    return wait


def away_kernel(here_ref, *refs):
    blocks, gates, (away_ref, half_ref, sem) = refs[:9], refs[9:13], refs[13:]
    count, _, width = half_ref.shape
    wait = fetch_half(here_ref[2], 1 - here_ref[1], blocks, half_ref, sem)
    for j in range(count):
        wait(j)
        at = slice(j * width, (j + 1) * width)
        for i, gate in enumerate(gates):
            away_ref[i, :, at] = mm(gate[...], half_ref[j]).astype(BF16)


def project_kernel(here_ref, *refs):
    blocks, weight_ref, fetched, others = refs[:9], refs[9], refs[10:14], refs[14:18]
    p0_ref, p1_ref, p2_ref, p3_ref, f_ref, w_ref, f_sem, w_sem = refs[18:]
    core, z, x = here_ref[1], here_ref[2], here_ref[3]
    nz, tokens, _ = f_ref.shape
    rows_x = w_ref.shape[1]
    half = rows_x // 2
    feat = [
        pltpu.make_async_copy(ref, place(at), signal(at))
        for at, ref, place, signal in block_copies(z, blocks, f_ref, f_sem)
    ]
    weight = {
        0: [
            pltpu.make_async_copy(
                weight_ref.at[pl.ds(pl.multiple_of(x * rows_x, rows_x), rows_x), :], w_ref.at[0], w_sem.at[0]
            )
        ]
    }
    for k, (i, first) in enumerate(((1, 0), (2, 0), (2, half // 2), (3, 0))):
        for j, (ref, base) in enumerate(((fetched[k], core * half), (others[k], (1 - core) * half))):
            size = ref.shape[0]
            place = pl.ds(pl.multiple_of(base + first, half // 2), size)
            weight.setdefault(i, []).append(
                pltpu.make_async_copy(ref, w_ref.at[i, place, :], w_sem.at[2 * k + j + 1])
            )
    for copy in weight[2] + feat + weight[1] + weight[3] + weight[0]:
        copy.start()
    for copy in feat:
        copy.wait()
    tile = TILE
    for i, out in ((2, p2_ref), (1, p1_ref), (3, p3_ref), (0, p0_ref)):
        for copy in weight[i]:
            copy.wait()
        for m in range(tokens // tile):
            at = slice(m * tile, (m + 1) * tile)
            lhs = jnp.concatenate([f_ref[j, at, :] for j in range(nz)], axis=1)
            out[at, :] = mm(lhs, w_ref[i]).astype(BF16)


def chip_kernel(here_ref, *refs):
    blocks, came_ref, gates, outs, (gate_ref, half_ref, sem) = refs[:9], refs[9], refs[10:14], refs[14:18], refs[18:]
    y, core = here_ref[0], here_ref[1]
    count, _, width = half_ref.shape
    wait = fetch_half(here_ref[2], core, blocks, half_ref, sem)
    for i, gate in enumerate(gates):
        gate_ref[i] = gate[...]
    for j in range(count):
        wait(j)
        at = slice(j * width, (j + 1) * width)
        for r, out in enumerate(outs):
            i = lax.rem(8 - y - r, 4)
            part = mm(gate_ref[i], half_ref[j])
            out[:, at] = (part + came_ref[i, :, at].astype(F32)).astype(BF16)


def column_kernel(a_ref, b_ref, c_ref, d_ref, out_ref):
    total = (a_ref[...].astype(F32) + b_ref[...].astype(F32)) + (
        c_ref[...].astype(F32) + d_ref[...].astype(F32)
    )
    out_ref[...] = total.astype(BF16)


def total_kernel(scale, in_ref, out_ref):
    for b in range(in_ref.shape[1] // BLK):
        at = slice(b * BLK, (b + 1) * BLK)
        out_ref[at, :] = in_ref[:, at].astype(F32).T * scale


MIB = 2**20


def call(kernel, outs, scratch, ops, vmem, us, scalars=0, far=()):
    spec = pl.BlockSpec(memory_space=pltpu.VMEM)
    return pl.pallas_call(
        kernel,
        out_shape=outs,
        in_specs=[
            pl.BlockSpec(memory_space=pltpu.SMEM)
            if i < scalars
            else (pl.BlockSpec(memory_space=pltpu.HBM) if i in far else spec)
            for i in range(len(ops))
        ],
        out_specs=[spec] * len(outs),
        scratch_shapes=scratch,
        compiler_params=pltpu.CompilerParams(vmem_limit_bytes=vmem * MIB),
        cost_estimate=pl.CostEstimate(
            flops=1000, bytes_accessed=int(us * 3.69e6), transcendentals=0
        ),
    )(*ops)


def shift(n, by):
    return [(i, (i + by) % n) for i in range(n)]


def gather_ctx(item):
    n = lax.axis_size(CTX)
    return lax.all_to_all(
        jnp.broadcast_to(item[None], (n,) + item.shape), CTX, split_axis=0, concat_axis=0
    )


def after(value, *others):
    return lax.optimization_barrier((value, others))[0]


def local(query, key, value, out_grad, out_weight, rate, residue):
    tokens, channels = query.shape
    groups, poles = rate.shape
    feats = out_weight.shape[0]
    y, core = lax.axis_index("y"), lax.axis_index("core")
    x, z = lax.axis_index("x"), lax.axis_index("z")
    nx, ny, nz = lax.axis_size("x"), lax.axis_size("y"), lax.axis_size("z")
    here = jnp.stack([y, core, z, x]).astype(jnp.int32)
    swap = [(0, 1), (1, 0)]
    sds = jax.ShapeDtypeStruct
    half_scratch = [
        pltpu.VMEM((nz // 2, tokens, channels), BF16),
        pltpu.SemaphoreType.DMA((nz // 2, 2)),
    ]
    stack_shape = (groups, tokens // BLK * (channels // groups))

    def both_ways(axis, pair):
        n = lax.axis_size(axis)
        return (
            lax.ppermute(pair[0], axis, shift(n, 1)),
            lax.ppermute(pair[1], axis, shift(n, -1)),
        )

    rows_x = feats // nx
    half_rows = rows_x // 2

    def rows_for(by, start, size):
        first = ((x + by) % nx) * rows_x + core * half_rows + start
        return lax.dynamic_slice(out_weight, (first, 0), (size, channels))

    hop1 = both_ways("z", (out_grad, out_grad))
    near = both_ways("x", (rows_for(1, 0, half_rows), rows_for(-1, 0, half_rows)))

    conv_own, ends, xt, states = call(
        forward_kernel,
        [
            sds((tokens, channels), F32),
            sds((2 * poles, channels), F32),
            sds((channels, tokens), BF16),
            sds(stack_shape + (BLK,), F32),
        ],
        [
            pltpu.VMEM((channels, tokens), F32),
            pltpu.VMEM(stack_shape + (2 * BLK,), F32),
            pltpu.VMEM((channels, BLK), F32),
        ],
        [key, value, rate, residue],
        12,
        10.0,
    )
    hop2 = both_ways("z", after(hop1, near, ends))
    half_a = both_ways("x", (rows_for(2, 0, half_rows // 2), rows_for(2, half_rows // 2, half_rows // 2)))
    all_ends = gather_ctx(ends)
    conv, gated, entering = call(
        enter_kernel,
        [
            sds((tokens, channels), F32),
            sds((channels, tokens), BF16),
            sds((2 * poles, channels), F32),
        ],
        [],
        [here, all_ends, conv_own, query, rate, residue],
        8,
        10.0,
        scalars=1,
    )
    hop3 = both_ways("z", after(hop2, gated, half_a))
    half_b = both_ways("x", half_a)
    sent = after(gated, half_b)
    gates = [gated] + [lax.ppermute(sent, "x", shift(nx, i)) for i in range(1, nx)]
    fetched = [near[0], *half_b, near[1]]
    others = [lax.ppermute(piece, "core", swap) for piece in fetched]
    right, left = after(hop3, others)
    hop4 = both_ways("z", (right[: tokens // 2], left[tokens // 2 :]))
    blocks = [out_grad, *hop1, *hop2, *hop3, *hop4]

    own, one, two, three = call(
        project_kernel,
        [sds((tokens, channels), BF16)] * nx,
        [
            pltpu.VMEM((nz, tokens, channels), BF16),
            pltpu.VMEM((nx, rows_x, channels), BF16),
            pltpu.SemaphoreType.DMA((nz, 2)),
            pltpu.SemaphoreType.DMA((2 * nx + 1,)),
        ],
        [here] + blocks + [out_weight] + fetched + others,
        16,
        6.0,
        scalars=1,
        far=tuple(range(1, 19)),
    )
    sums = [
        lax.ppermute(part, "x", shift(nx, -i)) for i, part in ((2, two), (1, one), (3, three))
    ]

    (away,) = call(
        away_kernel,
        [sds((nx, channels, half_rows), BF16)],
        half_scratch,
        [here] + after(blocks, own) + gates,
        12,
        0.5,
        scalars=1,
        far=tuple(range(1, 10)),
    )
    came = lax.ppermute(away, "core", swap)

    chip = call(
        chip_kernel,
        [sds((channels, half_rows), BF16)] * nx,
        [pltpu.VMEM((nx, channels, tokens), BF16)] + half_scratch,
        [here] + blocks + [came] + gates,
        16,
        0.5,
        scalars=1,
        far=tuple(range(1, 10)),
    )
    parts = [chip[0]] + [lax.ppermute(chip[r], "y", shift(ny, r)) for r in range(1, ny)]
    d_query, back_own, pay = call(
        backward_kernel,
        [
            sds((tokens, channels), BF16),
            sds((tokens, channels), F32),
            sds((3 * poles, channels), F32),
        ],
        [
            pltpu.VMEM((channels, tokens), BF16),
            pltpu.VMEM((channels, tokens), F32),
            pltpu.VMEM(stack_shape + (2 * BLK,), F32),
            pltpu.VMEM(stack_shape + (BLK,), F32),
            pltpu.VMEM((channels, BLK), F32),
            pltpu.VMEM((2, channels, BLK), F32),
        ],
        [after(own, chip)] + sums + [query, conv, xt, states, entering, rate, residue],
        16,
        20.0,
    )
    parts[0] = after(parts[0], pay)
    (column,) = call(column_kernel, [sds((channels, half_rows), BF16)], [], parts, 8, 1.0)
    all_pay = gather_ctx(after(pay, column))
    route = [(a * nx + b, b * nx + (a + b) % nx) for a in range(ny) for b in range(nx)]
    column = lax.ppermute(column, ("y", "x"), route)

    d_key, d_value, d_residue, d_rate = call(
        leave_kernel,
        [
            sds((tokens, channels), BF16),
            sds((tokens, channels), BF16),
            sds((groups, poles), F32),
            sds((groups, poles), F32),
        ],
        [],
        [here, all_pay, back_own, key, value, rate, residue],
        8,
        2.5,
        scalars=1,
    )
    (d_weight,) = call(
        functools.partial(total_kernel, 1.0 / float(tokens * 2 * nx)),
        [sds((half_rows, channels), F32)],
        [],
        [column],
        8,
        1.5,
    )
    return (d_query, d_key, d_value, d_weight, d_residue, d_rate)


def solution(mesh):
    fine = Mesh(mesh.devices.reshape(4, 2, 4, 8), ("y", "core", "x", "z"))
    both = P(CTX, CHAN)
    param = P(CHAN, None)
    return jax.shard_map(
        local,
        mesh=fine,
        in_specs=(both, both, both, both, P(None, CHAN), param, param),
        out_specs=(both, both, both, both, param, param),
        check_vma=False,
    )
```

profile of v0, /device:TPU:1, one launch (start us, length us, event | category | flops | bytes accessed | tf_op | source)
XLA Modules:
  0.0 159.4 jit_solution(1973900261194130532)
XLA Ops:
  0.7 6.5 %collective-permute-start.1 = (bf16[1024,256]{1,0:T(8,128)(2,1)}, bf16[1024,256]{1,0:T(8,128)(2,1)S(1)}, u32[]{:S(2)}, u32[]{:S(2)}) collective-permute-start(bf16[1024,256]{1,0:T(8,128)(2,1)} %refs_0_.4), channel_id=1, source_target_pairs={{0,7},{1,0},{2,1},{3,2},{4,3},{5,4},{6,5},{7,6},{8,15},{9,8},{10,9... | collective-permute-start | bytes 1572872 | tf_op jit(solution)/shard_map/ppermute | solution.py:526
  7.2 2.2 %constant_dynamic-slice_fusion.2 = (bf16[1024,256]{1,0:T(8,128)(2,1)}, bf16[1024,256]{1,0:T(8,128)(2,1)}) fusion(bf16[8192,256]{1,0:T(8,128)(2,1)} %refs_9_.1, s32[]{:T(128)S(6)} %select_n.32, s32[]{:T(128)S(6)} %select_n.30), kind=kLoop, calls=%fused_computation.2 | loop fusion | bytes 2097160 | tf_op jit(solution)/shard_map/dynamic_slice | solution.py:534
  9.4 2.5 %collective-permute-start.3 = (bf16[1024,256]{1,0:T(8,128)(2,1)}, bf16[1024,256]{1,0:T(8,128)(2,1)S(1)}, u32[]{:S(2)}, u32[]{:S(2)}) collective-permute-start(bf16[1024,256]{1,0:T(8,128)(2,1)} %get-tuple-element.90), channel_id=1, source_target_pairs={{0,24},{8,0},{16,8},{24,16},{1,25},{9,1},{17,9},{25,17},{2,26},{10... | collective-permute-start | bytes 1572872 | tf_op jit(solution)/shard_map/ppermute | solution.py:526
  11.9 1.1 constant_dynamic-slice_fusion
  12.9 2.8 %collective-permute-start.7 = (bf16[512,256]{1,0:T(8,128)(2,1)S(1)}, bf16[512,256]{1,0:T(8,128)(2,1)S(1)}, u32[]{:S(2)}, u32[]{:S(2)}) collective-permute-start(bf16[512,256]{1,0:T(8,128)(2,1)S(1)} %get-tuple-element.88), channel_id=1, source_target_pairs={{0,24},{8,0},{16,8},{24,16},{1,25},{9,1},{17,9},{25,17},{2,26},{10... | collective-permute-start | bytes 786440 | tf_op jit(solution)/shard_map/ppermute | solution.py:526
  15.7 1.0 copy-done.3
  16.7 1.0 copy-done.5
  19.2 2.7 %shard_map.118 = (f32[1024,256]{1,0:T(8,128)S(1)}, f32[32,256]{1,0:T(8,128)S(1)}, bf16[256,1024]{1,0:T(8,128)(2,1)S(1)}, f32[16,128,128]{2,1,0:T(8,128)S(1)}) custom-call(bf16[1024,256]{1,0:T(8,128)(2,1)S(1)} %copy-done.3, bf16[1024,256]{1,0:T(8,128)(2,1)S(1)} %copy-done.5, f32[16,16]{1,0:T(8,128)S(1)} %copy-done.17, f32[16,16]{1,0:T(8,128)S(1)} %copy-done.19), custom_call_target="tpu_custom_call" | custom-call | flops 1000 | bytes 36900000 | tf_op jit(solution)/shard_map/pallas_call | solution.py:473
  21.9 1.0 copy-done.7
  22.9 1.0 copy-done.9
  26.3 2.7 %collective-permute-start.5 = (bf16[1024,256]{1,0:T(8,128)(2,1)S(1)}, bf16[1024,256]{1,0:T(8,128)(2,1)S(1)}, u32[]{:S(2)}, u32[]{:S(2)}) collective-permute-start(bf16[1024,256]{1,0:T(8,128)(2,1)S(1)} %collective-permute-done.1.refs_2_), channel_id=1, source_target_pairs={{0,7},{1,0},{2,1},{3,2},{4,3},{5,4},{6,5},{7,6},{8,15},{9,8},{10,9... | collective-permute-start | bytes 1572872 | tf_op jit(solution)/shard_map/ppermute | solution.py:526
  29.0 2.7 %collective-permute-start.13 = (bf16[512,256]{1,0:T(8,128)(2,1)S(1)}, bf16[512,256]{1,0:T(8,128)(2,1)}, u32[]{:S(2)}, u32[]{:S(2)}) collective-permute-start(bf16[512,256]{1,0:T(8,128)(2,1)S(1)} %collective-permute-done.7), channel_id=1, source_target_pairs={{0,24},{8,0},{16,8},{24,16},{1,25},{9,1},{17,9},{25,17},{2,26},{10... | collective-permute-start | bytes 786440 | tf_op jit(solution)/shard_map/ppermute | solution.py:526
  31.6 4.0 %collective-permute-done.6 = bf16[512,256]{1,0:T(8,128)(2,1)} collective-permute-done((bf16[512,256]{1,0:T(8,128)(2,1)S(1)}, bf16[512,256]{1,0:T(8,128)(2,1)}, u32[]{:S(2)}, u32[]{:S(2)}) %collective-permute-start.6) | collective-permute-done | bytes 262176 | tf_op jit(solution)/shard_map/ppermute | solution.py:525
  35.7 3.7 %collective-permute-start.14 = (bf16[512,256]{1,0:T(8,128)(2,1)}, bf16[512,256]{1,0:T(8,128)(2,1)}, u32[]{:S(2)}, u32[]{:S(2)}) collective-permute-start(bf16[512,256]{1,0:T(8,128)(2,1)} %collective-permute-done.13.refs_12_), channel_id=1, source_target_pairs={{0,32},{32,0},{1,33},{33,1},{2,34},{34,2},{3,35},{35,3},{4,36},{36... | collective-permute-start | bytes 786440 | tf_op jit(solution)/shard_map/ppermute | solution.py:577
  39.5 2.4 %collective-permute-start.10 = (bf16[1024,256]{1,0:T(8,128)(2,1)}, bf16[1024,256]{1,0:T(8,128)(2,1)}, u32[]{:S(2)}, u32[]{:S(2)}) collective-permute-start(bf16[1024,256]{1,0:T(8,128)(2,1)} %copy-done.15), channel_id=1, source_target_pairs={{0,32},{32,0},{1,33},{33,1},{2,34},{34,2},{3,35},{35,3},{4,36},{36... | collective-permute-start | bytes 1572872 | tf_op jit(solution)/shard_map/ppermute | solution.py:577
  42.5 4.6 %all-to-all-start = ((f32[8,32,256]{2,1,0:T(8,128)}), f32[8,32,256]{2,1,0:T(8,128)S(1)}, u32[]{:S(2)}, u32[]{:S(2)}) async-start(f32[8,32,256]{2,1,0:T(8,128)} %broadcast_in_dim.4), calls=%async_computation | async-start | bytes 524288 | tf_op jit(solution)/shard_map/all_to_all | solution.py:497
  47.2 6.4 %all-to-all-done.all_ref = f32[8,32,256]{2,1,0:T(8,128)S(1)} async-done(((f32[8,32,256]{2,1,0:T(8,128)}), f32[8,32,256]{2,1,0:T(8,128)S(1)}, u32[]{:S(2)}, u32[]{:S(2)}) %all-to-all-start) | async-done | bytes 262176 | tf_op jit(solution)/shard_map/all_to_all | solution.py:497
  53.7 1.2 copy-done.10
  54.9 1.5 shard_map.119
  56.5 2.7 %collective-permute-start.9 = (bf16[1024,256]{1,0:T(8,128)(2,1)S(1)}, bf16[1024,256]{1,0:T(8,128)(2,1)S(1)}, u32[]{:S(2)}, u32[]{:S(2)}) collective-permute-start(bf16[1024,256]{1,0:T(8,128)(2,1)S(1)} %collective-permute-done.5.refs_4_), channel_id=1, source_target_pairs={{0,7},{1,0},{2,1},{3,2},{4,3},{5,4},{6,5},{7,6},{8,15},{9,8},{10,9... | collective-permute-start | bytes 1572872 | tf_op jit(solution)/shard_map/ppermute | solution.py:526
  59.2 1.6 %collective-permute-start.12 = (bf16[512,256]{1,0:T(8,128)(2,1)}, bf16[512,256]{1,0:T(8,128)(2,1)S(1)}, u32[]{:S(2)}, u32[]{:S(2)}) collective-permute-start(bf16[512,256]{1,0:T(8,128)(2,1)} %collective-permute-done.11.refs_11_), channel_id=1, source_target_pairs={{0,32},{32,0},{1,33},{33,1},{2,34},{34,2},{3,35},{35,3},{4,36},{36... | collective-permute-start | bytes 786440 | tf_op jit(solution)/shard_map/ppermute | solution.py:577
  60.8 1.4 collective-permute-done.12.refs_15_
  62.1 1.1 collective-permute-start.20
  63.2 0.9 collective-permute-start.19
  65.0 5.1 %collective-permute-done.8.refs_5_ = bf16[1024,256]{1,0:T(8,128)(2,1)S(1)} collective-permute-done((bf16[1024,256]{1,0:T(8,128)(2,1)S(1)}, bf16[1024,256]{1,0:T(8,128)(2,1)S(1)}, u32[]{:S(2)}, u32[]{:S(2)}) %collective-permute-start.8) | collective-permute-done | bytes 524320 | tf_op jit(solution)/shard_map/ppermute | solution.py:525
  70.1 2.5 %collective-permute-start.17 = (bf16[512,256]{1,0:T(8,128)(2,1)S(1)}, bf16[512,256]{1,0:T(8,128)(2,1)S(1)}, u32[]{:S(2)}, u32[]{:S(2)}) collective-permute-start(bf16[512,256]{1,0:T(8,128)(2,1)S(1)} %slice.7), channel_id=1, source_target_pairs={{0,7},{1,0},{2,1},{3,2},{4,3},{5,4},{6,5},{7,6},{8,15},{9,8},{10,9... | collective-permute-start | bytes 786440 | tf_op jit(solution)/shard_map/ppermute | solution.py:526
  72.6 3.4 %collective-permute-done.17.refs_8_ = bf16[512,256]{1,0:T(8,128)(2,1)S(1)} collective-permute-done((bf16[512,256]{1,0:T(8,128)(2,1)S(1)}, bf16[512,256]{1,0:T(8,128)(2,1)S(1)}, u32[]{:S(2)}, u32[]{:S(2)}) %collective-permute-start.17) | collective-permute-done | bytes 262176 | tf_op jit(solution)/shard_map/ppermute | solution.py:526
  76.0 3.3 %collective-permute-done.16.refs_7_ = bf16[512,256]{1,0:T(8,128)(2,1)S(1)} collective-permute-done((bf16[512,256]{1,0:T(8,128)(2,1)S(1)}, bf16[512,256]{1,0:T(8,128)(2,1)S(1)}, u32[]{:S(2)}, u32[]{:S(2)}) %collective-permute-start.16) | collective-permute-done | bytes 262176 | tf_op jit(solution)/shard_map/ppermute | solution.py:525
  79.3 2.2 %copy-done = bf16[8192,256]{1,0:T(8,128)(2,1)S(1)} copy-done((bf16[8192,256]{1,0:T(8,128)(2,1)S(1)}, bf16[8192,256]{1,0:T(8,128)(2,1)}, u32[]{:S(2)}) %copy-start) | copy-done | bytes 4194328
  81.5 1.0 copy-done.14
  82.6 1.0 copy-done.16
  83.6 6.9 %shard_map.120 = (bf16[1024,256]{1,0:T(8,128)(2,1)S(1)}, bf16[1024,256]{1,0:T(8,128)(2,1)S(1)}, bf16[1024,256]{1,0:T(8,128)(2,1)S(1)}, bf16[1024,256]{1,0:T(8,128)(2,1)S(1)}) custom-call(s32[4]{0:T(128)S(1)} %pad_add_fusion.here_ref, bf16[1024,256]{1,0:T(8,128)(2,1)S(1)} %copy-done.1, bf16[1024,256]{1,0:T(8,128)(2,1)S(1)} %collective-permute-done.refs_1_, ...), custom_call_target="tpu_custom_call" | custom-call | flops 1000 | bytes 22140000 | tf_op jit(solution)/shard_map/pallas_call | solution.py:473
  90.5 3.7 %shard_map.121 = bf16[4,256,1024]{2,1,0:T(8,128)(2,1)S(1)} custom-call(s32[4]{0:T(128)S(1)} %pad_add_fusion.here_ref, bf16[1024,256]{1,0:T(8,128)(2,1)S(1)} %copy-done.1, bf16[1024,256]{1,0:T(8,128)(2,1)S(1)} %collective-permute-done.refs_1_, bf16[1024,256]{1,0:T(8,128)(2,1)S(1)} %collective-permute-done.1.refs_2_, ...), custom_call_target="tpu_custom_call" | custom-call | flops 1000 | bytes 1845000 | tf_op jit(solution)/shard_map/pallas_call | solution.py:473
  94.2 3.7 %collective-permute-start.21 = (bf16[4,256,1024]{2,1,0:T(8,128)(2,1)S(1)}, bf16[4,256,1024]{2,1,0:T(8,128)(2,1)S(1)}, u32[]{:S(2)}, u32[]{:S(2)}) collective-permute-start(bf16[4,256,1024]{2,1,0:T(8,128)(2,1)S(1)} %shard_map.121), channel_id=1, source_target_pairs={{0,32},{32,0},{1,33},{33,1},{2,34},{34,2},{3,35},{35,3},{4,36},{36... | collective-permute-start | bytes 6291464 | tf_op jit(solution)/shard_map/ppermute | solution.py:611
  97.9 2.0 %collective-permute-start.22 = (bf16[1024,256]{1,0:T(8,128)(2,1)S(1)}, bf16[1024,256]{1,0:T(8,128)(2,1)S(1)}, u32[]{:S(2)}, u32[]{:S(2)}) collective-permute-start(bf16[1024,256]{1,0:T(8,128)(2,1)S(1)} %get-tuple-element.72), channel_id=1, source_target_pairs={{0,16},{8,24},{16,0},{24,8},{1,17},{9,25},{17,1},{25,9},{2,18},{10... | collective-permute-start | bytes 1572872 | tf_op jit(solution)/shard_map/ppermute | solution.py:598
  100.0 1.5 collective-permute-start.24
  101.7 3.8 %shard_map.122 = (bf16[256,1024]{1,0:T(8,128)(2,1)S(1)}, bf16[256,1024]{1,0:T(8,128)(2,1)S(1)}, bf16[256,1024]{1,0:T(8,128)(2,1)S(1)}, bf16[256,1024]{1,0:T(8,128)(2,1)S(1)}) custom-call(s32[4]{0:T(128)S(1)} %pad_add_fusion.here_ref, bf16[1024,256]{1,0:T(8,128)(2,1)S(1)} %copy-done.1, bf16[1024,256]{1,0:T(8,128)(2,1)S(1)} %collective-permute-done.refs_1_, ...), custom_call_target="tpu_custom_call" | custom-call | flops 1000 | bytes 1845000 | tf_op jit(solution)/shard_map/pallas_call | solution.py:473
  105.9 1.8 %collective-permute-start.26 = (bf16[256,1024]{1,0:T(8,128)(2,1)S(1)}, bf16[256,1024]{1,0:T(8,128)(2,1)S(1)}, u32[]{:S(2)}, u32[]{:S(2)}) collective-permute-start(bf16[256,1024]{1,0:T(8,128)(2,1)S(1)} %get-tuple-element.69), channel_id=1, source_target_pairs={{0,128},{64,192},{128,0},{192,64},{1,129},{65,193},{129,1},{193,65... | collective-permute-start | bytes 1572872 | tf_op jit(solution)/shard_map/ppermute | solution.py:623
  107.7 5.3 %collective-permute-done.22.p1_ref = bf16[1024,256]{1,0:T(8,128)(2,1)S(1)} collective-permute-done((bf16[1024,256]{1,0:T(8,128)(2,1)S(1)}, bf16[1024,256]{1,0:T(8,128)(2,1)S(1)}, u32[]{:S(2)}, u32[]{:S(2)}) %collective-permute-start.22) | collective-permute-done | bytes 524320 | tf_op jit(solution)/shard_map/ppermute | solution.py:598
  113.0 0.9 collective-permute-start.27
  113.8 9.1 %collective-permute-done.23.p2_ref = bf16[1024,256]{1,0:T(8,128)(2,1)S(1)} collective-permute-done((bf16[1024,256]{1,0:T(8,128)(2,1)S(1)}, bf16[1024,256]{1,0:T(8,128)(2,1)S(1)}, u32[]{:S(2)}, u32[]{:S(2)}) %collective-permute-start.23) | collective-permute-done | bytes 524320 | tf_op jit(solution)/shard_map/ppermute | solution.py:598
  122.9 1.6 %collective-permute-done.24.p3_ref = bf16[1024,256]{1,0:T(8,128)(2,1)S(1)} collective-permute-done((bf16[1024,256]{1,0:T(8,128)(2,1)S(1)}, bf16[1024,256]{1,0:T(8,128)(2,1)S(1)}, u32[]{:S(2)}, u32[]{:S(2)}) %collective-permute-start.24) | collective-permute-done | bytes 524320 | tf_op jit(solution)/shard_map/ppermute | solution.py:598
  124.6 4.5 %shard_map.123 = (bf16[1024,256]{1,0:T(8,128)(2,1)}, f32[1024,256]{1,0:T(8,128)S(1)}, f32[48,256]{1,0:T(8,128)S(1)}) custom-call(bf16[1024,256]{1,0:T(8,128)(2,1)S(1)} %get-tuple-element.71.own_ref, bf16[1024,256]{1,0:T(8,128)(2,1)S(1)} %collective-permute-done.22.p1_ref, bf16[1024,256]{1,0:T(8,128)(2,1)S(1)} %collective-permute-done.23.p2_ref, ...), custom_call_target="tpu_custom_call" | custom-call | flops 1000 | bytes 73800000 | tf_op jit(solution)/shard_map/pallas_call | solution.py:473
  129.1 1.3 collective-permute-done.26.c_ref
  130.4 1.1 collective-permute-done.27.d_ref
  132.5 23.2 %all_to_all.10.all_ref = f32[8,48,256]{2,1,0:T(8,128)S(1)} all-to-all(f32[8,48,256]{2,1,0:T(8,128)S(1)} %broadcast_in_dim.5), channel_id=1, replica_groups=mesh['y'=4,'core'=2,'x'=4,'z'=8] {'y','core'}, dimensions={0} | all-to-all | bytes 786432 | tf_op jit(solution)/shard_map/all_to_all | solution.py:497
  155.7 2.5 %shard_map.125 = (bf16[1024,256]{1,0:T(8,128)(2,1)}, bf16[1024,256]{1,0:T(8,128)(2,1)}, f32[16,16]{1,0:T(8,128)}, f32[16,16]{1,0:T(8,128)}) custom-call(s32[4]{0:T(128)S(1)} %pad_add_fusion.here_ref, f32[8,48,256]{2,1,0:T(8,128)S(1)} %all_to_all.10.all_ref, f32[1024,256]{1,0:T(8,128)S(1)} %get-tuple-element.83.back_ref, bf16[1024,256]{1,0:T(8,128)(2,1)S(1)} %copy-done.4, ...), custom_call_target="tpu_custom_call" | custom-call | flops 1000 | bytes 9225000 | tf_op jit(solution)/shard_map/pallas_call | solution.py:473
  158.2 1.2 shard_map.126
  (71 shorter events, 7.4 us)
Async XLA Ops:
  0.6 78.7 %copy-start.1 = (bf16[1024,256]{1,0:T(8,128)(2,1)S(1)}, bf16[1024,256]{1,0:T(8,128)(2,1)}, u32[]{:S(2)}) copy-start(bf16[1024,256]{1,0:T(8,128)(2,1)} %refs_0_.4) | copy-start | bytes 1572868
  0.6 53.0 %copy-start.20 = (f32[16,16]{1,0:T(8,128)S(1)}, f32[16,16]{1,0:T(8,128)}, u32[]{:S(2)}) copy-start(f32[16,16]{1,0:T(8,128)} %res_ref.7) | copy-start | bytes 3076
  0.7 53.0 %copy-start.18 = (f32[16,16]{1,0:T(8,128)S(1)}, f32[16,16]{1,0:T(8,128)}, u32[]{:S(2)}) copy-start(f32[16,16]{1,0:T(8,128)} %rate_ref.7) | copy-start | bytes 3076
  0.7 53.0 %copy-start.2 = (bf16[1024,256]{1,0:T(8,128)(2,1)S(1)}, bf16[1024,256]{1,0:T(8,128)(2,1)}, u32[]{:S(2)}) copy-start(bf16[1024,256]{1,0:T(8,128)(2,1)} %query_ref.3) | copy-start | bytes 1572868
  0.7 24.0 %collective-permute-start.1 = (bf16[1024,256]{1,0:T(8,128)(2,1)}, bf16[1024,256]{1,0:T(8,128)(2,1)S(1)}, u32[]{:S(2)}, u32[]{:S(2)}) collective-permute-start(bf16[1024,256]{1,0:T(8,128)(2,1)} %refs_0_.4), channel_id=1, source_target_pairs={{0,7},{1,0},{2,1},{3,2},{4,3},{5,4},{6,5},{7,6},{8,15},{9,8},{10,9... | collective-permute-start | bytes 1572872 | tf_op jit(solution)/shard_map/ppermute | solution.py:526
  7.2 17.5 %collective-permute-start = (bf16[1024,256]{1,0:T(8,128)(2,1)}, bf16[1024,256]{1,0:T(8,128)(2,1)S(1)}, u32[]{:S(2)}, u32[]{:S(2)}) collective-permute-start(bf16[1024,256]{1,0:T(8,128)(2,1)} %refs_0_.4), channel_id=1, source_target_pairs={{0,1},{1,2},{2,3},{3,4},{4,5},{5,6},{6,7},{7,0},{8,9},{9,10},{10,1... | collective-permute-start | bytes 1572872 | tf_op jit(solution)/shard_map/ppermute | solution.py:525
  9.4 15.3 %collective-permute-start.3 = (bf16[1024,256]{1,0:T(8,128)(2,1)}, bf16[1024,256]{1,0:T(8,128)(2,1)S(1)}, u32[]{:S(2)}, u32[]{:S(2)}) collective-permute-start(bf16[1024,256]{1,0:T(8,128)(2,1)} %get-tuple-element.90), channel_id=1, source_target_pairs={{0,24},{8,0},{16,8},{24,16},{1,25},{9,1},{17,9},{25,17},{2,26},{10... | collective-permute-start | bytes 1572872 | tf_op jit(solution)/shard_map/ppermute | solution.py:526
  11.9 13.6 %collective-permute-start.2 = (bf16[1024,256]{1,0:T(8,128)(2,1)}, bf16[1024,256]{1,0:T(8,128)(2,1)S(1)}, u32[]{:S(2)}, u32[]{:S(2)}) collective-permute-start(bf16[1024,256]{1,0:T(8,128)(2,1)} %get-tuple-element.91), channel_id=1, source_target_pairs={{0,8},{8,16},{16,24},{24,0},{1,9},{9,17},{17,25},{25,1},{2,10},{10... | collective-permute-start | bytes 1572872 | tf_op jit(solution)/shard_map/ppermute | solution.py:525
  12.9 16.0 %collective-permute-start.7 = (bf16[512,256]{1,0:T(8,128)(2,1)S(1)}, bf16[512,256]{1,0:T(8,128)(2,1)S(1)}, u32[]{:S(2)}, u32[]{:S(2)}) collective-permute-start(bf16[512,256]{1,0:T(8,128)(2,1)S(1)} %get-tuple-element.88), channel_id=1, source_target_pairs={{0,24},{8,0},{16,8},{24,16},{1,25},{9,1},{17,9},{25,17},{2,26},{10... | collective-permute-start | bytes 786440 | tf_op jit(solution)/shard_map/ppermute | solution.py:526
  15.7 1.0 copy-start.3
  16.7 1.0 copy-start.5
  21.9 1.0 copy-start.7
  22.9 1.0 copy-start.9
  24.7 0.8 copy-start.13
  25.5 0.8 copy-start.15
  26.3 13.2 %collective-permute-start.4 = (bf16[1024,256]{1,0:T(8,128)(2,1)S(1)}, bf16[1024,256]{1,0:T(8,128)(2,1)S(1)}, u32[]{:S(2)}, u32[]{:S(2)}) collective-permute-start(bf16[1024,256]{1,0:T(8,128)(2,1)S(1)} %collective-permute-done.refs_1_), channel_id=1, source_target_pairs={{0,1},{1,2},{2,3},{3,4},{4,5},{5,6},{6,7},{7,0},{8,9},{9,10},{10,1... | collective-permute-start | bytes 1572872 | tf_op jit(solution)/shard_map/ppermute | solution.py:525
  26.3 30.1 %collective-permute-start.5 = (bf16[1024,256]{1,0:T(8,128)(2,1)S(1)}, bf16[1024,256]{1,0:T(8,128)(2,1)S(1)}, u32[]{:S(2)}, u32[]{:S(2)}) collective-permute-start(bf16[1024,256]{1,0:T(8,128)(2,1)S(1)} %collective-permute-done.1.refs_2_), channel_id=1, source_target_pairs={{0,7},{1,0},{2,1},{3,2},{4,3},{5,4},{6,5},{7,6},{8,15},{9,8},{10,9... | collective-permute-start | bytes 1572872 | tf_op jit(solution)/shard_map/ppermute | solution.py:526
  28.9 6.7 %collective-permute-start.6 = (bf16[512,256]{1,0:T(8,128)(2,1)S(1)}, bf16[512,256]{1,0:T(8,128)(2,1)}, u32[]{:S(2)}, u32[]{:S(2)}) collective-permute-start(bf16[512,256]{1,0:T(8,128)(2,1)S(1)} %get-tuple-element.89), channel_id=1, source_target_pairs={{0,8},{8,16},{16,24},{24,0},{1,9},{9,17},{17,25},{25,1},{2,10},{10... | collective-permute-start | bytes 786440 | tf_op jit(solution)/shard_map/ppermute | solution.py:525
  29.0 6.7 %collective-permute-start.13 = (bf16[512,256]{1,0:T(8,128)(2,1)S(1)}, bf16[512,256]{1,0:T(8,128)(2,1)}, u32[]{:S(2)}, u32[]{:S(2)}) collective-permute-start(bf16[512,256]{1,0:T(8,128)(2,1)S(1)} %collective-permute-done.7), channel_id=1, source_target_pairs={{0,24},{8,0},{16,8},{24,16},{1,25},{9,1},{17,9},{25,17},{2,26},{10... | collective-permute-start | bytes 786440 | tf_op jit(solution)/shard_map/ppermute | solution.py:526
  35.7 20.8 %collective-permute-start.11 = (bf16[512,256]{1,0:T(8,128)(2,1)}, bf16[512,256]{1,0:T(8,128)(2,1)}, u32[]{:S(2)}, u32[]{:S(2)}) collective-permute-start(bf16[512,256]{1,0:T(8,128)(2,1)} %collective-permute-done.6), channel_id=1, source_target_pairs={{0,8},{8,16},{16,24},{24,0},{1,9},{9,17},{17,25},{25,1},{2,10},{10... | collective-permute-start | bytes 786440 | tf_op jit(solution)/shard_map/ppermute | solution.py:525
  35.7 23.5 %collective-permute-start.14 = (bf16[512,256]{1,0:T(8,128)(2,1)}, bf16[512,256]{1,0:T(8,128)(2,1)}, u32[]{:S(2)}, u32[]{:S(2)}) collective-permute-start(bf16[512,256]{1,0:T(8,128)(2,1)} %collective-permute-done.13.refs_12_), channel_id=1, source_target_pairs={{0,32},{32,0},{1,33},{33,1},{2,34},{34,2},{3,35},{35,3},{4,36},{36... | collective-permute-start | bytes 786440 | tf_op jit(solution)/shard_map/ppermute | solution.py:577
  39.4 23.9 %collective-permute-start.15 = (bf16[1024,256]{1,0:T(8,128)(2,1)}, bf16[1024,256]{1,0:T(8,128)(2,1)}, u32[]{:S(2)}, u32[]{:S(2)}) collective-permute-start(bf16[1024,256]{1,0:T(8,128)(2,1)} %copy-done.13), channel_id=1, source_target_pairs={{0,32},{32,0},{1,33},{33,1},{2,34},{34,2},{3,35},{35,3},{4,36},{36... | collective-permute-start | bytes 1572872 | tf_op jit(solution)/shard_map/ppermute | solution.py:577
  39.5 24.7 %collective-permute-start.10 = (bf16[1024,256]{1,0:T(8,128)(2,1)}, bf16[1024,256]{1,0:T(8,128)(2,1)}, u32[]{:S(2)}, u32[]{:S(2)}) collective-permute-start(bf16[1024,256]{1,0:T(8,128)(2,1)} %copy-done.15), channel_id=1, source_target_pairs={{0,32},{32,0},{1,33},{33,1},{2,34},{34,2},{3,35},{35,3},{4,36},{36... | collective-permute-start | bytes 1572872 | tf_op jit(solution)/shard_map/ppermute | solution.py:577
  42.5 11.1 %all-to-all-start = ((f32[8,32,256]{2,1,0:T(8,128)}), f32[8,32,256]{2,1,0:T(8,128)S(1)}, u32[]{:S(2)}, u32[]{:S(2)}) async-start(f32[8,32,256]{2,1,0:T(8,128)} %broadcast_in_dim.4), calls=%async_computation | async-start | bytes 524288 | tf_op jit(solution)/shard_map/all_to_all | solution.py:497
  53.6 1.2 copy-start.10
  56.4 13.7 %collective-permute-start.8 = (bf16[1024,256]{1,0:T(8,128)(2,1)S(1)}, bf16[1024,256]{1,0:T(8,128)(2,1)S(1)}, u32[]{:S(2)}, u32[]{:S(2)}) collective-permute-start(bf16[1024,256]{1,0:T(8,128)(2,1)S(1)} %collective-permute-done.4.refs_3_), channel_id=1, source_target_pairs={{0,1},{1,2},{2,3},{3,4},{4,5},{5,6},{6,7},{7,0},{8,9},{9,10},{10,1... | collective-permute-start | bytes 1572872 | tf_op jit(solution)/shard_map/ppermute | solution.py:525
  56.5 13.6 %collective-permute-start.9 = (bf16[1024,256]{1,0:T(8,128)(2,1)S(1)}, bf16[1024,256]{1,0:T(8,128)(2,1)S(1)}, u32[]{:S(2)}, u32[]{:S(2)}) collective-permute-start(bf16[1024,256]{1,0:T(8,128)(2,1)S(1)} %collective-permute-done.5.refs_4_), channel_id=1, source_target_pairs={{0,7},{1,0},{2,1},{3,2},{4,3},{5,4},{6,5},{7,6},{8,15},{9,8},{10,9... | collective-permute-start | bytes 1572872 | tf_op jit(solution)/shard_map/ppermute | solution.py:526
  59.2 3.0 %collective-permute-start.12 = (bf16[512,256]{1,0:T(8,128)(2,1)}, bf16[512,256]{1,0:T(8,128)(2,1)S(1)}, u32[]{:S(2)}, u32[]{:S(2)}) collective-permute-start(bf16[512,256]{1,0:T(8,128)(2,1)} %collective-permute-done.11.refs_11_), channel_id=1, source_target_pairs={{0,32},{32,0},{1,33},{33,1},{2,34},{34,2},{3,35},{35,3},{4,36},{36... | collective-permute-start | bytes 786440 | tf_op jit(solution)/shard_map/ppermute | solution.py:577
  62.1 28.4 %collective-permute-start.20 = (bf16[256,1024]{1,0:T(8,128)(2,1)S(1)}, bf16[256,1024]{1,0:T(8,128)(2,1)S(1)}, u32[]{:S(2)}, u32[]{:S(2)}) collective-permute-start(bf16[256,1024]{1,0:T(8,128)(2,1)S(1)} %get-tuple-element.66.refs_9_.refs_10_), channel_id=1, source_target_pairs={{0,24},{8,0},{16,8},{24,16},{1,25},{9,1},{17,9},{25,17},{2,26},{10... | collective-permute-start | bytes 1572872 | tf_op jit(solution)/shard_map/ppermute | solution.py:575
  63.2 27.3 %collective-permute-start.19 = (bf16[256,1024]{1,0:T(8,128)(2,1)S(1)}, bf16[256,1024]{1,0:T(8,128)(2,1)S(1)}, u32[]{:S(2)}, u32[]{:S(2)}) collective-permute-start(bf16[256,1024]{1,0:T(8,128)(2,1)S(1)} %get-tuple-element.66.refs_9_.refs_10_), channel_id=1, source_target_pairs={{0,16},{8,24},{16,0},{24,8},{1,17},{9,25},{17,1},{25,9},{2,18},{10... | collective-permute-start | bytes 1572872 | tf_op jit(solution)/shard_map/ppermute | solution.py:575
  64.1 26.4 %collective-permute-start.18 = (bf16[256,1024]{1,0:T(8,128)(2,1)S(1)}, bf16[256,1024]{1,0:T(8,128)(2,1)S(1)}, u32[]{:S(2)}, u32[]{:S(2)}) collective-permute-start(bf16[256,1024]{1,0:T(8,128)(2,1)S(1)} %get-tuple-element.66.refs_9_.refs_10_), channel_id=1, source_target_pairs={{0,8},{8,16},{16,24},{24,0},{1,9},{9,17},{17,25},{25,1},{2,10},{10... | collective-permute-start | bytes 1572872 | tf_op jit(solution)/shard_map/ppermute | solution.py:575
  70.1 5.9 %collective-permute-start.17 = (bf16[512,256]{1,0:T(8,128)(2,1)S(1)}, bf16[512,256]{1,0:T(8,128)(2,1)S(1)}, u32[]{:S(2)}, u32[]{:S(2)}) collective-permute-start(bf16[512,256]{1,0:T(8,128)(2,1)S(1)} %slice.7), channel_id=1, source_target_pairs={{0,7},{1,0},{2,1},{3,2},{4,3},{5,4},{6,5},{7,6},{8,15},{9,8},{10,9... | collective-permute-start | bytes 786440 | tf_op jit(solution)/shard_map/ppermute | solution.py:526
  72.6 6.7 %collective-permute-start.16 = (bf16[512,256]{1,0:T(8,128)(2,1)S(1)}, bf16[512,256]{1,0:T(8,128)(2,1)S(1)}, u32[]{:S(2)}, u32[]{:S(2)}) collective-permute-start(bf16[512,256]{1,0:T(8,128)(2,1)S(1)} %slice.6), channel_id=1, source_target_pairs={{0,1},{1,2},{2,3},{3,4},{4,5},{5,6},{6,7},{7,0},{8,9},{9,10},{10,1... | collective-permute-start | bytes 786440 | tf_op jit(solution)/shard_map/ppermute | solution.py:525
  79.3 2.2 %copy-start = (bf16[8192,256]{1,0:T(8,128)(2,1)S(1)}, bf16[8192,256]{1,0:T(8,128)(2,1)}, u32[]{:S(2)}) copy-start(bf16[8192,256]{1,0:T(8,128)(2,1)} %refs_9_.1) | copy-start | bytes 12582916
  81.5 1.0 copy-start.14
  82.6 1.0 copy-start.16
  94.2 7.5 %collective-permute-start.21 = (bf16[4,256,1024]{2,1,0:T(8,128)(2,1)S(1)}, bf16[4,256,1024]{2,1,0:T(8,128)(2,1)S(1)}, u32[]{:S(2)}, u32[]{:S(2)}) collective-permute-start(bf16[4,256,1024]{2,1,0:T(8,128)(2,1)S(1)} %shard_map.121), channel_id=1, source_target_pairs={{0,32},{32,0},{1,33},{33,1},{2,34},{34,2},{3,35},{35,3},{4,36},{36... | collective-permute-start | bytes 6291464 | tf_op jit(solution)/shard_map/ppermute | solution.py:611
  97.9 15.0 %collective-permute-start.22 = (bf16[1024,256]{1,0:T(8,128)(2,1)S(1)}, bf16[1024,256]{1,0:T(8,128)(2,1)S(1)}, u32[]{:S(2)}, u32[]{:S(2)}) collective-permute-start(bf16[1024,256]{1,0:T(8,128)(2,1)S(1)} %get-tuple-element.72), channel_id=1, source_target_pairs={{0,16},{8,24},{16,0},{24,8},{1,17},{9,25},{17,1},{25,9},{2,18},{10... | collective-permute-start | bytes 1572872 | tf_op jit(solution)/shard_map/ppermute | solution.py:598
  100.0 22.9 %collective-permute-start.23 = (bf16[1024,256]{1,0:T(8,128)(2,1)S(1)}, bf16[1024,256]{1,0:T(8,128)(2,1)S(1)}, u32[]{:S(2)}, u32[]{:S(2)}) collective-permute-start(bf16[1024,256]{1,0:T(8,128)(2,1)S(1)} %get-tuple-element.73), channel_id=1, source_target_pairs={{0,24},{8,0},{16,8},{24,16},{1,25},{9,1},{17,9},{25,17},{2,26},{10... | collective-permute-start | bytes 1572872 | tf_op jit(solution)/shard_map/ppermute | solution.py:598
  100.0 24.6 %copy-start.8 = (f32[16,128,128]{2,1,0:T(8,128)S(1)}, f32[16,128,128]{2,1,0:T(8,128)}, u32[]{:S(2)}) copy-start(f32[16,128,128]{2,1,0:T(8,128)} %copy-done.7) | copy-start | bytes 3145732
  100.0 24.6 %copy-start.12 = (bf16[256,1024]{1,0:T(8,128)(2,1)S(1)}, bf16[256,1024]{1,0:T(8,128)(2,1)}, u32[]{:S(2)}) copy-start(bf16[256,1024]{1,0:T(8,128)(2,1)} %copy-done.11) | copy-start | bytes 1572868
  100.0 24.6 %collective-permute-start.24 = (bf16[1024,256]{1,0:T(8,128)(2,1)S(1)}, bf16[1024,256]{1,0:T(8,128)(2,1)S(1)}, u32[]{:S(2)}, u32[]{:S(2)}) collective-permute-start(bf16[1024,256]{1,0:T(8,128)(2,1)S(1)} %get-tuple-element.74), channel_id=1, source_target_pairs={{0,8},{8,16},{16,24},{24,0},{1,9},{9,17},{17,25},{25,1},{2,10},{10... | collective-permute-start | bytes 1572872 | tf_op jit(solution)/shard_map/ppermute | solution.py:598
  105.5 23.5 %collective-permute-start.25 = (bf16[256,1024]{1,0:T(8,128)(2,1)S(1)}, bf16[256,1024]{1,0:T(8,128)(2,1)S(1)}, u32[]{:S(2)}, u32[]{:S(2)}) collective-permute-start(bf16[256,1024]{1,0:T(8,128)(2,1)S(1)} %get-tuple-element.68), channel_id=1, source_target_pairs={{0,64},{64,128},{128,192},{192,0},{1,65},{65,129},{129,193},{193,1... | collective-permute-start | bytes 1572872 | tf_op jit(solution)/shard_map/ppermute | solution.py:623
  105.9 24.5 %collective-permute-start.26 = (bf16[256,1024]{1,0:T(8,128)(2,1)S(1)}, bf16[256,1024]{1,0:T(8,128)(2,1)S(1)}, u32[]{:S(2)}, u32[]{:S(2)}) collective-permute-start(bf16[256,1024]{1,0:T(8,128)(2,1)S(1)} %get-tuple-element.69), channel_id=1, source_target_pairs={{0,128},{64,192},{128,0},{192,64},{1,129},{65,193},{129,1},{193,65... | collective-permute-start | bytes 1572872 | tf_op jit(solution)/shard_map/ppermute | solution.py:623
  113.0 18.5 %collective-permute-start.27 = (bf16[256,1024]{1,0:T(8,128)(2,1)S(1)}, bf16[256,1024]{1,0:T(8,128)(2,1)S(1)}, u32[]{:S(2)}, u32[]{:S(2)}) collective-permute-start(bf16[256,1024]{1,0:T(8,128)(2,1)S(1)} %get-tuple-element.70), channel_id=1, source_target_pairs={{0,192},{64,0},{128,64},{192,128},{1,193},{65,1},{129,65},{193,129... | collective-permute-start | bytes 1572872 | tf_op jit(solution)/shard_map/ppermute | solution.py:623
  124.5 31.1 %copy-start.4 = (bf16[1024,256]{1,0:T(8,128)(2,1)S(1)}, bf16[1024,256]{1,0:T(8,128)(2,1)}, u32[]{:S(2)}) copy-start(bf16[1024,256]{1,0:T(8,128)(2,1)} %key_ref.3) | copy-start | bytes 1572868
  124.6 31.1 %copy-start.6 = (bf16[1024,256]{1,0:T(8,128)(2,1)S(1)}, bf16[1024,256]{1,0:T(8,128)(2,1)}, u32[]{:S(2)}) copy-start(bf16[1024,256]{1,0:T(8,128)(2,1)} %value_ref.3) | copy-start | bytes 1572868
  131.7 26.5 %collective-permute-start.28 = (bf16[256,1024]{1,0:T(8,128)(2,1)S(1)}, bf16[256,1024]{1,0:T(8,128)(2,1)S(1)}, u32[]{:S(2)}, u32[]{:S(2)}) collective-permute-start(bf16[256,1024]{1,0:T(8,128)(2,1)S(1)} %shard_map.124), channel_id=1, source_target_pairs={{0,0},{8,72},{16,144},{24,216},{64,8},{72,80},{80,152},{88,192},{1... | collective-permute-start | bytes 1572872 | tf_op jit(solution)/shard_map/ppermute | solution.py:647
  (3 other events, 2.2 us)
where the time goes:
time: 160 us; the launch traced here: 159 us
  starting transfers between devices  48.4 us (30%)
  waiting for transfers between devices  43.1 us (27%)
  Pallas kernels  27.1 us (17%)
  blocking collectives  23.2 us (14%)
  local copies, waits for them, and re-layouts  16.7 us (10%)
    pallas_call x9, Pallas kernels, call(): pl.pallas_call(kernel, out_shape=outs, in_specs=[pl.BlockSpec(memory_spac...  27.1 us
    all_to_all x1, blocking collectives, gather_ctx(): lax.all_to_all(jnp.broadcast_to(item[None], (n,) + item.shape), CTX, spli...  23.2 us
    ppermute x7, starting transfers between devices, both_ways(): lax.ppermute(pair[1], axis, shift(n, -1))  22.2 us
    ppermute x3, waiting for transfers between devices, local(): lax.ppermute(part, 'x', shift(nx, -i))  16 us
    ppermute x7, waiting for transfers between devices, both_ways(): lax.ppermute(pair[0], axis, shift(n, 1))  13.2 us
    unnamed x42, local copies, waits for them, and re-layouts  12.6 us
    ppermute x4, starting transfers between devices, local(): others = [lax.ppermute(piece, 'core', swap) for piece in fetched]  7.74 us
    all_to_all x1, waiting for transfers between devices, gather_ctx(): lax.all_to_all(jnp.broadcast_to(item[None], (n,) + item.shape), CTX, spli...  6.43 us
  transfers between devices with their start and end apart: 30, of which 13 were waited for; matrix products, arithmetic and copies ran while one was open for 3% of the time, Pallas kernels for 14%

commit v1 on v0

--- a/solution.py
+++ b/solution.py
@@ -175,24 +175,34 @@
     return mm(l_hi, s_hi) + mm(l_hi, s_lo) + mm(l_lo, s_hi)
 
 
+def arrived(y, core, own_ref, other_ref, pair_refs):
+    count = len(pair_refs) + 1
+    yield 2 * y + core, lambda lo, hi: own_ref[lo:hi, :]
+    yield 2 * y + 1 - core, lambda lo, hi: other_ref[lo:hi, :]
+    for i, ref in enumerate(pair_refs, 1):
+        far = lax.rem(y - i + count, count)
+        yield 2 * far + core, lambda lo, hi, ref=ref: ref[0, lo:hi, :]
+        yield 2 * far + 1 - core, lambda lo, hi, ref=ref: ref[1, lo:hi, :]
+
+
 def enter_kernel(
-    here_ref, all_ref, conv_ref, query_ref, rate_ref, res_ref, conv_out_ref, gated_ref, in_ref
+    here_ref, own_ref, other_ref, p1_ref, p2_ref, p3_ref, conv_ref, query_ref, rate_ref, res_ref, conv_out_ref, gated_ref, in_ref
 ):
     tokens, channels = conv_ref.shape
     groups, poles = rate_ref.shape
-    mine = 2 * here_ref[0] + here_ref[1]
-    count = all_ref.shape[0]
+    y, core = here_ref[0], here_ref[1]
+    mine = 2 * y + core
     rate_nc = by_channel(rate_ref[...], channels)
     rate_row, res_row = by_column(rate_ref[...]).T, by_column(res_ref[...]).T
     state = jnp.zeros((poles, channels), F32)
     slope = jnp.zeros((poles, channels), F32)
-    for place in range(count):
+    for place, read in arrived(y, core, own_ref, other_ref, (p1_ref, p2_ref, p3_ref)):
         gap = (mine - 1 - place).astype(F32)
         lag = jnp.maximum(gap, 0.0) * float(tokens)
         weight = jnp.where(gap >= 0.0, jnp.exp(-rate_nc * lag), 0.0)
-        end = all_ref[place, :poles, :]
+        end = read(0, poles)
         state = state + weight * end
-        slope = slope + weight * (all_ref[place, poles:, :] + lag * end)
+        slope = slope + weight * (read(poles, 2 * poles) + lag * end)
     in_ref[:poles, :] = state
     in_ref[poles:, :] = slope
     tall = spread(state, groups)
@@ -398,42 +408,30 @@
 
 
 def project_kernel(here_ref, *refs):
-    blocks, weight_ref, fetched, others = refs[:9], refs[9], refs[10:14], refs[14:18]
-    p0_ref, p1_ref, p2_ref, p3_ref, f_ref, w_ref, f_sem, w_sem = refs[18:]
-    core, z, x = here_ref[1], here_ref[2], here_ref[3]
+    blocks, weights_ref, outs, (f_ref, w_ref, f_sem, w_sem) = refs[:9], refs[9], refs[10:14], refs[14:]
+    z, x = here_ref[2], here_ref[3]
     nz, tokens, _ = f_ref.shape
-    rows_x = w_ref.shape[1]
-    half = rows_x // 2
+    nx = weights_ref.shape[0]
     feat = [
         pltpu.make_async_copy(ref, place(at), signal(at))
         for at, ref, place, signal in block_copies(z, blocks, f_ref, f_sem)
     ]
-    weight = {
-        0: [
-            pltpu.make_async_copy(
-                weight_ref.at[pl.ds(pl.multiple_of(x * rows_x, rows_x), rows_x), :], w_ref.at[0], w_sem.at[0]
-            )
-        ]
-    }
-    for k, (i, first) in enumerate(((1, 0), (2, 0), (2, half // 2), (3, 0))):
-        for j, (ref, base) in enumerate(((fetched[k], core * half), (others[k], (1 - core) * half))):
-            size = ref.shape[0]
-            place = pl.ds(pl.multiple_of(base + first, half // 2), size)
-            weight.setdefault(i, []).append(
-                pltpu.make_async_copy(ref, w_ref.at[i, place, :], w_sem.at[2 * k + j + 1])
-            )
-    for copy in weight[2] + feat + weight[1] + weight[3] + weight[0]:
+    order = (2, 1, 3, 0)
+    weight = {}
+    for i in order:
+        at = lax.rem(x - i + nx, nx)
+        weight[i] = pltpu.make_async_copy(weights_ref.at[at], w_ref.at[i], w_sem.at[i])
+    for copy in [weight[order[0]]] + feat + [weight[i] for i in order[1:]]:
         copy.start()
     for copy in feat:
         copy.wait()
     tile = TILE
-    for i, out in ((2, p2_ref), (1, p1_ref), (3, p3_ref), (0, p0_ref)):
-        for copy in weight[i]:
-            copy.wait()
+    for i in order:
+        weight[i].wait()
         for m in range(tokens // tile):
             at = slice(m * tile, (m + 1) * tile)
             lhs = jnp.concatenate([f_ref[j, at, :] for j in range(nz)], axis=1)
-            out[at, :] = mm(lhs, w_ref[i]).astype(BF16)
+            outs[i][at, :] = mm(lhs, w_ref[i]).astype(BF16)
 
 
 def chip_kernel(here_ref, *refs):
@@ -528,13 +526,11 @@
 
     rows_x = feats // nx
     half_rows = rows_x // 2
-
-    def rows_for(by, start, size):
-        first = ((x + by) % nx) * rows_x + core * half_rows + start
-        return lax.dynamic_slice(out_weight, (first, 0), (size, channels))
+    weights = lax.all_to_all(
+        out_weight.reshape(nx, rows_x, channels), "x", split_axis=0, concat_axis=0
+    )
 
     hop1 = both_ways("z", (out_grad, out_grad))
-    near = both_ways("x", (rows_for(1, 0, half_rows), rows_for(-1, 0, half_rows)))
 
     conv_own, ends, xt, states = call(
         forward_kernel,
@@ -553,9 +549,12 @@
         12,
         10.0,
     )
-    hop2 = both_ways("z", after(hop1, near, ends))
-    half_a = both_ways("x", (rows_for(2, 0, half_rows // 2), rows_for(2, half_rows // 2, half_rows // 2)))
-    all_ends = gather_ctx(ends)
+    other_ends = lax.ppermute(ends, "core", swap)
+    pair = jnp.stack([ends, other_ends])
+    hop2 = both_ways("z", after(hop1, ends))
+    all_ends = [ends, other_ends] + [
+        lax.ppermute(pair, "y", shift(ny, i)) for i in range(1, ny)
+    ]
     conv, gated, entering = call(
         enter_kernel,
         [
@@ -564,18 +563,14 @@
             sds((2 * poles, channels), F32),
         ],
         [],
-        [here, all_ends, conv_own, query, rate, residue],
+        [here] + all_ends + [after(conv_own, hop2), query, rate, residue],
         8,
         10.0,
         scalars=1,
     )
-    hop3 = both_ways("z", after(hop2, gated, half_a))
-    half_b = both_ways("x", half_a)
-    sent = after(gated, half_b)
-    gates = [gated] + [lax.ppermute(sent, "x", shift(nx, i)) for i in range(1, nx)]
-    fetched = [near[0], *half_b, near[1]]
-    others = [lax.ppermute(piece, "core", swap) for piece in fetched]
-    right, left = after(hop3, others)
+    hop3 = both_ways("z", after(hop2, all_ends))
+    gates = [gated] + [lax.ppermute(gated, "x", shift(nx, i)) for i in range(1, nx)]
+    right, left = after(hop3, gated)
     hop4 = both_ways("z", (right[: tokens // 2], left[tokens // 2 :]))
     blocks = [out_grad, *hop1, *hop2, *hop3, *hop4]
 
@@ -586,13 +581,13 @@
             pltpu.VMEM((nz, tokens, channels), BF16),
             pltpu.VMEM((nx, rows_x, channels), BF16),
             pltpu.SemaphoreType.DMA((nz, 2)),
-            pltpu.SemaphoreType.DMA((2 * nx + 1,)),
-        ],
-        [here] + blocks + [out_weight] + fetched + others,
+            pltpu.SemaphoreType.DMA((nx,)),
+        ],
+        [here] + blocks + [weights],
         16,
         6.0,
         scalars=1,
-        far=tuple(range(1, 19)),
+        far=tuple(range(1, 11)),
     )
     sums = [
         lax.ppermute(part, "x", shift(nx, -i)) for i, part in ((2, two), (1, one), (3, three))

time: 160 us -> 148 us (0.925)
  starting transfers between devices: 48.4 us -> 38.3 us
  local copies, waits for them, and re-layouts: 16.7 us -> 7.76 us
  waiting for transfers between devices: 43.1 us -> 46.7 us
  Pallas kernels: 27.1 us -> 30.2 us
    ppermute x7, waiting for transfers between devices: 1.39 us -> 11.9 us  [the longest x3 5.56 us: local(): lax.ppermute(gated, 'x', shift(nx, i))]
    ppermute x7 -> x4, starting transfers between devices: 22.2 us -> 14.5 us  [both_ways(): lax.ppermute(pair[1], axis, shift(n, -1))]
    all_to_all x1, waiting for transfers between devices: 6.43 us -> 0.01 us  [local(): lax.all_to_all(out_weight.reshape(nx, rows_x, channels), 'x', split_axis=...]
    ppermute x7 -> x4, waiting for transfers between devices: 3.46 us -> 8.7 us  [both_ways(): lax.ppermute(pair[1], axis, shift(n, -1))]
    unnamed x42 -> x40, local copies, waits for them, and re-layouts: 12.6 us -> 7.7 us
    ppermute x7 -> x4, waiting for transfers between devices: 13.2 us -> 8.34 us  [both_ways(): lax.ppermute(pair[0], axis, shift(n, 1))]
    ppermute x3, waiting for transfers between devices: 16 us -> 12.1 us  [local(): lax.ppermute(part, 'x', shift(nx, -i))]
    dynamic_slice x2 -> x0, local copies, waits for them, and re-layouts: 3.3 us -> none  [rows_for(): return lax.dynamic_slice(out_weight, (first, 0), (size, channels))]
  transfers between devices with their start and end apart: 30 -> 24, of which waited for: 13 -> 15; matrix products, arithmetic and copies ran while one was open for 3% -> 0% of each run, Pallas kernels for 14% -> 16%
where the time goes in v1:
time: 148 us; the launch traced here: 147 us
  waiting for transfers between devices  46.7 us (32%)
  starting transfers between devices  38.3 us (26%)
  Pallas kernels  30.2 us (20%)
  blocking collectives  23 us (16%)
  local copies, waits for them, and re-layouts  7.76 us (5%)
    pallas_call x9, Pallas kernels, call(): pl.pallas_call(kernel, out_shape=outs, in_specs=[pl.BlockSpec(memory_spac...  30.2 us
    all_to_all x1, blocking collectives, gather_ctx(): lax.all_to_all(jnp.broadcast_to(item[None], (n,) + item.shape), CTX, spli...  23 us
    ppermute x4, starting transfers between devices, both_ways(): lax.ppermute(pair[1], axis, shift(n, -1))  14.5 us
    ppermute x3, waiting for transfers between devices, local(): lax.ppermute(part, 'x', shift(nx, -i))  12.1 us
    ppermute x4, waiting for transfers between devices, both_ways(): lax.ppermute(pair[1], axis, shift(n, -1))  8.7 us
    ppermute x4, waiting for transfers between devices, both_ways(): lax.ppermute(pair[0], axis, shift(n, 1))  8.34 us
    unnamed x40, local copies, waits for them, and re-layouts  7.7 us
    ppermute x3, starting transfers between devices, local(): lax.ppermute(chip[r], 'y', shift(ny, r))  5.82 us
  transfers between devices with their start and end apart: 24, of which 15 were waited for; matrix products, arithmetic and copies ran while one was open for 0% of the time, Pallas kernels for 16%

profile of v1, /device:TPU:1, one launch (start us, length us, event | category | flops | bytes accessed | tf_op | source)
XLA Modules:
  0.0 146.9 jit_solution(16405431360860449443)
XLA Ops:
  0.7 5.0 %all-to-all-start = ((bf16[4,2048,256]{2,1,0:T(8,128)(2,1)}), bf16[4,2048,256]{2,1,0:T(8,128)(2,1)}, u32[]{:S(2)}, u32[]{:S(2)}) async-start(bf16[4,2048,256]{2,1,0:T(8,128)(2,1)} %bitcast.9), calls=%async_computation | async-start | bytes 8388608 | tf_op jit(solution)/shard_map/all_to_all | solution.py:529
  5.7 6.5 %collective-permute-start.1 = (bf16[1024,256]{1,0:T(8,128)(2,1)S(1)}, bf16[1024,256]{1,0:T(8,128)(2,1)S(1)}, u32[]{:S(2)}, u32[]{:S(2)}) collective-permute-start(bf16[1024,256]{1,0:T(8,128)(2,1)S(1)} %copy-done), channel_id=1, source_target_pairs={{0,7},{1,0},{2,1},{3,2},{4,3},{5,4},{6,5},{7,6},{8,15},{9,8},{10,9... | collective-permute-start | bytes 1572872 | tf_op jit(solution)/shard_map/ppermute | solution.py:524
  12.2 2.7 %shard_map.118 = (f32[1024,256]{1,0:T(8,128)S(1)}, f32[32,256]{1,0:T(8,128)S(1)}, bf16[256,1024]{1,0:T(8,128)(2,1)S(1)}, f32[16,128,128]{2,1,0:T(8,128)S(1)}) custom-call(bf16[1024,256]{1,0:T(8,128)(2,1)S(1)} %copy-done.6, bf16[1024,256]{1,0:T(8,128)(2,1)S(1)} %copy-done.8, f32[16,16]{1,0:T(8,128)S(1)} %copy-done.18, f32[16,16]{1,0:T(8,128)S(1)} %copy-done.19), custom_call_target="tpu_custom_call" | custom-call | flops 1000 | bytes 36900000 | tf_op jit(solution)/shard_map/pallas_call | solution.py:471
  14.9 1.0 copy-done.10
  15.9 1.0 copy-done.14
  16.9 0.8 copy-done.16
  17.7 5.1 %collective-permute-done.1.refs_2_ = bf16[1024,256]{1,0:T(8,128)(2,1)S(1)} collective-permute-done((bf16[1024,256]{1,0:T(8,128)(2,1)S(1)}, bf16[1024,256]{1,0:T(8,128)(2,1)S(1)}, u32[]{:S(2)}, u32[]{:S(2)}) %collective-permute-start.1) | collective-permute-done | bytes 524320 | tf_op jit(solution)/shard_map/ppermute | solution.py:524
  22.8 3.2 %collective-permute-done.refs_1_ = bf16[1024,256]{1,0:T(8,128)(2,1)S(1)} collective-permute-done((bf16[1024,256]{1,0:T(8,128)(2,1)S(1)}, bf16[1024,256]{1,0:T(8,128)(2,1)S(1)}, u32[]{:S(2)}, u32[]{:S(2)}) %collective-permute-start) | collective-permute-done | bytes 524320 | tf_op jit(solution)/shard_map/ppermute | solution.py:523
  26.0 2.7 %collective-permute-start.3 = (bf16[1024,256]{1,0:T(8,128)(2,1)S(1)}, bf16[1024,256]{1,0:T(8,128)(2,1)}, u32[]{:S(2)}, u32[]{:S(2)}) collective-permute-start(bf16[1024,256]{1,0:T(8,128)(2,1)S(1)} %collective-permute-done.1.refs_2_), channel_id=1, source_target_pairs={{0,7},{1,0},{2,1},{3,2},{4,3},{5,4},{6,5},{7,6},{8,15},{9,8},{10,9... | collective-permute-start | bytes 1572872 | tf_op jit(solution)/shard_map/ppermute | solution.py:524
  28.7 2.3 %collective-permute-start.4 = (f32[32,256]{1,0:T(8,128)S(1)}, f32[32,256]{1,0:T(8,128)S(1)}, u32[]{:S(2)}, u32[]{:S(2)}) collective-permute-start(f32[32,256]{1,0:T(8,128)S(1)} %get-tuple-element.47.own_ref), channel_id=1, source_target_pairs={{0,32},{32,0},{1,33},{33,1},{2,34},{34,2},{3,35},{35,3},{4,36},{36... | collective-permute-start | bytes 98312 | tf_op jit(solution)/shard_map/ppermute | solution.py:552
  31.0 0.9 collective-permute-done.4.other_ref
  31.8 2.7 %collective-permute-start.7 = (f32[2,32,256]{2,1,0:T(8,128)S(1)}, f32[2,32,256]{2,1,0:T(8,128)S(1)}, u32[]{:S(2)}, u32[]{:S(2)}) collective-permute-start(f32[2,32,256]{2,1,0:T(8,128)S(1)} %pad_maximum_fusion), channel_id=1, source_target_pairs={{0,192},{64,0},{128,64},{192,128},{1,193},{65,1},{129,65},{193,129... | collective-permute-start | bytes 196616 | tf_op jit(solution)/shard_map/ppermute | solution.py:556
  34.9 0.7 collective-permute-start.5
  35.9 3.7 %collective-permute-done.6.p2_ref = f32[2,32,256]{2,1,0:T(8,128)S(1)} collective-permute-done((f32[2,32,256]{2,1,0:T(8,128)S(1)}, f32[2,32,256]{2,1,0:T(8,128)S(1)}, u32[]{:S(2)}, u32[]{:S(2)}) %collective-permute-start.6) | collective-permute-done | bytes 65568 | tf_op jit(solution)/shard_map/ppermute | solution.py:556
  39.6 1.5 %collective-permute-done.5.p1_ref = f32[2,32,256]{2,1,0:T(8,128)S(1)} collective-permute-done((f32[2,32,256]{2,1,0:T(8,128)S(1)}, f32[2,32,256]{2,1,0:T(8,128)S(1)}, u32[]{:S(2)}, u32[]{:S(2)}) %collective-permute-start.5) | collective-permute-done | bytes 65568 | tf_op jit(solution)/shard_map/ppermute | solution.py:556
  41.1 2.7 %collective-permute-start.9 = (bf16[1024,256]{1,0:T(8,128)(2,1)}, bf16[1024,256]{1,0:T(8,128)(2,1)S(1)}, u32[]{:S(2)}, u32[]{:S(2)}) collective-permute-start(bf16[1024,256]{1,0:T(8,128)(2,1)} %collective-permute-done.3.refs_4_), channel_id=1, source_target_pairs={{0,7},{1,0},{2,1},{3,2},{4,3},{5,4},{6,5},{7,6},{8,15},{9,8},{10,9... | collective-permute-start | bytes 1572872 | tf_op jit(solution)/shard_map/ppermute | solution.py:524
  43.9 1.0 copy-done.4
  44.9 1.2 copy-done.15
  46.1 2.3 %shard_map.119 = (f32[1024,256]{1,0:T(8,128)S(1)}, bf16[256,1024]{1,0:T(8,128)(2,1)}, f32[32,256]{1,0:T(8,128)S(1)}) custom-call(s32[4]{0:T(128)S(1)} %pad_add_fusion.here_ref, f32[32,256]{1,0:T(8,128)S(1)} %get-tuple-element.47.own_ref, f32[32,256]{1,0:T(8,128)S(1)} %collective-permute-done.4.other_ref, f32[2,32,256]{2,1,0:T(8,128)S(1)} %collective-permute-done.5.p1_ref, ...), custom_call_target="tpu_custom_call" | custom-call | flops 1000 | bytes 36900000 | tf_op jit(solution)/shard_map/pallas_call | solution.py:471
  48.5 1.0 copy-done.12
  49.4 2.5 %collective-permute-start.14 = (bf16[256,1024]{1,0:T(8,128)(2,1)}, bf16[256,1024]{1,0:T(8,128)(2,1)}, u32[]{:S(2)}, u32[]{:S(2)}) collective-permute-start(bf16[256,1024]{1,0:T(8,128)(2,1)} %get-tuple-element.54.refs_9_.refs_10_), channel_id=1, source_target_pairs={{0,24},{8,0},{16,8},{24,16},{1,25},{9,1},{17,9},{25,17},{2,26},{10... | collective-permute-start | bytes 1572872 | tf_op jit(solution)/shard_map/ppermute | solution.py:572
  52.5 0.6 collective-permute-start.12
  53.0 1.9 %collective-permute-done.8.refs_5_ = bf16[1024,256]{1,0:T(8,128)(2,1)S(1)} collective-permute-done((bf16[1024,256]{1,0:T(8,128)(2,1)S(1)}, bf16[1024,256]{1,0:T(8,128)(2,1)S(1)}, u32[]{:S(2)}, u32[]{:S(2)}) %collective-permute-start.8) | collective-permute-done | bytes 524320 | tf_op jit(solution)/shard_map/ppermute | solution.py:523
  55.0 2.7 %collective-permute-start.11 = (bf16[512,256]{1,0:T(8,128)(2,1)S(1)}, bf16[512,256]{1,0:T(8,128)(2,1)S(1)}, u32[]{:S(2)}, u32[]{:S(2)}) collective-permute-start(bf16[512,256]{1,0:T(8,128)(2,1)S(1)} %slice.7), channel_id=1, source_target_pairs={{0,7},{1,0},{2,1},{3,2},{4,3},{5,4},{6,5},{7,6},{8,15},{9,8},{10,9... | collective-permute-start | bytes 786440 | tf_op jit(solution)/shard_map/ppermute | solution.py:524
  57.7 3.6 %collective-permute-done.11.refs_8_ = bf16[512,256]{1,0:T(8,128)(2,1)S(1)} collective-permute-done((bf16[512,256]{1,0:T(8,128)(2,1)S(1)}, bf16[512,256]{1,0:T(8,128)(2,1)S(1)}, u32[]{:S(2)}, u32[]{:S(2)}) %collective-permute-start.11) | collective-permute-done | bytes 262176 | tf_op jit(solution)/shard_map/ppermute | solution.py:524
  61.3 3.2 %collective-permute-done.10.refs_7_ = bf16[512,256]{1,0:T(8,128)(2,1)S(1)} collective-permute-done((bf16[512,256]{1,0:T(8,128)(2,1)S(1)}, bf16[512,256]{1,0:T(8,128)(2,1)S(1)}, u32[]{:S(2)}, u32[]{:S(2)}) %collective-permute-start.10) | collective-permute-done | bytes 262176 | tf_op jit(solution)/shard_map/ppermute | solution.py:523
  64.5 0.7 copy-done.1
  65.2 0.9 copy-done.2
  66.2 7.1 %shard_map.120 = (bf16[1024,256]{1,0:T(8,128)(2,1)S(1)}, bf16[1024,256]{1,0:T(8,128)(2,1)S(1)}, bf16[1024,256]{1,0:T(8,128)(2,1)S(1)}, bf16[1024,256]{1,0:T(8,128)(2,1)S(1)}) custom-call(s32[4]{0:T(128)S(1)} %pad_add_fusion.here_ref, bf16[1024,256]{1,0:T(8,128)(2,1)S(1)} %copy-done, bf16[1024,256]{1,0:T(8,128)(2,1)S(1)} %collective-permute-done.refs_1_, ...), custom_call_target="tpu_custom_call" | custom-call | flops 1000 | bytes 22140000 | tf_op jit(solution)/shard_map/pallas_call | solution.py:471
  73.3 5.6 %collective-permute-done.12.refs_10_.refs_11_ = bf16[256,1024]{1,0:T(8,128)(2,1)} collective-permute-done((bf16[256,1024]{1,0:T(8,128)(2,1)}, bf16[256,1024]{1,0:T(8,128)(2,1)}, u32[]{:S(2)}, u32[]{:S(2)}) %collective-permute-start.12) | collective-permute-done | bytes 524320 | tf_op jit(solution)/shard_map/ppermute | solution.py:572
  78.9 4.6 %shard_map.121 = bf16[4,256,1024]{2,1,0:T(8,128)(2,1)S(1)} custom-call(s32[4]{0:T(128)S(1)} %pad_add_fusion.here_ref, bf16[1024,256]{1,0:T(8,128)(2,1)S(1)} %copy-done, bf16[1024,256]{1,0:T(8,128)(2,1)S(1)} %collective-permute-done.refs_1_, bf16[1024,256]{1,0:T(8,128)(2,1)S(1)} %collective-permute-done.1.refs_2_, ...), custom_call_target="tpu_custom_call" | custom-call | flops 1000 | bytes 1845000 | tf_op jit(solution)/shard_map/pallas_call | solution.py:471
  83.5 0.6 collective-permute-start.15
  84.1 0.5 collective-permute-start.16
  84.6 1.5 collective-permute-start.17
  86.2 1.7 %collective-permute-done.15.refs_9_ = bf16[4,256,1024]{2,1,0:T(8,128)(2,1)S(1)} collective-permute-done((bf16[4,256,1024]{2,1,0:T(8,128)(2,1)S(1)}, bf16[4,256,1024]{2,1,0:T(8,128)(2,1)S(1)}, u32[]{:S(2)}, u32[]{:S(2)}) %collective-permute-start.15) | collective-permute-done | bytes 2097184 | tf_op jit(solution)/shard_map/ppermute | solution.py:606
  87.9 4.9 %shard_map.122 = (bf16[256,1024]{1,0:T(8,128)(2,1)S(1)}, bf16[256,1024]{1,0:T(8,128)(2,1)S(1)}, bf16[256,1024]{1,0:T(8,128)(2,1)S(1)}, bf16[256,1024]{1,0:T(8,128)(2,1)S(1)}) custom-call(s32[4]{0:T(128)S(1)} %pad_add_fusion.here_ref, bf16[1024,256]{1,0:T(8,128)(2,1)S(1)} %copy-done, bf16[1024,256]{1,0:T(8,128)(2,1)S(1)} %collective-permute-done.refs_1_, ...), custom_call_target="tpu_custom_call" | custom-call | flops 1000 | bytes 1845000 | tf_op jit(solution)/shard_map/pallas_call | solution.py:471
  92.8 1.0 collective-permute-start.19
  93.8 2.6 %collective-permute-start.20 = (bf16[256,1024]{1,0:T(8,128)(2,1)S(1)}, bf16[256,1024]{1,0:T(8,128)(2,1)S(1)}, u32[]{:S(2)}, u32[]{:S(2)}) collective-permute-start(bf16[256,1024]{1,0:T(8,128)(2,1)S(1)} %get-tuple-element.69), channel_id=1, source_target_pairs={{0,128},{64,192},{128,0},{192,64},{1,129},{65,193},{129,1},{193,65... | collective-permute-start | bytes 1572872 | tf_op jit(solution)/shard_map/ppermute | solution.py:618
  96.5 2.7 %collective-permute-done.16.p1_ref = bf16[1024,256]{1,0:T(8,128)(2,1)S(1)} collective-permute-done((bf16[1024,256]{1,0:T(8,128)(2,1)S(1)}, bf16[1024,256]{1,0:T(8,128)(2,1)S(1)}, u32[]{:S(2)}, u32[]{:S(2)}) %collective-permute-start.16) | collective-permute-done | bytes 524320 | tf_op jit(solution)/shard_map/ppermute | solution.py:593
  99.2 2.2 %collective-permute-start.21 = (bf16[256,1024]{1,0:T(8,128)(2,1)S(1)}, bf16[256,1024]{1,0:T(8,128)(2,1)S(1)}, u32[]{:S(2)}, u32[]{:S(2)}) collective-permute-start(bf16[256,1024]{1,0:T(8,128)(2,1)S(1)} %get-tuple-element.70), channel_id=1, source_target_pairs={{0,192},{64,0},{128,64},{192,128},{1,193},{65,1},{129,65},{193,129... | collective-permute-start | bytes 1572872 | tf_op jit(solution)/shard_map/ppermute | solution.py:618
  101.3 7.4 %collective-permute-done.17.p2_ref = bf16[1024,256]{1,0:T(8,128)(2,1)S(1)} collective-permute-done((bf16[1024,256]{1,0:T(8,128)(2,1)S(1)}, bf16[1024,256]{1,0:T(8,128)(2,1)S(1)}, u32[]{:S(2)}, u32[]{:S(2)}) %collective-permute-start.17) | collective-permute-done | bytes 524320 | tf_op jit(solution)/shard_map/ppermute | solution.py:593
  108.8 2.0 %collective-permute-done.18.p3_ref = bf16[1024,256]{1,0:T(8,128)(2,1)S(1)} collective-permute-done((bf16[1024,256]{1,0:T(8,128)(2,1)S(1)}, bf16[1024,256]{1,0:T(8,128)(2,1)S(1)}, u32[]{:S(2)}, u32[]{:S(2)}) %collective-permute-start.18) | collective-permute-done | bytes 524320 | tf_op jit(solution)/shard_map/ppermute | solution.py:593
  110.8 4.6 %shard_map.123 = (bf16[1024,256]{1,0:T(8,128)(2,1)}, f32[1024,256]{1,0:T(8,128)S(1)}, f32[48,256]{1,0:T(8,128)S(1)}) custom-call(bf16[1024,256]{1,0:T(8,128)(2,1)S(1)} %get-tuple-element.71.own_ref, bf16[1024,256]{1,0:T(8,128)(2,1)S(1)} %collective-permute-done.16.p1_ref, bf16[1024,256]{1,0:T(8,128)(2,1)S(1)} %collective-permute-done.17.p2_ref, ...), custom_call_target="tpu_custom_call" | custom-call | flops 1000 | bytes 73800000 | tf_op jit(solution)/shard_map/pallas_call | solution.py:471
  115.4 3.8 %collective-permute-done.20.c_ref = bf16[256,1024]{1,0:T(8,128)(2,1)S(1)} collective-permute-done((bf16[256,1024]{1,0:T(8,128)(2,1)S(1)}, bf16[256,1024]{1,0:T(8,128)(2,1)S(1)}, u32[]{:S(2)}, u32[]{:S(2)}) %collective-permute-start.20) | collective-permute-done | bytes 524320 | tf_op jit(solution)/shard_map/ppermute | solution.py:618
  119.5 0.7 collective-permute-start.22
  120.2 23.0 %all_to_all.10.all_ref = f32[8,48,256]{2,1,0:T(8,128)S(1)} all-to-all(f32[8,48,256]{2,1,0:T(8,128)S(1)} %broadcast_in_dim.2), channel_id=1, replica_groups=mesh['y'=4,'core'=2,'x'=4,'z'=8] {'y','core'}, dimensions={0} | all-to-all | bytes 786432 | tf_op jit(solution)/shard_map/all_to_all | solution.py:495
  143.2 2.5 %shard_map.125 = (bf16[1024,256]{1,0:T(8,128)(2,1)}, bf16[1024,256]{1,0:T(8,128)(2,1)}, f32[16,16]{1,0:T(8,128)}, f32[16,16]{1,0:T(8,128)}) custom-call(s32[4]{0:T(128)S(1)} %pad_add_fusion.here_ref, f32[8,48,256]{2,1,0:T(8,128)S(1)} %all_to_all.10.all_ref, f32[1024,256]{1,0:T(8,128)S(1)} %get-tuple-element.83.back_ref, bf16[1024,256]{1,0:T(8,128)(2,1)S(1)} %copy-done.7, ...), custom_call_target="tpu_custom_call" | custom-call | flops 1000 | bytes 9225000 | tf_op jit(solution)/shard_map/pallas_call | solution.py:471
  145.7 1.2 shard_map.126
  (55 shorter events, 1.7 us)
Async XLA Ops:
  0.6 5.1 %copy-start = (bf16[1024,256]{1,0:T(8,128)(2,1)S(1)}, bf16[1024,256]{1,0:T(8,128)(2,1)}, u32[]{:S(2)}) copy-start(bf16[1024,256]{1,0:T(8,128)(2,1)} %refs_0_.4) | copy-start | bytes 1572868
  0.6 11.6 %copy-start.6 = (bf16[1024,256]{1,0:T(8,128)(2,1)S(1)}, bf16[1024,256]{1,0:T(8,128)(2,1)}, u32[]{:S(2)}) copy-start(bf16[1024,256]{1,0:T(8,128)(2,1)} %key_ref.3) | copy-start | bytes 1572868
  0.7 11.5 %copy-start.8 = (bf16[1024,256]{1,0:T(8,128)(2,1)S(1)}, bf16[1024,256]{1,0:T(8,128)(2,1)}, u32[]{:S(2)}) copy-start(bf16[1024,256]{1,0:T(8,128)(2,1)} %value_ref.3) | copy-start | bytes 1572868
  0.7 11.5 %copy-start.18 = (f32[16,16]{1,0:T(8,128)S(1)}, f32[16,16]{1,0:T(8,128)}, u32[]{:S(2)}) copy-start(f32[16,16]{1,0:T(8,128)} %rate_ref.7) | copy-start | bytes 3076
  0.7 11.5 %copy-start.19 = (f32[16,16]{1,0:T(8,128)S(1)}, f32[16,16]{1,0:T(8,128)}, u32[]{:S(2)}) copy-start(f32[16,16]{1,0:T(8,128)} %res_ref.7) | copy-start | bytes 3076
  0.7 64.5 %all-to-all-start = ((bf16[4,2048,256]{2,1,0:T(8,128)(2,1)}), bf16[4,2048,256]{2,1,0:T(8,128)(2,1)}, u32[]{:S(2)}, u32[]{:S(2)}) async-start(bf16[4,2048,256]{2,1,0:T(8,128)(2,1)} %bitcast.9), calls=%async_computation | async-start | bytes 8388608 | tf_op jit(solution)/shard_map/all_to_all | solution.py:529
  5.7 17.1 %collective-permute-start.1 = (bf16[1024,256]{1,0:T(8,128)(2,1)S(1)}, bf16[1024,256]{1,0:T(8,128)(2,1)S(1)}, u32[]{:S(2)}, u32[]{:S(2)}) collective-permute-start(bf16[1024,256]{1,0:T(8,128)(2,1)S(1)} %copy-done), channel_id=1, source_target_pairs={{0,7},{1,0},{2,1},{3,2},{4,3},{5,4},{6,5},{7,6},{8,15},{9,8},{10,9... | collective-permute-start | bytes 1572872 | tf_op jit(solution)/shard_map/ppermute | solution.py:524
  12.2 13.8 %collective-permute-start = (bf16[1024,256]{1,0:T(8,128)(2,1)S(1)}, bf16[1024,256]{1,0:T(8,128)(2,1)S(1)}, u32[]{:S(2)}, u32[]{:S(2)}) collective-permute-start(bf16[1024,256]{1,0:T(8,128)(2,1)S(1)} %copy-done), channel_id=1, source_target_pairs={{0,1},{1,2},{2,3},{3,4},{4,5},{5,6},{6,7},{7,0},{8,9},{9,10},{10,1... | collective-permute-start | bytes 1572872 | tf_op jit(solution)/shard_map/ppermute | solution.py:523
  14.9 1.0 copy-start.10
  15.9 1.0 copy-start.14
  16.9 0.8 copy-start.16
  26.0 15.1 %collective-permute-start.2 = (bf16[1024,256]{1,0:T(8,128)(2,1)S(1)}, bf16[1024,256]{1,0:T(8,128)(2,1)S(1)}, u32[]{:S(2)}, u32[]{:S(2)}) collective-permute-start(bf16[1024,256]{1,0:T(8,128)(2,1)S(1)} %collective-permute-done.refs_1_), channel_id=1, source_target_pairs={{0,1},{1,2},{2,3},{3,4},{4,5},{5,6},{6,7},{7,0},{8,9},{9,10},{10,1... | collective-permute-start | bytes 1572872 | tf_op jit(solution)/shard_map/ppermute | solution.py:523
  26.0 15.1 %collective-permute-start.3 = (bf16[1024,256]{1,0:T(8,128)(2,1)S(1)}, bf16[1024,256]{1,0:T(8,128)(2,1)}, u32[]{:S(2)}, u32[]{:S(2)}) collective-permute-start(bf16[1024,256]{1,0:T(8,128)(2,1)S(1)} %collective-permute-done.1.refs_2_), channel_id=1, source_target_pairs={{0,7},{1,0},{2,1},{3,2},{4,3},{5,4},{6,5},{7,6},{8,15},{9,8},{10,9... | collective-permute-start | bytes 1572872 | tf_op jit(solution)/shard_map/ppermute | solution.py:524
  28.7 3.2 %collective-permute-start.4 = (f32[32,256]{1,0:T(8,128)S(1)}, f32[32,256]{1,0:T(8,128)S(1)}, u32[]{:S(2)}, u32[]{:S(2)}) collective-permute-start(f32[32,256]{1,0:T(8,128)S(1)} %get-tuple-element.47.own_ref), channel_id=1, source_target_pairs={{0,32},{32,0},{1,33},{33,1},{2,34},{34,2},{3,35},{35,3},{4,36},{36... | collective-permute-start | bytes 98312 | tf_op jit(solution)/shard_map/ppermute | solution.py:552
  31.8 4.1 %collective-permute-start.7 = (f32[2,32,256]{2,1,0:T(8,128)S(1)}, f32[2,32,256]{2,1,0:T(8,128)S(1)}, u32[]{:S(2)}, u32[]{:S(2)}) collective-permute-start(f32[2,32,256]{2,1,0:T(8,128)S(1)} %pad_maximum_fusion), channel_id=1, source_target_pairs={{0,192},{64,0},{128,64},{192,128},{1,193},{65,1},{129,65},{193,129... | collective-permute-start | bytes 196616 | tf_op jit(solution)/shard_map/ppermute | solution.py:556
  34.6 5.0 %collective-permute-start.6 = (f32[2,32,256]{2,1,0:T(8,128)S(1)}, f32[2,32,256]{2,1,0:T(8,128)S(1)}, u32[]{:S(2)}, u32[]{:S(2)}) collective-permute-start(f32[2,32,256]{2,1,0:T(8,128)S(1)} %pad_maximum_fusion), channel_id=1, source_target_pairs={{0,128},{64,192},{128,0},{192,64},{1,129},{65,193},{129,1},{193,65... | collective-permute-start | bytes 196616 | tf_op jit(solution)/shard_map/ppermute | solution.py:556
  34.9 6.2 %collective-permute-start.5 = (f32[2,32,256]{2,1,0:T(8,128)S(1)}, f32[2,32,256]{2,1,0:T(8,128)S(1)}, u32[]{:S(2)}, u32[]{:S(2)}) collective-permute-start(f32[2,32,256]{2,1,0:T(8,128)S(1)} %pad_maximum_fusion), channel_id=1, source_target_pairs={{0,64},{64,128},{128,192},{192,0},{1,65},{65,129},{129,193},{193,1... | collective-permute-start | bytes 196616 | tf_op jit(solution)/shard_map/ppermute | solution.py:556
  41.1 13.9 %collective-permute-start.8 = (bf16[1024,256]{1,0:T(8,128)(2,1)S(1)}, bf16[1024,256]{1,0:T(8,128)(2,1)S(1)}, u32[]{:S(2)}, u32[]{:S(2)}) collective-permute-start(bf16[1024,256]{1,0:T(8,128)(2,1)S(1)} %collective-permute-done.2.refs_3_), channel_id=1, source_target_pairs={{0,1},{1,2},{2,3},{3,4},{4,5},{5,6},{6,7},{7,0},{8,9},{9,10},{10,1... | collective-permute-start | bytes 1572872 | tf_op jit(solution)/shard_map/ppermute | solution.py:523
  41.1 13.8 %collective-permute-start.9 = (bf16[1024,256]{1,0:T(8,128)(2,1)}, bf16[1024,256]{1,0:T(8,128)(2,1)S(1)}, u32[]{:S(2)}, u32[]{:S(2)}) collective-permute-start(bf16[1024,256]{1,0:T(8,128)(2,1)} %collective-permute-done.3.refs_4_), channel_id=1, source_target_pairs={{0,7},{1,0},{2,1},{3,2},{4,3},{5,4},{6,5},{7,6},{8,15},{9,8},{10,9... | collective-permute-start | bytes 1572872 | tf_op jit(solution)/shard_map/ppermute | solution.py:524
  43.9 1.0 copy-start.4
  44.9 1.2 copy-start.15
  48.5 1.0 copy-start.12
  49.4 23.9 %collective-permute-start.14 = (bf16[256,1024]{1,0:T(8,128)(2,1)}, bf16[256,1024]{1,0:T(8,128)(2,1)}, u32[]{:S(2)}, u32[]{:S(2)}) collective-permute-start(bf16[256,1024]{1,0:T(8,128)(2,1)} %get-tuple-element.54.refs_9_.refs_10_), channel_id=1, source_target_pairs={{0,24},{8,0},{16,8},{24,16},{1,25},{9,1},{17,9},{25,17},{2,26},{10... | collective-permute-start | bytes 1572872 | tf_op jit(solution)/shard_map/ppermute | solution.py:572
  52.0 21.3 %collective-permute-start.13 = (bf16[256,1024]{1,0:T(8,128)(2,1)}, bf16[256,1024]{1,0:T(8,128)(2,1)}, u32[]{:S(2)}, u32[]{:S(2)}) collective-permute-start(bf16[256,1024]{1,0:T(8,128)(2,1)} %get-tuple-element.54.refs_9_.refs_10_), channel_id=1, source_target_pairs={{0,16},{8,24},{16,0},{24,8},{1,17},{9,25},{17,1},{25,9},{2,18},{10... | collective-permute-start | bytes 1572872 | tf_op jit(solution)/shard_map/ppermute | solution.py:572
  52.5 26.4 %collective-permute-start.12 = (bf16[256,1024]{1,0:T(8,128)(2,1)}, bf16[256,1024]{1,0:T(8,128)(2,1)}, u32[]{:S(2)}, u32[]{:S(2)}) collective-permute-start(bf16[256,1024]{1,0:T(8,128)(2,1)} %get-tuple-element.54.refs_9_.refs_10_), channel_id=1, source_target_pairs={{0,8},{8,16},{16,24},{24,0},{1,9},{9,17},{17,25},{25,1},{2,10},{10... | collective-permute-start | bytes 1572872 | tf_op jit(solution)/shard_map/ppermute | solution.py:572
  55.0 6.3 %collective-permute-start.11 = (bf16[512,256]{1,0:T(8,128)(2,1)S(1)}, bf16[512,256]{1,0:T(8,128)(2,1)S(1)}, u32[]{:S(2)}, u32[]{:S(2)}) collective-permute-start(bf16[512,256]{1,0:T(8,128)(2,1)S(1)} %slice.7), channel_id=1, source_target_pairs={{0,7},{1,0},{2,1},{3,2},{4,3},{5,4},{6,5},{7,6},{8,15},{9,8},{10,9... | collective-permute-start | bytes 786440 | tf_op jit(solution)/shard_map/ppermute | solution.py:524
  57.7 6.8 %collective-permute-start.10 = (bf16[512,256]{1,0:T(8,128)(2,1)S(1)}, bf16[512,256]{1,0:T(8,128)(2,1)S(1)}, u32[]{:S(2)}, u32[]{:S(2)}) collective-permute-start(bf16[512,256]{1,0:T(8,128)(2,1)S(1)} %slice.6), channel_id=1, source_target_pairs={{0,1},{1,2},{2,3},{3,4},{4,5},{5,6},{6,7},{7,0},{8,9},{9,10},{10,1... | collective-permute-start | bytes 786440 | tf_op jit(solution)/shard_map/ppermute | solution.py:523
  64.5 0.7 copy-start.1
  65.2 1.0 copy-start.2
  66.2 12.7 %copy-start.3 = (bf16[512,256]{1,0:T(8,128)(2,1)S(1)}, bf16[512,256]{1,0:T(8,128)(2,1)}, u32[]{:S(2)}) copy-start(bf16[512,256]{1,0:T(8,128)(2,1)} %copy-done.1) | copy-start | bytes 786436
  83.5 4.4 %collective-permute-start.15 = (bf16[4,256,1024]{2,1,0:T(8,128)(2,1)S(1)}, bf16[4,256,1024]{2,1,0:T(8,128)(2,1)S(1)}, u32[]{:S(2)}, u32[]{:S(2)}) collective-permute-start(bf16[4,256,1024]{2,1,0:T(8,128)(2,1)S(1)} %shard_map.121), channel_id=1, source_target_pairs={{0,32},{32,0},{1,33},{33,1},{2,34},{34,2},{3,35},{35,3},{4,36},{36... | collective-permute-start | bytes 6291464 | tf_op jit(solution)/shard_map/ppermute | solution.py:606
  84.1 15.0 %collective-permute-start.16 = (bf16[1024,256]{1,0:T(8,128)(2,1)S(1)}, bf16[1024,256]{1,0:T(8,128)(2,1)S(1)}, u32[]{:S(2)}, u32[]{:S(2)}) collective-permute-start(bf16[1024,256]{1,0:T(8,128)(2,1)S(1)} %get-tuple-element.72), channel_id=1, source_target_pairs={{0,16},{8,24},{16,0},{24,8},{1,17},{9,25},{17,1},{25,9},{2,18},{10... | collective-permute-start | bytes 1572872 | tf_op jit(solution)/shard_map/ppermute | solution.py:593
  84.6 24.1 %collective-permute-start.17 = (bf16[1024,256]{1,0:T(8,128)(2,1)S(1)}, bf16[1024,256]{1,0:T(8,128)(2,1)S(1)}, u32[]{:S(2)}, u32[]{:S(2)}) collective-permute-start(bf16[1024,256]{1,0:T(8,128)(2,1)S(1)} %get-tuple-element.73), channel_id=1, source_target_pairs={{0,24},{8,0},{16,8},{24,16},{1,25},{9,1},{17,9},{25,17},{2,26},{10... | collective-permute-start | bytes 1572872 | tf_op jit(solution)/shard_map/ppermute | solution.py:593
  86.1 24.7 %copy-start.5 = (bf16[1024,256]{1,0:T(8,128)(2,1)S(1)}, bf16[1024,256]{1,0:T(8,128)(2,1)}, u32[]{:S(2)}) copy-start(bf16[1024,256]{1,0:T(8,128)(2,1)} %query_ref.3) | copy-start | bytes 1572868
  86.1 24.7 %copy-start.11 = (f32[16,128,128]{2,1,0:T(8,128)S(1)}, f32[16,128,128]{2,1,0:T(8,128)}, u32[]{:S(2)}) copy-start(f32[16,128,128]{2,1,0:T(8,128)} %copy-done.10) | copy-start | bytes 3145732
  86.1 24.7 %copy-start.13 = (f32[1024,256]{1,0:T(8,128)S(1)}, f32[1024,256]{1,0:T(8,128)}, u32[]{:S(2)}) copy-start(f32[1024,256]{1,0:T(8,128)} %copy-done.12) | copy-start | bytes 3145732
  86.1 24.7 %copy-start.17 = (bf16[256,1024]{1,0:T(8,128)(2,1)S(1)}, bf16[256,1024]{1,0:T(8,128)(2,1)}, u32[]{:S(2)}) copy-start(bf16[256,1024]{1,0:T(8,128)(2,1)} %copy-done.16) | copy-start | bytes 1572868
  86.1 24.6 %collective-permute-start.18 = (bf16[1024,256]{1,0:T(8,128)(2,1)S(1)}, bf16[1024,256]{1,0:T(8,128)(2,1)S(1)}, u32[]{:S(2)}, u32[]{:S(2)}) collective-permute-start(bf16[1024,256]{1,0:T(8,128)(2,1)S(1)} %get-tuple-element.74), channel_id=1, source_target_pairs={{0,8},{8,16},{16,24},{24,0},{1,9},{9,17},{17,25},{25,1},{2,10},{10... | collective-permute-start | bytes 1572872 | tf_op jit(solution)/shard_map/ppermute | solution.py:593
  92.8 22.6 %collective-permute-start.19 = (bf16[256,1024]{1,0:T(8,128)(2,1)S(1)}, bf16[256,1024]{1,0:T(8,128)(2,1)S(1)}, u32[]{:S(2)}, u32[]{:S(2)}) collective-permute-start(bf16[256,1024]{1,0:T(8,128)(2,1)S(1)} %get-tuple-element.68), channel_id=1, source_target_pairs={{0,64},{64,128},{128,192},{192,0},{1,65},{65,129},{129,193},{193,1... | collective-permute-start | bytes 1572872 | tf_op jit(solution)/shard_map/ppermute | solution.py:618
  93.8 25.4 %collective-permute-start.20 = (bf16[256,1024]{1,0:T(8,128)(2,1)S(1)}, bf16[256,1024]{1,0:T(8,128)(2,1)S(1)}, u32[]{:S(2)}, u32[]{:S(2)}) collective-permute-start(bf16[256,1024]{1,0:T(8,128)(2,1)S(1)} %get-tuple-element.69), channel_id=1, source_target_pairs={{0,128},{64,192},{128,0},{192,64},{1,129},{65,193},{129,1},{193,65... | collective-permute-start | bytes 1572872 | tf_op jit(solution)/shard_map/ppermute | solution.py:618
  99.2 20.0 %collective-permute-start.21 = (bf16[256,1024]{1,0:T(8,128)(2,1)S(1)}, bf16[256,1024]{1,0:T(8,128)(2,1)S(1)}, u32[]{:S(2)}, u32[]{:S(2)}) collective-permute-start(bf16[256,1024]{1,0:T(8,128)(2,1)S(1)} %get-tuple-element.70), channel_id=1, source_target_pairs={{0,192},{64,0},{128,64},{192,128},{1,193},{65,1},{129,65},{193,129... | collective-permute-start | bytes 1572872 | tf_op jit(solution)/shard_map/ppermute | solution.py:618
  110.8 32.4 %copy-start.7 = (bf16[1024,256]{1,0:T(8,128)(2,1)S(1)}, bf16[1024,256]{1,0:T(8,128)(2,1)}, u32[]{:S(2)}) copy-start(bf16[1024,256]{1,0:T(8,128)(2,1)} %key_ref.3) | copy-start | bytes 1572868
  110.8 32.4 %copy-start.9 = (bf16[1024,256]{1,0:T(8,128)(2,1)S(1)}, bf16[1024,256]{1,0:T(8,128)(2,1)}, u32[]{:S(2)}) copy-start(bf16[1024,256]{1,0:T(8,128)(2,1)} %value_ref.3) | copy-start | bytes 1572868
  119.5 26.2 %collective-permute-start.22 = (bf16[256,1024]{1,0:T(8,128)(2,1)S(1)}, bf16[256,1024]{1,0:T(8,128)(2,1)S(1)}, u32[]{:S(2)}, u32[]{:S(2)}) collective-permute-start(bf16[256,1024]{1,0:T(8,128)(2,1)S(1)} %shard_map.124), channel_id=1, source_target_pairs={{0,0},{8,72},{16,144},{24,216},{64,8},{72,80},{80,152},{88,192},{1... | collective-permute-start | bytes 1572872 | tf_op jit(solution)/shard_map/ppermute | solution.py:642

commit v2 on v1

--- a/solution.py
+++ b/solution.py
@@ -312,13 +312,16 @@
     decay = jnp.exp(-by_channel(rate_ref[...], channels))
     res_cross = cross_ref[0].T[:poles]
     rate_cross = cross_ref[1].T
-    pay_ref[:poles, :] = start
-    pay_ref[poles : 2 * poles, :] = res_cross + decay * start * state_in
-    pay_ref[2 * poles :, :] = (
+    res_sum = res_cross + decay * start * state_in
+    rate_sum = (
         rate_cross[:poles]
         + rate_cross[poles : 2 * poles]
         + decay * ((start_lag + start) * state_in + start * slope_in)
     )
+    both = exact(indicator(groups, channels), jnp.concatenate([res_sum, rate_sum], axis=0), 1, 1)
+    both = jnp.concatenate([both, jnp.zeros((groups, BLK - 2 * poles), F32)], axis=1)
+    pay_ref[:poles, :] = start
+    pay_ref[poles:, :] = jnp.concatenate([both[: groups // 2], both[groups // 2 :]], axis=1)
     for b in range(blocks):
         at = slice(b * BLK, (b + 1) * BLK)
         back_ref[at, :] = bt_ref[:, at].T
@@ -334,7 +337,7 @@
     rate_nc = by_channel(rate_ref[...], channels)
     rate_row, res_row = by_column(rate_ref[...]).T, by_column(res_ref[...]).T
     state = jnp.zeros((poles, channels), F32)
-    total = jnp.zeros((2 * poles, channels), F32)
+    total = jnp.zeros((groups // 2, channels), F32)
     for place in range(count):
         gap = (place - 1 - mine).astype(F32)
         lag = jnp.maximum(gap, 0.0) * float(tokens)
@@ -343,7 +346,7 @@
         total = total + all_ref[place, poles:, :]
     tall = spread(state, groups)
     scale = 1.0 / float(tokens * count)
-    both = exact(indicator(groups, channels), total, 1, 1)
+    both = jnp.concatenate([total[:, : 2 * poles], total[:, BLK : BLK + 2 * poles]], axis=0)
     dres_ref[...] = both[:, :poles] * scale
     drate_ref[...] = -res_ref[...] * both[:, poles:] * scale
     for b in range(tokens // BLK):
@@ -408,10 +411,10 @@
 
 
 def project_kernel(here_ref, *refs):
-    blocks, weights_ref, outs, (f_ref, w_ref, f_sem, w_sem) = refs[:9], refs[9], refs[10:14], refs[14:]
-    z, x = here_ref[2], here_ref[3]
+    blocks, (mine_ref, other_ref), outs, (f_ref, w_ref, f_sem, w_sem) = refs[:9], refs[9:11], refs[11:15], refs[15:]
+    core, z, x = here_ref[1], here_ref[2], here_ref[3]
     nz, tokens, _ = f_ref.shape
-    nx = weights_ref.shape[0]
+    nx, half, _ = mine_ref.shape
     feat = [
         pltpu.make_async_copy(ref, place(at), signal(at))
         for at, ref, place, signal in block_copies(z, blocks, f_ref, f_sem)
@@ -420,14 +423,23 @@
     weight = {}
     for i in order:
         at = lax.rem(x - i + nx, nx)
-        weight[i] = pltpu.make_async_copy(weights_ref.at[at], w_ref.at[i], w_sem.at[i])
-    for copy in [weight[order[0]]] + feat + [weight[i] for i in order[1:]]:
+        weight[i] = [
+            pltpu.make_async_copy(
+                ref.at[at], w_ref.at[i, pl.ds(pl.multiple_of(first, half), half), :], w_sem.at[i, j]
+            )
+            for j, (ref, first) in enumerate(((mine_ref, core * half), (other_ref, (1 - core) * half)))
+        ]
+    for copy in weight[order[0]] + feat:
         copy.start()
+    for i in order[1:]:
+        for copy in weight[i]:
+            copy.start()
     for copy in feat:
         copy.wait()
     tile = TILE
     for i in order:
-        weight[i].wait()
+        for copy in weight[i]:
+            copy.wait()
         for m in range(tokens // tile):
             at = slice(m * tile, (m + 1) * tile)
             lhs = jnp.concatenate([f_ref[j, at, :] for j in range(nz)], axis=1)
@@ -526,9 +538,10 @@
 
     rows_x = feats // nx
     half_rows = rows_x // 2
-    weights = lax.all_to_all(
-        out_weight.reshape(nx, rows_x, channels), "x", split_axis=0, concat_axis=0
-    )
+    w_mine = lax.dynamic_index_in_dim(
+        out_weight.reshape(nx, 2, half_rows, channels), core, 1, keepdims=False
+    )
+    w_mine = lax.all_to_all(w_mine, "x", split_axis=0, concat_axis=0)
 
     hop1 = both_ways("z", (out_grad, out_grad))
 
@@ -569,7 +582,9 @@
         scalars=1,
     )
     hop3 = both_ways("z", after(hop2, all_ends))
-    gates = [gated] + [lax.ppermute(gated, "x", shift(nx, i)) for i in range(1, nx)]
+    w_other = lax.ppermute(after(w_mine, hop2, all_ends), "core", swap)
+    sent = after(gated, w_other)
+    gates = [gated] + [lax.ppermute(sent, "x", shift(nx, i)) for i in range(1, nx)]
     right, left = after(hop3, gated)
     hop4 = both_ways("z", (right[: tokens // 2], left[tokens // 2 :]))
     blocks = [out_grad, *hop1, *hop2, *hop3, *hop4]
@@ -581,13 +596,13 @@
             pltpu.VMEM((nz, tokens, channels), BF16),
             pltpu.VMEM((nx, rows_x, channels), BF16),
             pltpu.SemaphoreType.DMA((nz, 2)),
-            pltpu.SemaphoreType.DMA((nx,)),
-        ],
-        [here] + blocks + [weights],
+            pltpu.SemaphoreType.DMA((nx, 2)),
+        ],
+        [here] + blocks + [w_mine, w_other],
         16,
         6.0,
         scalars=1,
-        far=tuple(range(1, 11)),
+        far=tuple(range(1, 12)),
     )
     sums = [
         lax.ppermute(part, "x", shift(nx, -i)) for i, part in ((2, two), (1, one), (3, three))
@@ -621,7 +636,7 @@
         [
             sds((tokens, channels), BF16),
             sds((tokens, channels), F32),
-            sds((3 * poles, channels), F32),
+            sds((poles + groups // 2, channels), F32),
         ],
         [
             pltpu.VMEM((channels, tokens), BF16),
@@ -637,7 +652,7 @@
     )
     parts[0] = after(parts[0], pay)
     (column,) = call(column_kernel, [sds((channels, half_rows), BF16)], [], parts, 8, 1.0)
-    all_pay = gather_ctx(after(pay, column))
+    all_pay = gather_ctx(pay)
     route = [(a * nx + b, b * nx + (a + b) % nx) for a in range(ny) for b in range(nx)]
     column = lax.ppermute(column, ("y", "x"), route)
 

time: 148 us -> 146 us (0.986)
  local copies, waits for them, and re-layouts: 7.76 us -> 10.9 us
  Pallas kernels: 30.2 us -> 27.4 us
  blocking collectives: 23 us -> 20.7 us
  waiting for transfers between devices: 46.7 us -> 48.8 us
  starting transfers between devices: 38.3 us -> 36.5 us
    ppermute x3, waiting for transfers between devices: 12.1 us -> 15.9 us  [local(): lax.ppermute(part, 'x', shift(nx, -i))]
    squeeze x0 -> x1, local copies, waits for them, and re-layouts: none -> 3.07 us  [local(): lax.dynamic_index_in_dim(out_weight.reshape(nx, 2, half_rows, channels),...]
    ppermute x3, starting transfers between devices: 5.82 us -> 2.87 us  [local(): lax.ppermute(chip[r], 'y', shift(ny, r))]
    pallas_call x9, Pallas kernels: 30.2 us -> 27.4 us  [call(): pl.pallas_call(kernel, out_shape=outs, in_specs=[pl.BlockSpec(memory_spac...]
    all_to_all x1, blocking collectives: 23 us -> 20.7 us  [gather_ctx(): lax.all_to_all(jnp.broadcast_to(item[None], (n,) + item.shape), CTX, spli...]
    ppermute x4, waiting for transfers between devices: 8.34 us -> 10.3 us  [both_ways(): lax.ppermute(pair[0], axis, shift(n, 1))]
    ppermute x3 -> x4, waiting for transfers between devices: 5.56 us -> 3.87 us  [the longest x3 3.87 us: local(): lax.ppermute(sent, 'x', shift(nx, i))]
    ppermute x3 -> x4, starting transfers between devices: 3.59 us -> 5 us  [the longest x3 3.91 us: local(): lax.ppermute(sent, 'x', shift(nx, i))]
  transfers between devices with their start and end apart: 24 -> 25, of which waited for: 15 -> 16; matrix products, arithmetic and copies ran while one was open for 0% -> 0% of each run, Pallas kernels for 16% -> 15%
where the time goes in v2:
time: 146 us; the launch traced here: 145 us
  waiting for transfers between devices  48.8 us (33%)
  starting transfers between devices  36.5 us (25%)
  Pallas kernels  27.4 us (19%)
  blocking collectives  20.7 us (14%)
  local copies, waits for them, and re-layouts  10.9 us (7%)
    pallas_call x9, Pallas kernels, call(): pl.pallas_call(kernel, out_shape=outs, in_specs=[pl.BlockSpec(memory_spac...  27.4 us
    all_to_all x1, blocking collectives, gather_ctx(): lax.all_to_all(jnp.broadcast_to(item[None], (n,) + item.shape), CTX, spli...  20.7 us
    ppermute x3, waiting for transfers between devices, local(): lax.ppermute(part, 'x', shift(nx, -i))  15.9 us
    ppermute x4, starting transfers between devices, both_ways(): lax.ppermute(pair[1], axis, shift(n, -1))  13.4 us
    ppermute x4, waiting for transfers between devices, both_ways(): lax.ppermute(pair[0], axis, shift(n, 1))  10.3 us
    ppermute x4, waiting for transfers between devices, both_ways(): lax.ppermute(pair[1], axis, shift(n, -1))  8.38 us
    unnamed x40, local copies, waits for them, and re-layouts  7.76 us
    ppermute x3, waiting for transfers between devices, local(): lax.ppermute(pair, 'y', shift(ny, i))  5.37 us
  transfers between devices with their start and end apart: 25, of which 16 were waited for; matrix products, arithmetic and copies ran while one was open for 0% of the time, Pallas kernels for 15%

profile of v2, /device:TPU:1, one launch (start us, length us, event | category | flops | bytes accessed | tf_op | source)
XLA Modules:
  0.0 145.3 jit_solution(14930664767582777788)
XLA Ops:
  0.6 3.1 %dynamic-slice_bitcast_fusion = bf16[4,1024,256]{2,1,0:T(8,128)(2,1)} fusion(bf16[4,2,1024,256]{3,2,1,0:T(8,128)(2,1)} %bitcast.13, s32[]{:T(128)S(6)} %select_n.4), kind=kLoop, calls=%fused_computation | loop fusion | bytes 4194308 | tf_op jit(solution)/shard_map/jit(dynamic_index_in_dim)/squeeze | solution.py:541
  3.7 5.0 %all-to-all-start = ((bf16[4,1024,256]{2,1,0:T(8,128)(2,1)}), bf16[4,1024,256]{2,1,0:T(8,128)(2,1)S(1)}, u32[]{:S(2)}, u32[]{:S(2)}) async-start(bf16[4,1024,256]{2,1,0:T(8,128)(2,1)} %dynamic-slice_bitcast_fusion), calls=%async_computation | async-start | bytes 4194304 | tf_op jit(solution)/shard_map/all_to_all | solution.py:544
  8.7 5.6 %collective-permute-start.1 = (bf16[1024,256]{1,0:T(8,128)(2,1)S(1)}, bf16[1024,256]{1,0:T(8,128)(2,1)S(1)}, u32[]{:S(2)}, u32[]{:S(2)}) collective-permute-start(bf16[1024,256]{1,0:T(8,128)(2,1)S(1)} %copy-done), channel_id=1, source_target_pairs={{0,7},{1,0},{2,1},{3,2},{4,3},{5,4},{6,5},{7,6},{8,15},{9,8},{10,9... | collective-permute-start | bytes 1572872 | tf_op jit(solution)/shard_map/ppermute | solution.py:536
  14.3 1.0 copy-done.8
  15.4 2.7 %shard_map.118 = (f32[1024,256]{1,0:T(8,128)S(1)}, f32[32,256]{1,0:T(8,128)S(1)}, bf16[256,1024]{1,0:T(8,128)(2,1)S(1)}, f32[16,128,128]{2,1,0:T(8,128)S(1)}) custom-call(bf16[1024,256]{1,0:T(8,128)(2,1)S(1)} %copy-done.6, bf16[1024,256]{1,0:T(8,128)(2,1)S(1)} %copy-done.8, f32[16,16]{1,0:T(8,128)S(1)} %copy-done.18, f32[16,16]{1,0:T(8,128)S(1)} %copy-done.19), custom_call_target="tpu_custom_call" | custom-call | flops 1000 | bytes 36900000 | tf_op jit(solution)/shard_map/pallas_call | solution.py:483
  18.1 1.0 copy-done.12
  19.0 1.0 copy-done.14
  20.0 0.8 copy-done.16
  20.8 3.8 %collective-permute-done.1.refs_2_ = bf16[1024,256]{1,0:T(8,128)(2,1)S(1)} collective-permute-done((bf16[1024,256]{1,0:T(8,128)(2,1)S(1)}, bf16[1024,256]{1,0:T(8,128)(2,1)S(1)}, u32[]{:S(2)}, u32[]{:S(2)}) %collective-permute-start.1) | collective-permute-done | bytes 524320 | tf_op jit(solution)/shard_map/ppermute | solution.py:536
  24.6 3.1 %collective-permute-done.refs_1_ = bf16[1024,256]{1,0:T(8,128)(2,1)S(1)} collective-permute-done((bf16[1024,256]{1,0:T(8,128)(2,1)S(1)}, bf16[1024,256]{1,0:T(8,128)(2,1)S(1)}, u32[]{:S(2)}, u32[]{:S(2)}) %collective-permute-start) | collective-permute-done | bytes 524320 | tf_op jit(solution)/shard_map/ppermute | solution.py:535
  27.7 0.8 copy-done.4
  28.5 2.7 %collective-permute-start.3 = (bf16[1024,256]{1,0:T(8,128)(2,1)S(1)}, bf16[1024,256]{1,0:T(8,128)(2,1)}, u32[]{:S(2)}, u32[]{:S(2)}) collective-permute-start(bf16[1024,256]{1,0:T(8,128)(2,1)S(1)} %collective-permute-done.1.refs_2_), channel_id=1, source_target_pairs={{0,7},{1,0},{2,1},{3,2},{4,3},{5,4},{6,5},{7,6},{8,15},{9,8},{10,9... | collective-permute-start | bytes 1572872 | tf_op jit(solution)/shard_map/ppermute | solution.py:536
  31.1 0.8 copy-done.2
  31.9 2.7 %collective-permute-start.4 = (f32[32,256]{1,0:T(8,128)S(1)}, f32[32,256]{1,0:T(8,128)S(1)}, u32[]{:S(2)}, u32[]{:S(2)}) collective-permute-start(f32[32,256]{1,0:T(8,128)S(1)} %get-tuple-element.48.own_ref), channel_id=1, source_target_pairs={{0,32},{32,0},{1,33},{33,1},{2,34},{34,2},{3,35},{35,3},{4,36},{36... | collective-permute-start | bytes 98312 | tf_op jit(solution)/shard_map/ppermute | solution.py:565
  34.7 0.9 collective-permute-done.4.other_ref
  35.5 2.7 %collective-permute-start.7 = (f32[2,32,256]{2,1,0:T(8,128)S(1)}, f32[2,32,256]{2,1,0:T(8,128)S(1)}, u32[]{:S(2)}, u32[]{:S(2)}) collective-permute-start(f32[2,32,256]{2,1,0:T(8,128)S(1)} %pad_maximum_fusion), channel_id=1, source_target_pairs={{0,192},{64,0},{128,64},{192,128},{1,193},{65,1},{129,65},{193,129... | collective-permute-start | bytes 196616 | tf_op jit(solution)/shard_map/ppermute | solution.py:569
  38.6 0.7 collective-permute-start.5
  39.6 3.4 %collective-permute-done.6.p2_ref = f32[2,32,256]{2,1,0:T(8,128)S(1)} collective-permute-done((f32[2,32,256]{2,1,0:T(8,128)S(1)}, f32[2,32,256]{2,1,0:T(8,128)S(1)}, u32[]{:S(2)}, u32[]{:S(2)}) %collective-permute-start.6) | collective-permute-done | bytes 65568 | tf_op jit(solution)/shard_map/ppermute | solution.py:569
  43.0 1.7 %collective-permute-done.5.p1_ref = f32[2,32,256]{2,1,0:T(8,128)S(1)} collective-permute-done((f32[2,32,256]{2,1,0:T(8,128)S(1)}, f32[2,32,256]{2,1,0:T(8,128)S(1)}, u32[]{:S(2)}, u32[]{:S(2)}) %collective-permute-start.5) | collective-permute-done | bytes 65568 | tf_op jit(solution)/shard_map/ppermute | solution.py:569
  44.7 1.1 collective-permute-start.12
  45.8 2.7 %collective-permute-start.9 = (bf16[1024,256]{1,0:T(8,128)(2,1)}, bf16[1024,256]{1,0:T(8,128)(2,1)S(1)}, u32[]{:S(2)}, u32[]{:S(2)}) collective-permute-start(bf16[1024,256]{1,0:T(8,128)(2,1)} %collective-permute-done.3.refs_4_), channel_id=1, source_target_pairs={{0,7},{1,0},{2,1},{3,2},{4,3},{5,4},{6,5},{7,6},{8,15},{9,8},{10,9... | collective-permute-start | bytes 1572872 | tf_op jit(solution)/shard_map/ppermute | solution.py:536
  48.6 1.1 copy-done.10
  49.7 1.2 copy-done.15
  50.9 1.5 %shard_map.119 = (f32[1024,256]{1,0:T(8,128)S(1)}, bf16[256,1024]{1,0:T(8,128)(2,1)S(1)}, f32[32,256]{1,0:T(8,128)S(1)}) custom-call(s32[4]{0:T(128)S(1)} %pad_add_fusion.here_ref, f32[32,256]{1,0:T(8,128)S(1)} %get-tuple-element.48.own_ref, f32[32,256]{1,0:T(8,128)S(1)} %collective-permute-done.4.other_ref, ...), custom_call_target="tpu_custom_call" | custom-call | flops 1000 | bytes 36900000 | tf_op jit(solution)/shard_map/pallas_call | solution.py:483
  52.5 2.8 %collective-permute-start.15 = (bf16[256,1024]{1,0:T(8,128)(2,1)S(1)}, bf16[256,1024]{1,0:T(8,128)(2,1)S(1)}, u32[]{:S(2)}, u32[]{:S(2)}) collective-permute-start(bf16[256,1024]{1,0:T(8,128)(2,1)S(1)} %get-tuple-element.69.refs_9_.refs_10_), channel_id=1, source_target_pairs={{0,24},{8,0},{16,8},{24,16},{1,25},{9,1},{17,9},{25,17},{2,26},{10... | collective-permute-start | bytes 1572872 | tf_op jit(solution)/shard_map/ppermute | solution.py:587
  56.4 4.3 %collective-permute-done.8.refs_5_ = bf16[1024,256]{1,0:T(8,128)(2,1)S(1)} collective-permute-done((bf16[1024,256]{1,0:T(8,128)(2,1)}, bf16[1024,256]{1,0:T(8,128)(2,1)S(1)}, u32[]{:S(2)}, u32[]{:S(2)}) %collective-permute-start.8) | collective-permute-done | bytes 524320 | tf_op jit(solution)/shard_map/ppermute | solution.py:535
  60.7 2.4 %collective-permute-start.11 = (bf16[512,256]{1,0:T(8,128)(2,1)S(1)}, bf16[512,256]{1,0:T(8,128)(2,1)S(1)}, u32[]{:S(2)}, u32[]{:S(2)}) collective-permute-start(bf16[512,256]{1,0:T(8,128)(2,1)S(1)} %slice.7), channel_id=1, source_target_pairs={{0,7},{1,0},{2,1},{3,2},{4,3},{5,4},{6,5},{7,6},{8,15},{9,8},{10,9... | collective-permute-start | bytes 786440 | tf_op jit(solution)/shard_map/ppermute | solution.py:536
  63.2 4.6 %collective-permute-done.11.refs_8_ = bf16[512,256]{1,0:T(8,128)(2,1)S(1)} collective-permute-done((bf16[512,256]{1,0:T(8,128)(2,1)S(1)}, bf16[512,256]{1,0:T(8,128)(2,1)S(1)}, u32[]{:S(2)}, u32[]{:S(2)}) %collective-permute-start.11) | collective-permute-done | bytes 262176 | tf_op jit(solution)/shard_map/ppermute | solution.py:536
  67.8 2.9 %collective-permute-done.10.refs_7_ = bf16[512,256]{1,0:T(8,128)(2,1)S(1)} collective-permute-done((bf16[512,256]{1,0:T(8,128)(2,1)S(1)}, bf16[512,256]{1,0:T(8,128)(2,1)S(1)}, u32[]{:S(2)}, u32[]{:S(2)}) %collective-permute-start.10) | collective-permute-done | bytes 262176 | tf_op jit(solution)/shard_map/ppermute | solution.py:535
  70.7 7.2 %shard_map.120 = (bf16[1024,256]{1,0:T(8,128)(2,1)S(1)}, bf16[1024,256]{1,0:T(8,128)(2,1)S(1)}, bf16[1024,256]{1,0:T(8,128)(2,1)S(1)}, bf16[1024,256]{1,0:T(8,128)(2,1)S(1)}) custom-call(s32[4]{0:T(128)S(1)} %pad_add_fusion.here_ref, bf16[1024,256]{1,0:T(8,128)(2,1)S(1)} %copy-done.1, bf16[1024,256]{1,0:T(8,128)(2,1)S(1)} %copy-done.5, ...), custom_call_target="tpu_custom_call" | custom-call | flops 1000 | bytes 22140000 | tf_op jit(solution)/shard_map/pallas_call | solution.py:483
  78.0 3.9 %collective-permute-done.13.refs_10_.refs_11_ = bf16[256,1024]{1,0:T(8,128)(2,1)S(1)} collective-permute-done((bf16[256,1024]{1,0:T(8,128)(2,1)S(1)}, bf16[256,1024]{1,0:T(8,128)(2,1)S(1)}, u32[]{:S(2)}, u32[]{:S(2)}) %collective-permute-start.13) | collective-permute-done | bytes 524320 | tf_op jit(solution)/shard_map/ppermute | solution.py:587
  81.8 3.7 %shard_map.121 = bf16[4,256,1024]{2,1,0:T(8,128)(2,1)S(1)} custom-call(s32[4]{0:T(128)S(1)} %pad_add_fusion.here_ref, bf16[1024,256]{1,0:T(8,128)(2,1)S(1)} %copy-done.1, bf16[1024,256]{1,0:T(8,128)(2,1)S(1)} %copy-done.5, bf16[1024,256]{1,0:T(8,128)(2,1)S(1)} %copy-done.3, bf16[1024,256]{1,0:T(8,128)(2,1)} %collective-permute-done.2.refs_3_, ...), custom_call_target="tpu_custom_call" | custom-call | flops 1000 | bytes 1845000 | tf_op jit(solution)/shard_map/pallas_call | solution.py:483
  86.1 1.0 collective-permute-start.17
  87.1 0.9 collective-permute-start.18
  88.6 1.3 collective-permute-done.16.refs_9_
  89.9 4.0 %shard_map.122 = (bf16[256,1024]{1,0:T(8,128)(2,1)S(1)}, bf16[256,1024]{1,0:T(8,128)(2,1)S(1)}, bf16[256,1024]{1,0:T(8,128)(2,1)S(1)}, bf16[256,1024]{1,0:T(8,128)(2,1)S(1)}) custom-call(s32[4]{0:T(128)S(1)} %pad_add_fusion.here_ref, bf16[1024,256]{1,0:T(8,128)(2,1)S(1)} %copy-done.1, bf16[1024,256]{1,0:T(8,128)(2,1)S(1)} %copy-done.5, ...), custom_call_target="tpu_custom_call" | custom-call | flops 1000 | bytes 1845000 | tf_op jit(solution)/shard_map/pallas_call | solution.py:483
  94.0 2.0 %collective-permute-start.21 = (bf16[256,1024]{1,0:T(8,128)(2,1)S(1)}, bf16[256,1024]{1,0:T(8,128)(2,1)S(1)}, u32[]{:S(2)}, u32[]{:S(2)}) collective-permute-start(bf16[256,1024]{1,0:T(8,128)(2,1)S(1)} %get-tuple-element.72), channel_id=1, source_target_pairs={{0,128},{64,192},{128,0},{192,64},{1,129},{65,193},{129,1},{193,65... | collective-permute-start | bytes 1572872 | tf_op jit(solution)/shard_map/ppermute | solution.py:633
  96.0 5.1 %collective-permute-done.17.p1_ref = bf16[1024,256]{1,0:T(8,128)(2,1)S(1)} collective-permute-done((bf16[1024,256]{1,0:T(8,128)(2,1)S(1)}, bf16[1024,256]{1,0:T(8,128)(2,1)S(1)}, u32[]{:S(2)}, u32[]{:S(2)}) %collective-permute-start.17) | collective-permute-done | bytes 524320 | tf_op jit(solution)/shard_map/ppermute | solution.py:608
  101.1 0.8 collective-permute-start.22
  101.9 8.8 %collective-permute-done.18.p2_ref = bf16[1024,256]{1,0:T(8,128)(2,1)S(1)} collective-permute-done((bf16[1024,256]{1,0:T(8,128)(2,1)S(1)}, bf16[1024,256]{1,0:T(8,128)(2,1)S(1)}, u32[]{:S(2)}, u32[]{:S(2)}) %collective-permute-start.18) | collective-permute-done | bytes 524320 | tf_op jit(solution)/shard_map/ppermute | solution.py:608
  110.7 2.0 %collective-permute-done.19.p3_ref = bf16[1024,256]{1,0:T(8,128)(2,1)S(1)} collective-permute-done((bf16[1024,256]{1,0:T(8,128)(2,1)S(1)}, bf16[1024,256]{1,0:T(8,128)(2,1)S(1)}, u32[]{:S(2)}, u32[]{:S(2)}) %collective-permute-start.19) | collective-permute-done | bytes 524320 | tf_op jit(solution)/shard_map/ppermute | solution.py:608
  112.7 4.4 %shard_map.123 = (bf16[1024,256]{1,0:T(8,128)(2,1)}, f32[1024,256]{1,0:T(8,128)S(1)}, f32[24,256]{1,0:T(8,128)S(1)}) custom-call(bf16[1024,256]{1,0:T(8,128)(2,1)S(1)} %get-tuple-element.74.own_ref, bf16[1024,256]{1,0:T(8,128)(2,1)S(1)} %collective-permute-done.17.p1_ref, bf16[1024,256]{1,0:T(8,128)(2,1)S(1)} %collective-permute-done.18.p2_ref, ...), custom_call_target="tpu_custom_call" | custom-call | flops 1000 | bytes 73800000 | tf_op jit(solution)/shard_map/pallas_call | solution.py:483
  117.1 1.8 %collective-permute-done.21.c_ref = bf16[256,1024]{1,0:T(8,128)(2,1)S(1)} collective-permute-done((bf16[256,1024]{1,0:T(8,128)(2,1)S(1)}, bf16[256,1024]{1,0:T(8,128)(2,1)S(1)}, u32[]{:S(2)}, u32[]{:S(2)}) %collective-permute-start.21) | collective-permute-done | bytes 524320 | tf_op jit(solution)/shard_map/ppermute | solution.py:633
  118.9 0.9 collective-permute-done.22.d_ref
  120.1 0.7 collective-permute-start.23
  120.9 20.7 %all_to_all.10.all_ref = f32[8,24,256]{2,1,0:T(8,128)S(1)} all-to-all(f32[8,24,256]{2,1,0:T(8,128)S(1)} %broadcast_in_dim.2), channel_id=1, replica_groups=mesh['y'=4,'core'=2,'x'=4,'z'=8] {'y','core'}, dimensions={0} | all-to-all | bytes 393216 | tf_op jit(solution)/shard_map/all_to_all | solution.py:507
  141.6 2.5 %shard_map.124 = (bf16[1024,256]{1,0:T(8,128)(2,1)}, bf16[1024,256]{1,0:T(8,128)(2,1)}, f32[16,16]{1,0:T(8,128)}, f32[16,16]{1,0:T(8,128)}) custom-call(s32[4]{0:T(128)S(1)} %pad_add_fusion.here_ref, f32[8,24,256]{2,1,0:T(8,128)S(1)} %all_to_all.10.all_ref, f32[1024,256]{1,0:T(8,128)S(1)} %get-tuple-element.84.back_ref, bf16[1024,256]{1,0:T(8,128)(2,1)S(1)} %copy-done.7, ...), custom_call_target="tpu_custom_call" | custom-call | flops 1000 | bytes 9225000 | tf_op jit(solution)/shard_map/pallas_call | solution.py:483
  144.1 1.2 shard_map.126
  (58 shorter events, 3.5 us)
Async XLA Ops:
  3.7 5.0 %copy-start = (bf16[1024,256]{1,0:T(8,128)(2,1)S(1)}, bf16[1024,256]{1,0:T(8,128)(2,1)}, u32[]{:S(2)}) copy-start(bf16[1024,256]{1,0:T(8,128)(2,1)} %refs_0_.4) | copy-start | bytes 1572868
  3.7 10.6 %copy-start.6 = (bf16[1024,256]{1,0:T(8,128)(2,1)S(1)}, bf16[1024,256]{1,0:T(8,128)(2,1)}, u32[]{:S(2)}) copy-start(bf16[1024,256]{1,0:T(8,128)(2,1)} %key_ref.3) | copy-start | bytes 1572868
  3.7 10.6 %copy-start.18 = (f32[16,16]{1,0:T(8,128)S(1)}, f32[16,16]{1,0:T(8,128)}, u32[]{:S(2)}) copy-start(f32[16,16]{1,0:T(8,128)} %rate_ref.7) | copy-start | bytes 3076
  3.7 10.6 %copy-start.19 = (f32[16,16]{1,0:T(8,128)S(1)}, f32[16,16]{1,0:T(8,128)}, u32[]{:S(2)}) copy-start(f32[16,16]{1,0:T(8,128)} %res_ref.7) | copy-start | bytes 3076
  3.7 41.0 %all-to-all-start = ((bf16[4,1024,256]{2,1,0:T(8,128)(2,1)}), bf16[4,1024,256]{2,1,0:T(8,128)(2,1)S(1)}, u32[]{:S(2)}, u32[]{:S(2)}) async-start(bf16[4,1024,256]{2,1,0:T(8,128)(2,1)} %dynamic-slice_bitcast_fusion), calls=%async_computation | async-start | bytes 4194304 | tf_op jit(solution)/shard_map/all_to_all | solution.py:544
  8.7 15.8 %collective-permute-start.1 = (bf16[1024,256]{1,0:T(8,128)(2,1)S(1)}, bf16[1024,256]{1,0:T(8,128)(2,1)S(1)}, u32[]{:S(2)}, u32[]{:S(2)}) collective-permute-start(bf16[1024,256]{1,0:T(8,128)(2,1)S(1)} %copy-done), channel_id=1, source_target_pairs={{0,7},{1,0},{2,1},{3,2},{4,3},{5,4},{6,5},{7,6},{8,15},{9,8},{10,9... | collective-permute-start | bytes 1572872 | tf_op jit(solution)/shard_map/ppermute | solution.py:536
  14.3 13.4 %collective-permute-start = (bf16[1024,256]{1,0:T(8,128)(2,1)S(1)}, bf16[1024,256]{1,0:T(8,128)(2,1)S(1)}, u32[]{:S(2)}, u32[]{:S(2)}) collective-permute-start(bf16[1024,256]{1,0:T(8,128)(2,1)S(1)} %copy-done), channel_id=1, source_target_pairs={{0,1},{1,2},{2,3},{3,4},{4,5},{5,6},{6,7},{7,0},{8,9},{9,10},{10,1... | collective-permute-start | bytes 1572872 | tf_op jit(solution)/shard_map/ppermute | solution.py:535
  14.3 1.0 copy-start.8
  18.0 1.0 copy-start.12
  19.0 1.0 copy-start.14
  20.0 0.8 copy-start.16
  27.7 17.0 %collective-permute-start.2 = (bf16[1024,256]{1,0:T(8,128)(2,1)S(1)}, bf16[1024,256]{1,0:T(8,128)(2,1)}, u32[]{:S(2)}, u32[]{:S(2)}) collective-permute-start(bf16[1024,256]{1,0:T(8,128)(2,1)S(1)} %collective-permute-done.refs_1_), channel_id=1, source_target_pairs={{0,1},{1,2},{2,3},{3,4},{4,5},{5,6},{6,7},{7,0},{8,9},{9,10},{10,1... | collective-permute-start | bytes 1572872 | tf_op jit(solution)/shard_map/ppermute | solution.py:535
  27.7 0.8 copy-start.4
  28.5 16.2 %collective-permute-start.3 = (bf16[1024,256]{1,0:T(8,128)(2,1)S(1)}, bf16[1024,256]{1,0:T(8,128)(2,1)}, u32[]{:S(2)}, u32[]{:S(2)}) collective-permute-start(bf16[1024,256]{1,0:T(8,128)(2,1)S(1)} %collective-permute-done.1.refs_2_), channel_id=1, source_target_pairs={{0,7},{1,0},{2,1},{3,2},{4,3},{5,4},{6,5},{7,6},{8,15},{9,8},{10,9... | collective-permute-start | bytes 1572872 | tf_op jit(solution)/shard_map/ppermute | solution.py:536
  31.1 0.8 copy-start.2
  31.9 3.6 %collective-permute-start.4 = (f32[32,256]{1,0:T(8,128)S(1)}, f32[32,256]{1,0:T(8,128)S(1)}, u32[]{:S(2)}, u32[]{:S(2)}) collective-permute-start(f32[32,256]{1,0:T(8,128)S(1)} %get-tuple-element.48.own_ref), channel_id=1, source_target_pairs={{0,32},{32,0},{1,33},{33,1},{2,34},{34,2},{3,35},{35,3},{4,36},{36... | collective-permute-start | bytes 98312 | tf_op jit(solution)/shard_map/ppermute | solution.py:565
  35.5 4.1 %collective-permute-start.7 = (f32[2,32,256]{2,1,0:T(8,128)S(1)}, f32[2,32,256]{2,1,0:T(8,128)S(1)}, u32[]{:S(2)}, u32[]{:S(2)}) collective-permute-start(f32[2,32,256]{2,1,0:T(8,128)S(1)} %pad_maximum_fusion), channel_id=1, source_target_pairs={{0,192},{64,0},{128,64},{192,128},{1,193},{65,1},{129,65},{193,129... | collective-permute-start | bytes 196616 | tf_op jit(solution)/shard_map/ppermute | solution.py:569
  38.3 4.7 %collective-permute-start.6 = (f32[2,32,256]{2,1,0:T(8,128)S(1)}, f32[2,32,256]{2,1,0:T(8,128)S(1)}, u32[]{:S(2)}, u32[]{:S(2)}) collective-permute-start(f32[2,32,256]{2,1,0:T(8,128)S(1)} %pad_maximum_fusion), channel_id=1, source_target_pairs={{0,128},{64,192},{128,0},{192,64},{1,129},{65,193},{129,1},{193,65... | collective-permute-start | bytes 196616 | tf_op jit(solution)/shard_map/ppermute | solution.py:569
  38.6 6.1 %collective-permute-start.5 = (f32[2,32,256]{2,1,0:T(8,128)S(1)}, f32[2,32,256]{2,1,0:T(8,128)S(1)}, u32[]{:S(2)}, u32[]{:S(2)}) collective-permute-start(f32[2,32,256]{2,1,0:T(8,128)S(1)} %pad_maximum_fusion), channel_id=1, source_target_pairs={{0,64},{64,128},{128,192},{192,0},{1,65},{65,129},{129,193},{193,1... | collective-permute-start | bytes 196616 | tf_op jit(solution)/shard_map/ppermute | solution.py:569
  44.7 7.8 %collective-permute-start.12 = (bf16[4,1024,256]{2,1,0:T(8,128)(2,1)S(1)}, bf16[4,1024,256]{2,1,0:T(8,128)(2,1)}, u32[]{:S(2)}, u32[]{:S(2)}) collective-permute-start(bf16[4,1024,256]{2,1,0:T(8,128)(2,1)S(1)} %all-to-all-done.refs_9_), channel_id=1, source_target_pairs={{0,32},{32,0},{1,33},{33,1},{2,34},{34,2},{3,35},{35,3},{4,36},{36... | collective-permute-start | bytes 6291464 | tf_op jit(solution)/shard_map/ppermute | solution.py:585
  45.8 14.9 %collective-permute-start.8 = (bf16[1024,256]{1,0:T(8,128)(2,1)}, bf16[1024,256]{1,0:T(8,128)(2,1)S(1)}, u32[]{:S(2)}, u32[]{:S(2)}) collective-permute-start(bf16[1024,256]{1,0:T(8,128)(2,1)} %collective-permute-done.2.refs_3_), channel_id=1, source_target_pairs={{0,1},{1,2},{2,3},{3,4},{4,5},{5,6},{6,7},{7,0},{8,9},{9,10},{10,1... | collective-permute-start | bytes 1572872 | tf_op jit(solution)/shard_map/ppermute | solution.py:535
  45.8 14.9 %collective-permute-start.9 = (bf16[1024,256]{1,0:T(8,128)(2,1)}, bf16[1024,256]{1,0:T(8,128)(2,1)S(1)}, u32[]{:S(2)}, u32[]{:S(2)}) collective-permute-start(bf16[1024,256]{1,0:T(8,128)(2,1)} %collective-permute-done.3.refs_4_), channel_id=1, source_target_pairs={{0,7},{1,0},{2,1},{3,2},{4,3},{5,4},{6,5},{7,6},{8,15},{9,8},{10,9... | collective-permute-start | bytes 1572872 | tf_op jit(solution)/shard_map/ppermute | solution.py:536
  48.5 22.2 %copy-start.1 = (bf16[1024,256]{1,0:T(8,128)(2,1)S(1)}, bf16[1024,256]{1,0:T(8,128)(2,1)}, u32[]{:S(2)}) copy-start(bf16[1024,256]{1,0:T(8,128)(2,1)} %refs_0_.4) | copy-start | bytes 1572868
  48.5 22.2 %copy-start.3 = (bf16[1024,256]{1,0:T(8,128)(2,1)S(1)}, bf16[1024,256]{1,0:T(8,128)(2,1)}, u32[]{:S(2)}) copy-start(bf16[1024,256]{1,0:T(8,128)(2,1)} %copy-done.2) | copy-start | bytes 1572868
  48.5 22.2 %copy-start.5 = (bf16[1024,256]{1,0:T(8,128)(2,1)S(1)}, bf16[1024,256]{1,0:T(8,128)(2,1)}, u32[]{:S(2)}) copy-start(bf16[1024,256]{1,0:T(8,128)(2,1)} %copy-done.4) | copy-start | bytes 1572868
  48.6 1.1 copy-start.10
  49.7 1.2 copy-start.15
  52.5 25.5 %collective-permute-start.15 = (bf16[256,1024]{1,0:T(8,128)(2,1)S(1)}, bf16[256,1024]{1,0:T(8,128)(2,1)S(1)}, u32[]{:S(2)}, u32[]{:S(2)}) collective-permute-start(bf16[256,1024]{1,0:T(8,128)(2,1)S(1)} %get-tuple-element.69.refs_9_.refs_10_), channel_id=1, source_target_pairs={{0,24},{8,0},{16,8},{24,16},{1,25},{9,1},{17,9},{25,17},{2,26},{10... | collective-permute-start | bytes 1572872 | tf_op jit(solution)/shard_map/ppermute | solution.py:587
  55.2 22.7 %collective-permute-start.14 = (bf16[256,1024]{1,0:T(8,128)(2,1)S(1)}, bf16[256,1024]{1,0:T(8,128)(2,1)S(1)}, u32[]{:S(2)}, u32[]{:S(2)}) collective-permute-start(bf16[256,1024]{1,0:T(8,128)(2,1)S(1)} %get-tuple-element.69.refs_9_.refs_10_), channel_id=1, source_target_pairs={{0,16},{8,24},{16,0},{24,8},{1,17},{9,25},{17,1},{25,9},{2,18},{10... | collective-permute-start | bytes 1572872 | tf_op jit(solution)/shard_map/ppermute | solution.py:587
  55.8 26.0 %collective-permute-start.13 = (bf16[256,1024]{1,0:T(8,128)(2,1)S(1)}, bf16[256,1024]{1,0:T(8,128)(2,1)S(1)}, u32[]{:S(2)}, u32[]{:S(2)}) collective-permute-start(bf16[256,1024]{1,0:T(8,128)(2,1)S(1)} %get-tuple-element.69.refs_9_.refs_10_), channel_id=1, source_target_pairs={{0,8},{8,16},{16,24},{24,0},{1,9},{9,17},{17,25},{25,1},{2,10},{10... | collective-permute-start | bytes 1572872 | tf_op jit(solution)/shard_map/ppermute | solution.py:587
  60.7 7.0 %collective-permute-start.11 = (bf16[512,256]{1,0:T(8,128)(2,1)S(1)}, bf16[512,256]{1,0:T(8,128)(2,1)S(1)}, u32[]{:S(2)}, u32[]{:S(2)}) collective-permute-start(bf16[512,256]{1,0:T(8,128)(2,1)S(1)} %slice.7), channel_id=1, source_target_pairs={{0,7},{1,0},{2,1},{3,2},{4,3},{5,4},{6,5},{7,6},{8,15},{9,8},{10,9... | collective-permute-start | bytes 786440 | tf_op jit(solution)/shard_map/ppermute | solution.py:536
  63.2 7.5 %collective-permute-start.10 = (bf16[512,256]{1,0:T(8,128)(2,1)S(1)}, bf16[512,256]{1,0:T(8,128)(2,1)S(1)}, u32[]{:S(2)}, u32[]{:S(2)}) collective-permute-start(bf16[512,256]{1,0:T(8,128)(2,1)S(1)} %slice.6), channel_id=1, source_target_pairs={{0,1},{1,2},{2,3},{3,4},{4,5},{5,6},{6,7},{7,0},{8,9},{9,10},{10,1... | collective-permute-start | bytes 786440 | tf_op jit(solution)/shard_map/ppermute | solution.py:535
  85.5 4.4 %collective-permute-start.16 = (bf16[4,256,1024]{2,1,0:T(8,128)(2,1)S(1)}, bf16[4,256,1024]{2,1,0:T(8,128)(2,1)S(1)}, u32[]{:S(2)}, u32[]{:S(2)}) collective-permute-start(bf16[4,256,1024]{2,1,0:T(8,128)(2,1)S(1)} %shard_map.121), channel_id=1, source_target_pairs={{0,32},{32,0},{1,33},{33,1},{2,34},{34,2},{3,35},{35,3},{4,36},{36... | collective-permute-start | bytes 6291464 | tf_op jit(solution)/shard_map/ppermute | solution.py:621
  86.1 15.0 %collective-permute-start.17 = (bf16[1024,256]{1,0:T(8,128)(2,1)S(1)}, bf16[1024,256]{1,0:T(8,128)(2,1)S(1)}, u32[]{:S(2)}, u32[]{:S(2)}) collective-permute-start(bf16[1024,256]{1,0:T(8,128)(2,1)S(1)} %get-tuple-element.75), channel_id=1, source_target_pairs={{0,16},{8,24},{16,0},{24,8},{1,17},{9,25},{17,1},{25,9},{2,18},{10... | collective-permute-start | bytes 1572872 | tf_op jit(solution)/shard_map/ppermute | solution.py:608
  87.1 23.6 %collective-permute-start.18 = (bf16[1024,256]{1,0:T(8,128)(2,1)S(1)}, bf16[1024,256]{1,0:T(8,128)(2,1)S(1)}, u32[]{:S(2)}, u32[]{:S(2)}) collective-permute-start(bf16[1024,256]{1,0:T(8,128)(2,1)S(1)} %get-tuple-element.76), channel_id=1, source_target_pairs={{0,24},{8,0},{16,8},{24,16},{1,25},{9,1},{17,9},{25,17},{2,26},{10... | collective-permute-start | bytes 1572872 | tf_op jit(solution)/shard_map/ppermute | solution.py:608
  88.0 24.7 %copy-start.11 = (bf16[1024,256]{1,0:T(8,128)(2,1)S(1)}, bf16[1024,256]{1,0:T(8,128)(2,1)}, u32[]{:S(2)}) copy-start(bf16[1024,256]{1,0:T(8,128)(2,1)} %query_ref.3) | copy-start | bytes 1572868
  88.0 24.7 %copy-start.13 = (f32[16,128,128]{2,1,0:T(8,128)S(1)}, f32[16,128,128]{2,1,0:T(8,128)}, u32[]{:S(2)}) copy-start(f32[16,128,128]{2,1,0:T(8,128)} %copy-done.12) | copy-start | bytes 3145732
  88.0 24.7 %copy-start.17 = (bf16[256,1024]{1,0:T(8,128)(2,1)S(1)}, bf16[256,1024]{1,0:T(8,128)(2,1)}, u32[]{:S(2)}) copy-start(bf16[256,1024]{1,0:T(8,128)(2,1)} %copy-done.16) | copy-start | bytes 1572868
  88.0 24.7 %collective-permute-start.19 = (bf16[1024,256]{1,0:T(8,128)(2,1)S(1)}, bf16[1024,256]{1,0:T(8,128)(2,1)S(1)}, u32[]{:S(2)}, u32[]{:S(2)}) collective-permute-start(bf16[1024,256]{1,0:T(8,128)(2,1)S(1)} %get-tuple-element.77), channel_id=1, source_target_pairs={{0,8},{8,16},{16,24},{24,0},{1,9},{9,17},{17,25},{25,1},{2,10},{10... | collective-permute-start | bytes 1572872 | tf_op jit(solution)/shard_map/ppermute | solution.py:608
  93.9 23.2 %collective-permute-start.20 = (bf16[256,1024]{1,0:T(8,128)(2,1)S(1)}, bf16[256,1024]{1,0:T(8,128)(2,1)S(1)}, u32[]{:S(2)}, u32[]{:S(2)}) collective-permute-start(bf16[256,1024]{1,0:T(8,128)(2,1)S(1)} %get-tuple-element.71), channel_id=1, source_target_pairs={{0,64},{64,128},{128,192},{192,0},{1,65},{65,129},{129,193},{193,1... | collective-permute-start | bytes 1572872 | tf_op jit(solution)/shard_map/ppermute | solution.py:633
  94.0 24.9 %collective-permute-start.21 = (bf16[256,1024]{1,0:T(8,128)(2,1)S(1)}, bf16[256,1024]{1,0:T(8,128)(2,1)S(1)}, u32[]{:S(2)}, u32[]{:S(2)}) collective-permute-start(bf16[256,1024]{1,0:T(8,128)(2,1)S(1)} %get-tuple-element.72), channel_id=1, source_target_pairs={{0,128},{64,192},{128,0},{192,64},{1,129},{65,193},{129,1},{193,65... | collective-permute-start | bytes 1572872 | tf_op jit(solution)/shard_map/ppermute | solution.py:633
  101.1 18.7 %collective-permute-start.22 = (bf16[256,1024]{1,0:T(8,128)(2,1)S(1)}, bf16[256,1024]{1,0:T(8,128)(2,1)S(1)}, u32[]{:S(2)}, u32[]{:S(2)}) collective-permute-start(bf16[256,1024]{1,0:T(8,128)(2,1)S(1)} %get-tuple-element.73), channel_id=1, source_target_pairs={{0,192},{64,0},{128,64},{192,128},{1,193},{65,1},{129,65},{193,129... | collective-permute-start | bytes 1572872 | tf_op jit(solution)/shard_map/ppermute | solution.py:633
  117.1 24.5 %copy-start.7 = (bf16[1024,256]{1,0:T(8,128)(2,1)S(1)}, bf16[1024,256]{1,0:T(8,128)(2,1)}, u32[]{:S(2)}) copy-start(bf16[1024,256]{1,0:T(8,128)(2,1)} %key_ref.3) | copy-start | bytes 1572868
  117.1 24.5 %copy-start.9 = (bf16[1024,256]{1,0:T(8,128)(2,1)S(1)}, bf16[1024,256]{1,0:T(8,128)(2,1)}, u32[]{:S(2)}) copy-start(bf16[1024,256]{1,0:T(8,128)(2,1)} %value_ref.3) | copy-start | bytes 1572868
  120.1 24.0 %collective-permute-start.23 = (bf16[256,1024]{1,0:T(8,128)(2,1)S(1)}, bf16[256,1024]{1,0:T(8,128)(2,1)S(1)}, u32[]{:S(2)}, u32[]{:S(2)}) collective-permute-start(bf16[256,1024]{1,0:T(8,128)(2,1)S(1)} %shard_map.125), channel_id=1, source_target_pairs={{0,0},{8,72},{16,144},{24,216},{64,8},{72,80},{80,152},{88,192},{1... | collective-permute-start | bytes 1572872 | tf_op jit(solution)/shard_map/ppermute | solution.py:657

commit v3 on v2

--- a/solution.py
+++ b/solution.py
@@ -583,8 +583,7 @@
     )
     hop3 = both_ways("z", after(hop2, all_ends))
     w_other = lax.ppermute(after(w_mine, hop2, all_ends), "core", swap)
-    sent = after(gated, w_other)
-    gates = [gated] + [lax.ppermute(sent, "x", shift(nx, i)) for i in range(1, nx)]
+    gates = [gated] + [lax.ppermute(gated, "x", shift(nx, i)) for i in range(1, nx)]
     right, left = after(hop3, gated)
     hop4 = both_ways("z", (right[: tokens // 2], left[tokens // 2 :]))
     blocks = [out_grad, *hop1, *hop2, *hop3, *hop4]

time: 146 us -> 156 us (1.068)
  waiting for transfers between devices: 48.8 us -> 59.2 us
    ppermute x4, waiting for transfers between devices: 10.3 us -> 19 us  [both_ways(): lax.ppermute(pair[0], axis, shift(n, 1))]
    ppermute x3, waiting for transfers between devices: 3.87 us -> 9.67 us  [local(): lax.ppermute(gated, 'x', shift(nx, i))]
    ppermute x4, waiting for transfers between devices: 8.38 us -> 4.54 us  [both_ways(): lax.ppermute(pair[1], axis, shift(n, -1))]
  transfers between devices with their start and end apart: 25 -> 25, of which waited for: 16 -> 16; matrix products, arithmetic and copies ran while one was open for 0% -> 0% of each run, Pallas kernels for 15% -> 14%
where the time goes in v3:
time: 156 us
  waiting for transfers between devices  59.2 us (38%)
  starting transfers between devices  36.6 us (23%)
  Pallas kernels  27.4 us (18%)
  blocking collectives  20.7 us (13%)
  local copies, waits for them, and re-layouts  10.9 us (7%)
    pallas_call x9, Pallas kernels, call(): pl.pallas_call(kernel, out_shape=outs, in_specs=[pl.BlockSpec(memory_spac...  27.4 us
    all_to_all x1, blocking collectives, gather_ctx(): lax.all_to_all(jnp.broadcast_to(item[None], (n,) + item.shape), CTX, spli...  20.7 us
    ppermute x4, waiting for transfers between devices, both_ways(): lax.ppermute(pair[0], axis, shift(n, 1))  19 us
    ppermute x3, waiting for transfers between devices, local(): lax.ppermute(part, 'x', shift(nx, -i))  15.3 us
    ppermute x4, starting transfers between devices, both_ways(): lax.ppermute(pair[1], axis, shift(n, -1))  13.4 us
    ppermute x3, waiting for transfers between devices, local(): lax.ppermute(gated, 'x', shift(nx, i))  9.67 us
    unnamed x40, local copies, waits for them, and re-layouts  7.76 us
    ppermute x3, waiting for transfers between devices, local(): lax.ppermute(pair, 'y', shift(ny, i))  5.37 us
  transfers between devices with their start and end apart: 25, of which 16 were waited for; matrix products, arithmetic and copies ran while one was open for 0% of the time, Pallas kernels for 14%

profile of v3, /device:TPU:1, one launch (start us, length us, event | category | flops | bytes accessed | tf_op | source)
XLA Modules:
  0.0 155.9 jit_solution(11947090374915645744)
XLA Ops:
  0.6 3.1 %dynamic-slice_bitcast_fusion = bf16[4,1024,256]{2,1,0:T(8,128)(2,1)} fusion(bf16[4,2,1024,256]{3,2,1,0:T(8,128)(2,1)} %bitcast.13, s32[]{:T(128)S(6)} %select_n.4), kind=kLoop, calls=%fused_computation | loop fusion | bytes 4194308 | tf_op jit(solution)/shard_map/jit(dynamic_index_in_dim)/squeeze | solution.py:541
  3.7 5.0 %all-to-all-start = ((bf16[4,1024,256]{2,1,0:T(8,128)(2,1)}), bf16[4,1024,256]{2,1,0:T(8,128)(2,1)S(1)}, u32[]{:S(2)}, u32[]{:S(2)}) async-start(bf16[4,1024,256]{2,1,0:T(8,128)(2,1)} %dynamic-slice_bitcast_fusion), calls=%async_computation | async-start | bytes 4194304 | tf_op jit(solution)/shard_map/all_to_all | solution.py:544
  8.7 5.6 %collective-permute-start.1 = (bf16[1024,256]{1,0:T(8,128)(2,1)S(1)}, bf16[1024,256]{1,0:T(8,128)(2,1)S(1)}, u32[]{:S(2)}, u32[]{:S(2)}) collective-permute-start(bf16[1024,256]{1,0:T(8,128)(2,1)S(1)} %copy-done), channel_id=1, source_target_pairs={{0,7},{1,0},{2,1},{3,2},{4,3},{5,4},{6,5},{7,6},{8,15},{9,8},{10,9... | collective-permute-start | bytes 1572872 | tf_op jit(solution)/shard_map/ppermute | solution.py:536
  14.3 1.0 copy-done.8
  15.4 2.7 %shard_map.118 = (f32[1024,256]{1,0:T(8,128)S(1)}, f32[32,256]{1,0:T(8,128)S(1)}, bf16[256,1024]{1,0:T(8,128)(2,1)S(1)}, f32[16,128,128]{2,1,0:T(8,128)S(1)}) custom-call(bf16[1024,256]{1,0:T(8,128)(2,1)S(1)} %copy-done.6, bf16[1024,256]{1,0:T(8,128)(2,1)S(1)} %copy-done.8, f32[16,16]{1,0:T(8,128)S(1)} %copy-done.18, f32[16,16]{1,0:T(8,128)S(1)} %copy-done.19), custom_call_target="tpu_custom_call" | custom-call | flops 1000 | bytes 36900000 | tf_op jit(solution)/shard_map/pallas_call | solution.py:483
  18.1 1.0 copy-done.12
  19.0 1.0 copy-done.14
  20.0 0.8 copy-done.16
  20.8 3.8 %collective-permute-done.1.refs_2_ = bf16[1024,256]{1,0:T(8,128)(2,1)S(1)} collective-permute-done((bf16[1024,256]{1,0:T(8,128)(2,1)S(1)}, bf16[1024,256]{1,0:T(8,128)(2,1)S(1)}, u32[]{:S(2)}, u32[]{:S(2)}) %collective-permute-start.1) | collective-permute-done | bytes 524320 | tf_op jit(solution)/shard_map/ppermute | solution.py:536
  24.6 3.1 %collective-permute-done.refs_1_ = bf16[1024,256]{1,0:T(8,128)(2,1)S(1)} collective-permute-done((bf16[1024,256]{1,0:T(8,128)(2,1)S(1)}, bf16[1024,256]{1,0:T(8,128)(2,1)S(1)}, u32[]{:S(2)}, u32[]{:S(2)}) %collective-permute-start) | collective-permute-done | bytes 524320 | tf_op jit(solution)/shard_map/ppermute | solution.py:535
  27.7 0.8 copy-done.4
  28.5 2.7 %collective-permute-start.3 = (bf16[1024,256]{1,0:T(8,128)(2,1)S(1)}, bf16[1024,256]{1,0:T(8,128)(2,1)}, u32[]{:S(2)}, u32[]{:S(2)}) collective-permute-start(bf16[1024,256]{1,0:T(8,128)(2,1)S(1)} %collective-permute-done.1.refs_2_), channel_id=1, source_target_pairs={{0,7},{1,0},{2,1},{3,2},{4,3},{5,4},{6,5},{7,6},{8,15},{9,8},{10,9... | collective-permute-start | bytes 1572872 | tf_op jit(solution)/shard_map/ppermute | solution.py:536
  31.1 0.8 copy-done.2
  31.9 2.7 %collective-permute-start.4 = (f32[32,256]{1,0:T(8,128)S(1)}, f32[32,256]{1,0:T(8,128)S(1)}, u32[]{:S(2)}, u32[]{:S(2)}) collective-permute-start(f32[32,256]{1,0:T(8,128)S(1)} %get-tuple-element.47.own_ref), channel_id=1, source_target_pairs={{0,32},{32,0},{1,33},{33,1},{2,34},{34,2},{3,35},{35,3},{4,36},{36... | collective-permute-start | bytes 98312 | tf_op jit(solution)/shard_map/ppermute | solution.py:565
  34.7 0.9 collective-permute-done.4.other_ref
  35.5 2.7 %collective-permute-start.7 = (f32[2,32,256]{2,1,0:T(8,128)S(1)}, f32[2,32,256]{2,1,0:T(8,128)S(1)}, u32[]{:S(2)}, u32[]{:S(2)}) collective-permute-start(f32[2,32,256]{2,1,0:T(8,128)S(1)} %pad_maximum_fusion), channel_id=1, source_target_pairs={{0,192},{64,0},{128,64},{192,128},{1,193},{65,1},{129,65},{193,129... | collective-permute-start | bytes 196616 | tf_op jit(solution)/shard_map/ppermute | solution.py:569
  38.6 0.7 collective-permute-start.5
  39.6 3.4 %collective-permute-done.6.p2_ref = f32[2,32,256]{2,1,0:T(8,128)S(1)} collective-permute-done((f32[2,32,256]{2,1,0:T(8,128)S(1)}, f32[2,32,256]{2,1,0:T(8,128)S(1)}, u32[]{:S(2)}, u32[]{:S(2)}) %collective-permute-start.6) | collective-permute-done | bytes 65568 | tf_op jit(solution)/shard_map/ppermute | solution.py:569
  43.0 1.7 %collective-permute-done.5.p1_ref = f32[2,32,256]{2,1,0:T(8,128)S(1)} collective-permute-done((f32[2,32,256]{2,1,0:T(8,128)S(1)}, f32[2,32,256]{2,1,0:T(8,128)S(1)}, u32[]{:S(2)}, u32[]{:S(2)}) %collective-permute-start.5) | collective-permute-done | bytes 65568 | tf_op jit(solution)/shard_map/ppermute | solution.py:569
  44.7 1.1 collective-permute-start.12
  45.8 2.7 %collective-permute-start.9 = (bf16[1024,256]{1,0:T(8,128)(2,1)}, bf16[1024,256]{1,0:T(8,128)(2,1)S(1)}, u32[]{:S(2)}, u32[]{:S(2)}) collective-permute-start(bf16[1024,256]{1,0:T(8,128)(2,1)} %collective-permute-done.3.refs_4_), channel_id=1, source_target_pairs={{0,7},{1,0},{2,1},{3,2},{4,3},{5,4},{6,5},{7,6},{8,15},{9,8},{10,9... | collective-permute-start | bytes 1572872 | tf_op jit(solution)/shard_map/ppermute | solution.py:536
  48.6 1.1 copy-done.10
  49.7 1.2 copy-done.15
  50.9 1.5 shard_map.119
  52.5 8.2 %collective-permute-done.8.refs_5_ = bf16[1024,256]{1,0:T(8,128)(2,1)S(1)} collective-permute-done((bf16[1024,256]{1,0:T(8,128)(2,1)}, bf16[1024,256]{1,0:T(8,128)(2,1)S(1)}, u32[]{:S(2)}, u32[]{:S(2)}) %collective-permute-start.8) | collective-permute-done | bytes 524320 | tf_op jit(solution)/shard_map/ppermute | solution.py:535
  60.7 2.4 %collective-permute-start.11 = (bf16[512,256]{1,0:T(8,128)(2,1)S(1)}, bf16[512,256]{1,0:T(8,128)(2,1)S(1)}, u32[]{:S(2)}, u32[]{:S(2)}) collective-permute-start(bf16[512,256]{1,0:T(8,128)(2,1)S(1)} %slice.7), channel_id=1, source_target_pairs={{0,7},{1,0},{2,1},{3,2},{4,3},{5,4},{6,5},{7,6},{8,15},{9,8},{10,9... | collective-permute-start | bytes 786440 | tf_op jit(solution)/shard_map/ppermute | solution.py:536
  63.1 2.7 %collective-permute-start.15 = (bf16[256,1024]{1,0:T(8,128)(2,1)S(1)}, bf16[256,1024]{1,0:T(8,128)(2,1)S(1)}, u32[]{:S(2)}, u32[]{:S(2)}) collective-permute-start(bf16[256,1024]{1,0:T(8,128)(2,1)S(1)} %get-tuple-element.54.refs_9_.refs_10_), channel_id=1, source_target_pairs={{0,24},{8,0},{16,8},{24,16},{1,25},{9,1},{17,9},{25,17},{2,26},{10... | collective-permute-start | bytes 1572872 | tf_op jit(solution)/shard_map/ppermute | solution.py:586
  67.0 0.7 collective-permute-done.11.refs_8_
  67.7 7.7 %collective-permute-done.10.refs_7_ = bf16[512,256]{1,0:T(8,128)(2,1)S(1)} collective-permute-done((bf16[512,256]{1,0:T(8,128)(2,1)S(1)}, bf16[512,256]{1,0:T(8,128)(2,1)S(1)}, u32[]{:S(2)}, u32[]{:S(2)}) %collective-permute-start.10) | collective-permute-done | bytes 262176 | tf_op jit(solution)/shard_map/ppermute | solution.py:535
  75.5 7.2 %shard_map.120 = (bf16[1024,256]{1,0:T(8,128)(2,1)S(1)}, bf16[1024,256]{1,0:T(8,128)(2,1)S(1)}, bf16[1024,256]{1,0:T(8,128)(2,1)S(1)}, bf16[1024,256]{1,0:T(8,128)(2,1)S(1)}) custom-call(s32[4]{0:T(128)S(1)} %pad_add_fusion.here_ref, bf16[1024,256]{1,0:T(8,128)(2,1)S(1)} %copy-done.1, bf16[1024,256]{1,0:T(8,128)(2,1)S(1)} %copy-done.5, ...), custom_call_target="tpu_custom_call" | custom-call | flops 1000 | bytes 22140000 | tf_op jit(solution)/shard_map/pallas_call | solution.py:483
  82.7 9.7 %collective-permute-done.13.refs_10_.refs_11_ = bf16[256,1024]{1,0:T(8,128)(2,1)S(1)} collective-permute-done((bf16[256,1024]{1,0:T(8,128)(2,1)S(1)}, bf16[256,1024]{1,0:T(8,128)(2,1)S(1)}, u32[]{:S(2)}, u32[]{:S(2)}) %collective-permute-start.13) | collective-permute-done | bytes 524320 | tf_op jit(solution)/shard_map/ppermute | solution.py:586
  92.4 3.7 %shard_map.121 = bf16[4,256,1024]{2,1,0:T(8,128)(2,1)S(1)} custom-call(s32[4]{0:T(128)S(1)} %pad_add_fusion.here_ref, bf16[1024,256]{1,0:T(8,128)(2,1)S(1)} %copy-done.1, bf16[1024,256]{1,0:T(8,128)(2,1)S(1)} %copy-done.5, bf16[1024,256]{1,0:T(8,128)(2,1)S(1)} %copy-done.3, bf16[1024,256]{1,0:T(8,128)(2,1)} %collective-permute-done.2.refs_3_, ...), custom_call_target="tpu_custom_call" | custom-call | flops 1000 | bytes 1845000 | tf_op jit(solution)/shard_map/pallas_call | solution.py:483
  96.7 0.6 collective-permute-start.17
  97.3 0.9 collective-permute-start.18
  98.7 1.7 %collective-permute-done.16.refs_9_ = bf16[4,256,1024]{2,1,0:T(8,128)(2,1)S(1)} collective-permute-done((bf16[4,256,1024]{2,1,0:T(8,128)(2,1)S(1)}, bf16[4,256,1024]{2,1,0:T(8,128)(2,1)S(1)}, u32[]{:S(2)}, u32[]{:S(2)}) %collective-permute-start.16) | collective-permute-done | bytes 2097184 | tf_op jit(solution)/shard_map/ppermute | solution.py:620
  100.5 4.0 %shard_map.122 = (bf16[256,1024]{1,0:T(8,128)(2,1)S(1)}, bf16[256,1024]{1,0:T(8,128)(2,1)S(1)}, bf16[256,1024]{1,0:T(8,128)(2,1)S(1)}, bf16[256,1024]{1,0:T(8,128)(2,1)S(1)}) custom-call(s32[4]{0:T(128)S(1)} %pad_add_fusion.here_ref, bf16[1024,256]{1,0:T(8,128)(2,1)S(1)} %copy-done.1, bf16[1024,256]{1,0:T(8,128)(2,1)S(1)} %copy-done.5, ...), custom_call_target="tpu_custom_call" | custom-call | flops 1000 | bytes 1845000 | tf_op jit(solution)/shard_map/pallas_call | solution.py:483
  104.6 2.3 %collective-permute-start.21 = (bf16[256,1024]{1,0:T(8,128)(2,1)S(1)}, bf16[256,1024]{1,0:T(8,128)(2,1)S(1)}, u32[]{:S(2)}, u32[]{:S(2)}) collective-permute-start(bf16[256,1024]{1,0:T(8,128)(2,1)S(1)} %get-tuple-element.70), channel_id=1, source_target_pairs={{0,128},{64,192},{128,0},{192,64},{1,129},{65,193},{129,1},{193,65... | collective-permute-start | bytes 1572872 | tf_op jit(solution)/shard_map/ppermute | solution.py:632
  106.9 4.8 %collective-permute-done.17.p1_ref = bf16[1024,256]{1,0:T(8,128)(2,1)S(1)} collective-permute-done((bf16[1024,256]{1,0:T(8,128)(2,1)S(1)}, bf16[1024,256]{1,0:T(8,128)(2,1)S(1)}, u32[]{:S(2)}, u32[]{:S(2)}) %collective-permute-start.17) | collective-permute-done | bytes 524320 | tf_op jit(solution)/shard_map/ppermute | solution.py:607
  111.7 1.1 collective-permute-start.22
  112.8 8.0 %collective-permute-done.18.p2_ref = bf16[1024,256]{1,0:T(8,128)(2,1)S(1)} collective-permute-done((bf16[1024,256]{1,0:T(8,128)(2,1)S(1)}, bf16[1024,256]{1,0:T(8,128)(2,1)S(1)}, u32[]{:S(2)}, u32[]{:S(2)}) %collective-permute-start.18) | collective-permute-done | bytes 524320 | tf_op jit(solution)/shard_map/ppermute | solution.py:607
  120.9 2.4 %collective-permute-done.19.p3_ref = bf16[1024,256]{1,0:T(8,128)(2,1)S(1)} collective-permute-done((bf16[1024,256]{1,0:T(8,128)(2,1)S(1)}, bf16[1024,256]{1,0:T(8,128)(2,1)S(1)}, u32[]{:S(2)}, u32[]{:S(2)}) %collective-permute-start.19) | collective-permute-done | bytes 524320 | tf_op jit(solution)/shard_map/ppermute | solution.py:607
  123.3 4.4 %shard_map.123 = (bf16[1024,256]{1,0:T(8,128)(2,1)}, f32[1024,256]{1,0:T(8,128)S(1)}, f32[24,256]{1,0:T(8,128)S(1)}) custom-call(bf16[1024,256]{1,0:T(8,128)(2,1)S(1)} %get-tuple-element.72.own_ref, bf16[1024,256]{1,0:T(8,128)(2,1)S(1)} %collective-permute-done.17.p1_ref, bf16[1024,256]{1,0:T(8,128)(2,1)S(1)} %collective-permute-done.18.p2_ref, ...), custom_call_target="tpu_custom_call" | custom-call | flops 1000 | bytes 73800000 | tf_op jit(solution)/shard_map/pallas_call | solution.py:483
  127.7 2.2 %collective-permute-done.21.c_ref = bf16[256,1024]{1,0:T(8,128)(2,1)S(1)} collective-permute-done((bf16[256,1024]{1,0:T(8,128)(2,1)S(1)}, bf16[256,1024]{1,0:T(8,128)(2,1)S(1)}, u32[]{:S(2)}, u32[]{:S(2)}) %collective-permute-start.21) | collective-permute-done | bytes 524320 | tf_op jit(solution)/shard_map/ppermute | solution.py:632
  129.8 0.6 collective-permute-done.22.d_ref
  130.7 0.7 collective-permute-start.23
  131.4 20.7 %all_to_all.10.all_ref = f32[8,24,256]{2,1,0:T(8,128)S(1)} all-to-all(f32[8,24,256]{2,1,0:T(8,128)S(1)} %broadcast_in_dim.2), channel_id=1, replica_groups=mesh['y'=4,'core'=2,'x'=4,'z'=8] {'y','core'}, dimensions={0} | all-to-all | bytes 393216 | tf_op jit(solution)/shard_map/all_to_all | solution.py:507
  152.2 2.5 %shard_map.124 = (bf16[1024,256]{1,0:T(8,128)(2,1)}, bf16[1024,256]{1,0:T(8,128)(2,1)}, f32[16,16]{1,0:T(8,128)}, f32[16,16]{1,0:T(8,128)}) custom-call(s32[4]{0:T(128)S(1)} %pad_add_fusion.here_ref, f32[8,24,256]{2,1,0:T(8,128)S(1)} %all_to_all.10.all_ref, f32[1024,256]{1,0:T(8,128)S(1)} %get-tuple-element.82.back_ref, bf16[1024,256]{1,0:T(8,128)(2,1)S(1)} %copy-done.7, ...), custom_call_target="tpu_custom_call" | custom-call | flops 1000 | bytes 9225000 | tf_op jit(solution)/shard_map/pallas_call | solution.py:483
  154.7 1.2 shard_map.126
  (58 shorter events, 3.5 us)
Async XLA Ops:
  3.7 5.0 %copy-start = (bf16[1024,256]{1,0:T(8,128)(2,1)S(1)}, bf16[1024,256]{1,0:T(8,128)(2,1)}, u32[]{:S(2)}) copy-start(bf16[1024,256]{1,0:T(8,128)(2,1)} %refs_0_.4) | copy-start | bytes 1572868
  3.7 10.6 %copy-start.6 = (bf16[1024,256]{1,0:T(8,128)(2,1)S(1)}, bf16[1024,256]{1,0:T(8,128)(2,1)}, u32[]{:S(2)}) copy-start(bf16[1024,256]{1,0:T(8,128)(2,1)} %key_ref.3) | copy-start | bytes 1572868
  3.7 10.6 %copy-start.18 = (f32[16,16]{1,0:T(8,128)S(1)}, f32[16,16]{1,0:T(8,128)}, u32[]{:S(2)}) copy-start(f32[16,16]{1,0:T(8,128)} %rate_ref.7) | copy-start | bytes 3076
  3.7 10.6 %copy-start.19 = (f32[16,16]{1,0:T(8,128)S(1)}, f32[16,16]{1,0:T(8,128)}, u32[]{:S(2)}) copy-start(f32[16,16]{1,0:T(8,128)} %res_ref.7) | copy-start | bytes 3076
  3.7 41.0 %all-to-all-start = ((bf16[4,1024,256]{2,1,0:T(8,128)(2,1)}), bf16[4,1024,256]{2,1,0:T(8,128)(2,1)S(1)}, u32[]{:S(2)}, u32[]{:S(2)}) async-start(bf16[4,1024,256]{2,1,0:T(8,128)(2,1)} %dynamic-slice_bitcast_fusion), calls=%async_computation | async-start | bytes 4194304 | tf_op jit(solution)/shard_map/all_to_all | solution.py:544
  8.7 15.8 %collective-permute-start.1 = (bf16[1024,256]{1,0:T(8,128)(2,1)S(1)}, bf16[1024,256]{1,0:T(8,128)(2,1)S(1)}, u32[]{:S(2)}, u32[]{:S(2)}) collective-permute-start(bf16[1024,256]{1,0:T(8,128)(2,1)S(1)} %copy-done), channel_id=1, source_target_pairs={{0,7},{1,0},{2,1},{3,2},{4,3},{5,4},{6,5},{7,6},{8,15},{9,8},{10,9... | collective-permute-start | bytes 1572872 | tf_op jit(solution)/shard_map/ppermute | solution.py:536
  14.3 13.4 %collective-permute-start = (bf16[1024,256]{1,0:T(8,128)(2,1)S(1)}, bf16[1024,256]{1,0:T(8,128)(2,1)S(1)}, u32[]{:S(2)}, u32[]{:S(2)}) collective-permute-start(bf16[1024,256]{1,0:T(8,128)(2,1)S(1)} %copy-done), channel_id=1, source_target_pairs={{0,1},{1,2},{2,3},{3,4},{4,5},{5,6},{6,7},{7,0},{8,9},{9,10},{10,1... | collective-permute-start | bytes 1572872 | tf_op jit(solution)/shard_map/ppermute | solution.py:535
  14.3 1.0 copy-start.8
  18.0 1.0 copy-start.12
  19.0 1.0 copy-start.14
  20.0 0.8 copy-start.16
  27.7 17.0 %collective-permute-start.2 = (bf16[1024,256]{1,0:T(8,128)(2,1)S(1)}, bf16[1024,256]{1,0:T(8,128)(2,1)}, u32[]{:S(2)}, u32[]{:S(2)}) collective-permute-start(bf16[1024,256]{1,0:T(8,128)(2,1)S(1)} %collective-permute-done.refs_1_), channel_id=1, source_target_pairs={{0,1},{1,2},{2,3},{3,4},{4,5},{5,6},{6,7},{7,0},{8,9},{9,10},{10,1... | collective-permute-start | bytes 1572872 | tf_op jit(solution)/shard_map/ppermute | solution.py:535
  27.7 0.8 copy-start.4
  28.5 16.2 %collective-permute-start.3 = (bf16[1024,256]{1,0:T(8,128)(2,1)S(1)}, bf16[1024,256]{1,0:T(8,128)(2,1)}, u32[]{:S(2)}, u32[]{:S(2)}) collective-permute-start(bf16[1024,256]{1,0:T(8,128)(2,1)S(1)} %collective-permute-done.1.refs_2_), channel_id=1, source_target_pairs={{0,7},{1,0},{2,1},{3,2},{4,3},{5,4},{6,5},{7,6},{8,15},{9,8},{10,9... | collective-permute-start | bytes 1572872 | tf_op jit(solution)/shard_map/ppermute | solution.py:536
  31.1 0.8 copy-start.2
  31.9 3.6 %collective-permute-start.4 = (f32[32,256]{1,0:T(8,128)S(1)}, f32[32,256]{1,0:T(8,128)S(1)}, u32[]{:S(2)}, u32[]{:S(2)}) collective-permute-start(f32[32,256]{1,0:T(8,128)S(1)} %get-tuple-element.47.own_ref), channel_id=1, source_target_pairs={{0,32},{32,0},{1,33},{33,1},{2,34},{34,2},{3,35},{35,3},{4,36},{36... | collective-permute-start | bytes 98312 | tf_op jit(solution)/shard_map/ppermute | solution.py:565
  35.5 4.1 %collective-permute-start.7 = (f32[2,32,256]{2,1,0:T(8,128)S(1)}, f32[2,32,256]{2,1,0:T(8,128)S(1)}, u32[]{:S(2)}, u32[]{:S(2)}) collective-permute-start(f32[2,32,256]{2,1,0:T(8,128)S(1)} %pad_maximum_fusion), channel_id=1, source_target_pairs={{0,192},{64,0},{128,64},{192,128},{1,193},{65,1},{129,65},{193,129... | collective-permute-start | bytes 196616 | tf_op jit(solution)/shard_map/ppermute | solution.py:569
  38.3 4.7 %collective-permute-start.6 = (f32[2,32,256]{2,1,0:T(8,128)S(1)}, f32[2,32,256]{2,1,0:T(8,128)S(1)}, u32[]{:S(2)}, u32[]{:S(2)}) collective-permute-start(f32[2,32,256]{2,1,0:T(8,128)S(1)} %pad_maximum_fusion), channel_id=1, source_target_pairs={{0,128},{64,192},{128,0},{192,64},{1,129},{65,193},{129,1},{193,65... | collective-permute-start | bytes 196616 | tf_op jit(solution)/shard_map/ppermute | solution.py:569
  38.6 6.1 %collective-permute-start.5 = (f32[2,32,256]{2,1,0:T(8,128)S(1)}, f32[2,32,256]{2,1,0:T(8,128)S(1)}, u32[]{:S(2)}, u32[]{:S(2)}) collective-permute-start(f32[2,32,256]{2,1,0:T(8,128)S(1)} %pad_maximum_fusion), channel_id=1, source_target_pairs={{0,64},{64,128},{128,192},{192,0},{1,65},{65,129},{129,193},{193,1... | collective-permute-start | bytes 196616 | tf_op jit(solution)/shard_map/ppermute | solution.py:569
  44.7 30.8 %collective-permute-start.12 = (bf16[4,1024,256]{2,1,0:T(8,128)(2,1)S(1)}, bf16[4,1024,256]{2,1,0:T(8,128)(2,1)}, u32[]{:S(2)}, u32[]{:S(2)}) collective-permute-start(bf16[4,1024,256]{2,1,0:T(8,128)(2,1)S(1)} %all-to-all-done.refs_9_), channel_id=1, source_target_pairs={{0,32},{32,0},{1,33},{33,1},{2,34},{34,2},{3,35},{35,3},{4,36},{36... | collective-permute-start | bytes 6291464 | tf_op jit(solution)/shard_map/ppermute | solution.py:585
  45.8 14.9 %collective-permute-start.8 = (bf16[1024,256]{1,0:T(8,128)(2,1)}, bf16[1024,256]{1,0:T(8,128)(2,1)S(1)}, u32[]{:S(2)}, u32[]{:S(2)}) collective-permute-start(bf16[1024,256]{1,0:T(8,128)(2,1)} %collective-permute-done.2.refs_3_), channel_id=1, source_target_pairs={{0,1},{1,2},{2,3},{3,4},{4,5},{5,6},{6,7},{7,0},{8,9},{9,10},{10,1... | collective-permute-start | bytes 1572872 | tf_op jit(solution)/shard_map/ppermute | solution.py:535
  45.8 14.9 %collective-permute-start.9 = (bf16[1024,256]{1,0:T(8,128)(2,1)}, bf16[1024,256]{1,0:T(8,128)(2,1)S(1)}, u32[]{:S(2)}, u32[]{:S(2)}) collective-permute-start(bf16[1024,256]{1,0:T(8,128)(2,1)} %collective-permute-done.3.refs_4_), channel_id=1, source_target_pairs={{0,7},{1,0},{2,1},{3,2},{4,3},{5,4},{6,5},{7,6},{8,15},{9,8},{10,9... | collective-permute-start | bytes 1572872 | tf_op jit(solution)/shard_map/ppermute | solution.py:536
  48.5 27.0 %copy-start.1 = (bf16[1024,256]{1,0:T(8,128)(2,1)S(1)}, bf16[1024,256]{1,0:T(8,128)(2,1)}, u32[]{:S(2)}) copy-start(bf16[1024,256]{1,0:T(8,128)(2,1)} %refs_0_.4) | copy-start | bytes 1572868
  48.5 27.0 %copy-start.3 = (bf16[1024,256]{1,0:T(8,128)(2,1)S(1)}, bf16[1024,256]{1,0:T(8,128)(2,1)}, u32[]{:S(2)}) copy-start(bf16[1024,256]{1,0:T(8,128)(2,1)} %copy-done.2) | copy-start | bytes 1572868
  48.5 27.0 %copy-start.5 = (bf16[1024,256]{1,0:T(8,128)(2,1)S(1)}, bf16[1024,256]{1,0:T(8,128)(2,1)}, u32[]{:S(2)}) copy-start(bf16[1024,256]{1,0:T(8,128)(2,1)} %copy-done.4) | copy-start | bytes 1572868
  48.6 1.1 copy-start.10
  49.7 1.2 copy-start.15
  60.7 7.0 %collective-permute-start.11 = (bf16[512,256]{1,0:T(8,128)(2,1)S(1)}, bf16[512,256]{1,0:T(8,128)(2,1)S(1)}, u32[]{:S(2)}, u32[]{:S(2)}) collective-permute-start(bf16[512,256]{1,0:T(8,128)(2,1)S(1)} %slice.7), channel_id=1, source_target_pairs={{0,7},{1,0},{2,1},{3,2},{4,3},{5,4},{6,5},{7,6},{8,15},{9,8},{10,9... | collective-permute-start | bytes 786440 | tf_op jit(solution)/shard_map/ppermute | solution.py:536
  63.1 19.6 %collective-permute-start.15 = (bf16[256,1024]{1,0:T(8,128)(2,1)S(1)}, bf16[256,1024]{1,0:T(8,128)(2,1)S(1)}, u32[]{:S(2)}, u32[]{:S(2)}) collective-permute-start(bf16[256,1024]{1,0:T(8,128)(2,1)S(1)} %get-tuple-element.54.refs_9_.refs_10_), channel_id=1, source_target_pairs={{0,24},{8,0},{16,8},{24,16},{1,25},{9,1},{17,9},{25,17},{2,26},{10... | collective-permute-start | bytes 1572872 | tf_op jit(solution)/shard_map/ppermute | solution.py:586
  65.8 16.9 %collective-permute-start.14 = (bf16[256,1024]{1,0:T(8,128)(2,1)S(1)}, bf16[256,1024]{1,0:T(8,128)(2,1)S(1)}, u32[]{:S(2)}, u32[]{:S(2)}) collective-permute-start(bf16[256,1024]{1,0:T(8,128)(2,1)S(1)} %get-tuple-element.54.refs_9_.refs_10_), channel_id=1, source_target_pairs={{0,16},{8,24},{16,0},{24,8},{1,17},{9,25},{17,1},{25,9},{2,18},{10... | collective-permute-start | bytes 1572872 | tf_op jit(solution)/shard_map/ppermute | solution.py:586
  66.4 26.0 %collective-permute-start.13 = (bf16[256,1024]{1,0:T(8,128)(2,1)S(1)}, bf16[256,1024]{1,0:T(8,128)(2,1)S(1)}, u32[]{:S(2)}, u32[]{:S(2)}) collective-permute-start(bf16[256,1024]{1,0:T(8,128)(2,1)S(1)} %get-tuple-element.54.refs_9_.refs_10_), channel_id=1, source_target_pairs={{0,8},{8,16},{16,24},{24,0},{1,9},{9,17},{17,25},{25,1},{2,10},{10... | collective-permute-start | bytes 1572872 | tf_op jit(solution)/shard_map/ppermute | solution.py:586
  67.7 7.7 %collective-permute-start.10 = (bf16[512,256]{1,0:T(8,128)(2,1)S(1)}, bf16[512,256]{1,0:T(8,128)(2,1)S(1)}, u32[]{:S(2)}, u32[]{:S(2)}) collective-permute-start(bf16[512,256]{1,0:T(8,128)(2,1)S(1)} %slice.6), channel_id=1, source_target_pairs={{0,1},{1,2},{2,3},{3,4},{4,5},{5,6},{6,7},{7,0},{8,9},{9,10},{10,1... | collective-permute-start | bytes 786440 | tf_op jit(solution)/shard_map/ppermute | solution.py:535
  96.1 4.4 %collective-permute-start.16 = (bf16[4,256,1024]{2,1,0:T(8,128)(2,1)S(1)}, bf16[4,256,1024]{2,1,0:T(8,128)(2,1)S(1)}, u32[]{:S(2)}, u32[]{:S(2)}) collective-permute-start(bf16[4,256,1024]{2,1,0:T(8,128)(2,1)S(1)} %shard_map.121), channel_id=1, source_target_pairs={{0,32},{32,0},{1,33},{33,1},{2,34},{34,2},{3,35},{35,3},{4,36},{36... | collective-permute-start | bytes 6291464 | tf_op jit(solution)/shard_map/ppermute | solution.py:620
  96.7 15.0 %collective-permute-start.17 = (bf16[1024,256]{1,0:T(8,128)(2,1)S(1)}, bf16[1024,256]{1,0:T(8,128)(2,1)S(1)}, u32[]{:S(2)}, u32[]{:S(2)}) collective-permute-start(bf16[1024,256]{1,0:T(8,128)(2,1)S(1)} %get-tuple-element.73), channel_id=1, source_target_pairs={{0,16},{8,24},{16,0},{24,8},{1,17},{9,25},{17,1},{25,9},{2,18},{10... | collective-permute-start | bytes 1572872 | tf_op jit(solution)/shard_map/ppermute | solution.py:607
  97.3 23.6 %collective-permute-start.18 = (bf16[1024,256]{1,0:T(8,128)(2,1)S(1)}, bf16[1024,256]{1,0:T(8,128)(2,1)S(1)}, u32[]{:S(2)}, u32[]{:S(2)}) collective-permute-start(bf16[1024,256]{1,0:T(8,128)(2,1)S(1)} %get-tuple-element.74), channel_id=1, source_target_pairs={{0,24},{8,0},{16,8},{24,16},{1,25},{9,1},{17,9},{25,17},{2,26},{10... | collective-permute-start | bytes 1572872 | tf_op jit(solution)/shard_map/ppermute | solution.py:607
  98.2 25.1 %copy-start.11 = (bf16[1024,256]{1,0:T(8,128)(2,1)S(1)}, bf16[1024,256]{1,0:T(8,128)(2,1)}, u32[]{:S(2)}) copy-start(bf16[1024,256]{1,0:T(8,128)(2,1)} %query_ref.3) | copy-start | bytes 1572868
  98.2 25.1 %copy-start.13 = (f32[16,128,128]{2,1,0:T(8,128)S(1)}, f32[16,128,128]{2,1,0:T(8,128)}, u32[]{:S(2)}) copy-start(f32[16,128,128]{2,1,0:T(8,128)} %copy-done.12) | copy-start | bytes 3145732
  98.2 25.1 %copy-start.17 = (bf16[256,1024]{1,0:T(8,128)(2,1)S(1)}, bf16[256,1024]{1,0:T(8,128)(2,1)}, u32[]{:S(2)}) copy-start(bf16[256,1024]{1,0:T(8,128)(2,1)} %copy-done.16) | copy-start | bytes 1572868
  98.2 25.1 %collective-permute-start.19 = (bf16[1024,256]{1,0:T(8,128)(2,1)S(1)}, bf16[1024,256]{1,0:T(8,128)(2,1)S(1)}, u32[]{:S(2)}, u32[]{:S(2)}) collective-permute-start(bf16[1024,256]{1,0:T(8,128)(2,1)S(1)} %get-tuple-element.75), channel_id=1, source_target_pairs={{0,8},{8,16},{16,24},{24,0},{1,9},{9,17},{17,25},{25,1},{2,10},{10... | collective-permute-start | bytes 1572872 | tf_op jit(solution)/shard_map/ppermute | solution.py:607
  104.5 23.2 %collective-permute-start.20 = (bf16[256,1024]{1,0:T(8,128)(2,1)S(1)}, bf16[256,1024]{1,0:T(8,128)(2,1)S(1)}, u32[]{:S(2)}, u32[]{:S(2)}) collective-permute-start(bf16[256,1024]{1,0:T(8,128)(2,1)S(1)} %get-tuple-element.69), channel_id=1, source_target_pairs={{0,64},{64,128},{128,192},{192,0},{1,65},{65,129},{129,193},{193,1... | collective-permute-start | bytes 1572872 | tf_op jit(solution)/shard_map/ppermute | solution.py:632
  104.6 25.3 %collective-permute-start.21 = (bf16[256,1024]{1,0:T(8,128)(2,1)S(1)}, bf16[256,1024]{1,0:T(8,128)(2,1)S(1)}, u32[]{:S(2)}, u32[]{:S(2)}) collective-permute-start(bf16[256,1024]{1,0:T(8,128)(2,1)S(1)} %get-tuple-element.70), channel_id=1, source_target_pairs={{0,128},{64,192},{128,0},{192,64},{1,129},{65,193},{129,1},{193,65... | collective-permute-start | bytes 1572872 | tf_op jit(solution)/shard_map/ppermute | solution.py:632
  111.7 18.7 %collective-permute-start.22 = (bf16[256,1024]{1,0:T(8,128)(2,1)S(1)}, bf16[256,1024]{1,0:T(8,128)(2,1)S(1)}, u32[]{:S(2)}, u32[]{:S(2)}) collective-permute-start(bf16[256,1024]{1,0:T(8,128)(2,1)S(1)} %get-tuple-element.71), channel_id=1, source_target_pairs={{0,192},{64,0},{128,64},{192,128},{1,193},{65,1},{129,65},{193,129... | collective-permute-start | bytes 1572872 | tf_op jit(solution)/shard_map/ppermute | solution.py:632
  127.6 24.5 %copy-start.7 = (bf16[1024,256]{1,0:T(8,128)(2,1)S(1)}, bf16[1024,256]{1,0:T(8,128)(2,1)}, u32[]{:S(2)}) copy-start(bf16[1024,256]{1,0:T(8,128)(2,1)} %key_ref.3) | copy-start | bytes 1572868
  127.7 24.5 %copy-start.9 = (bf16[1024,256]{1,0:T(8,128)(2,1)S(1)}, bf16[1024,256]{1,0:T(8,128)(2,1)}, u32[]{:S(2)}) copy-start(bf16[1024,256]{1,0:T(8,128)(2,1)} %value_ref.3) | copy-start | bytes 1572868
  130.7 24.0 %collective-permute-start.23 = (bf16[256,1024]{1,0:T(8,128)(2,1)S(1)}, bf16[256,1024]{1,0:T(8,128)(2,1)S(1)}, u32[]{:S(2)}, u32[]{:S(2)}) collective-permute-start(bf16[256,1024]{1,0:T(8,128)(2,1)S(1)} %shard_map.125), channel_id=1, source_target_pairs={{0,0},{8,72},{16,144},{24,216},{64,8},{72,80},{80,152},{88,192},{1... | collective-permute-start | bytes 1572872 | tf_op jit(solution)/shard_map/ppermute | solution.py:656
